TPU v7x, 32 devices: a whole 2x2x4 slice. The times are simulated.
32 devices in a mesh: groups: 2 (over y), blk: 4 (over z), shell: 2 (over x), sub: 2 (over core).
Axes of the slice: x: 2, y: 2, z: 4, core: 2. Of those that a mesh axis runs over, the one named last changes fastest.
Arguments:
- images: bfloat16 [4096, 2, 8192], P(('groups', 'blk'), None, ('shell', 'sub')), parts along dimension 0, may hold values from -12 to 12
- ctf: bfloat16 [4096, 8192], P(('groups', 'blk'), ('shell', 'sub')), parts along dimension 0, may hold values from -1 to 1
- projections: bfloat16 [32, 2, 8192], P(('groups', 'blk'), None, ('shell', 'sub')), parts along dimension 0, may hold values from -5 to 5
- shifts: int32 [4096, 2], P(('groups', 'blk')), parts along dimension 0, may hold values from -6 to 6
- inv_sigma2: float32 [8192], P(('shell', 'sub')), may hold values from 0.5 to 2
- class_ids: int32 [32], P('groups'), parts along dimension 0, may hold values from 0 to 3
- log_prior: float32 [4], replicated, may hold values from -1.5 to 0
- allowed: int32 [8, 2], P(('groups', 'blk')), parts along dimension 0, may hold values from -1 to 3, as said below
Outputs:
- back_data: float32 [32, 2, 8192], P(('groups', 'blk'), None, ('shell', 'sub')), parts along dimension 0
- back_weight: float32 [32, 8192], P(('groups', 'blk'), ('shell', 'sub')), parts along dimension 0
- best_weight: float32 [4096], P(('groups', 'blk', 'shell', 'sub')), parts along dimension 0
There are 2 independent parts, one for each index of `groups`. A program takes and returns all parts, laid end to end along the dimension named above; an argument that names none is the same for every part. Nothing has to cross between parts.
Inputs may be any that keep to these rules, and one draw needn't show every extreme that they name: `allowed`: row b lists distinct orientation block numbers in its first slots, block b always first, then -1 in the remaining slots; between 1 and 2 blocks are listed, and some row lists 2.
All inputs are finite; a program needn't handle non-finite values.
Results may differ from a plain program's by a relative error of at most 0.0055.
Values may be sent and summed in bfloat16 or wider, within the bound.
No kernel may reach another device: no remote copies, remote signals or barrier semaphores. Data moves between devices by JAX's collectives and lax.ppermute only.
A program may use at most 64 MiB of HBM per device.

v0:
```python
import math

import jax
import jax.numpy as jnp
from jax import lax
from jax.sharding import PartitionSpec as P

KMAX = 64
BOX = 360
CLASSES = 4
PIXC = 8192


def prepare(images, ctf, shifts, inv_sigma2, first_pixel):
    width = images.shape[2]
    pixel = first_pixel + jnp.arange(width, dtype=jnp.int32)
    freq_x = (pixel // (2 * KMAX)).astype(jnp.float32)
    freq_y = (pixel % (2 * KMAX) - KMAX).astype(jnp.float32)
    moves = shifts.astype(jnp.float32)
    theta = (
        2.0 * math.pi / BOX * (moves[:, 0:1] * freq_x[None, :] + moves[:, 1:2] * freq_y[None, :])
    )
    cosine = jnp.cos(theta)
    sine = jnp.sin(theta)
    real_part = images[:, 0].astype(jnp.float32)
    imag_part = images[:, 1].astype(jnp.float32)
    shifted_real = real_part * cosine + imag_part * sine
    shifted_imag = imag_part * cosine - real_part * sine
    factor = ctf.astype(jnp.float32) * inv_sigma2[None, :]
    weighted = jnp.stack([factor * shifted_real, factor * shifted_imag], axis=1).astype(
        jnp.bfloat16
    )
    curvature = (factor * ctf.astype(jnp.float32)).astype(jnp.bfloat16)
    return (weighted, curvature)


def posterior(rows, keep_cols):
    masked = jnp.where(keep_cols[None, :], rows, jnp.float32(-1e30))
    top = jnp.max(masked, axis=1, keepdims=True)
    expo = jnp.exp(masked - top)
    total = jnp.sum(expo, axis=1, keepdims=True)
    return ((expo / total).astype(jnp.bfloat16), 1.0 / total[:, 0])


def contract_rows(left, right):
    return lax.dot_general(
        left, right, (((0,), (0,)), ((), ())), preferred_element_type=jnp.float32
    )


def contract_cols(left, right):
    return lax.dot_general(
        left, right, (((1,), (1,)), ((), ())), preferred_element_type=jnp.float32
    )


def body(images, ctf, projections, shifts, inv_sigma2, class_ids, log_prior, allowed):
    img_rows = images.shape[0]
    pix_dev = images.shape[2]
    orient_dev = projections.shape[0]
    blocks = lax.axis_size("blk")
    pieces = lax.axis_size(("shell", "sub"))
    place = lax.axis_index(("shell", "sub"))
    weighted, curvature = prepare(images, ctf, shifts, inv_sigma2, place * pix_dev)
    flat = weighted.reshape(img_rows, 2 * pix_dev)
    factor = 1.0 / math.sqrt(PIXC)
    listed = jnp.any(allowed[0][:, None] == jnp.arange(blocks, dtype=jnp.int32)[None, :], axis=0)
    piece = lax.all_gather(projections, "blk", axis=0, tiled=True)
    count = piece.shape[0]
    piece_wide = piece.astype(jnp.float32)
    power = (piece_wide[:, 0] * piece_wide[:, 0] + piece_wide[:, 1] * piece_wide[:, 1]).astype(
        jnp.bfloat16
    )
    cross = contract_cols(flat, piece.reshape(count, 2 * pix_dev))
    own_term = contract_cols(curvature, power)
    values = (2.0 * cross - own_term) * factor
    classes = class_ids[:, None] == jnp.arange(CLASSES, dtype=jnp.int32)[None, :]
    prior = jnp.sum(jnp.where(classes, log_prior[None, :], jnp.float32(0.0)), axis=1)
    keep_cols = jnp.repeat(listed, orient_dev)
    share = img_rows // pieces
    rows = lax.psum(values, ("shell", "sub")) + prior[None, :]
    weights, best_all = posterior(rows, keep_cols)
    best_share = lax.dynamic_slice_in_dim(best_all, place * share, share)
    summed = lax.psum_scatter(
        jnp.concatenate([contract_rows(weights, flat), contract_rows(weights, curvature)], axis=1),
        "blk",
        scatter_dimension=0,
        tiled=True,
    )
    back_data = summed[:, : 2 * pix_dev].reshape(orient_dev, 2, pix_dev)
    back_weight = summed[:, 2 * pix_dev :]
    return (back_data, back_weight, best_share)


def solution(mesh):
    in_specs = (
        P(("groups", "blk"), None, ("shell", "sub")),
        P(("groups", "blk"), ("shell", "sub")),
        P(("groups", "blk"), None, ("shell", "sub")),
        P(("groups", "blk"), None),
        P(("shell", "sub")),
        P("groups"),
        P(),
        P(("groups", "blk"), None),
    )
    out_specs = (
        P(("groups", "blk"), None, ("shell", "sub")),
        P(("groups", "blk"), ("shell", "sub")),
        P(("groups", "blk", "shell", "sub")),
    )
    return jax.shard_map(body, mesh=mesh, in_specs=in_specs, out_specs=out_specs, check_vma=False)
```

profile of v0, /device:TPU:0, one launch (start us, length us, event | category | flops | bytes accessed | tf_op | source)
XLA Modules:
  0.0 124.9 jit_solution(7851069101983071810)
XLA Ops:
  7.3 8.9 %fusion.34 = (bf16[512,1,2048]{2,1,0:T(2,128)(2,1)S(1)}, bf16[512,1,2048]{2,1,0:T(2,128)(2,1)S(1)}) fusion(bf16[512,2,2048]{2,1,0:T(2,128)(2,1)} %param.8), kind=kLoop, calls=%fused_computation.58 | loop fusion | bytes 8388608 | tf_op jit(solution)/shard_map/slice | solution.py:26
  16.3 15.1 %all_gather.3 = bf16[16,2,2048]{2,1,0:T(2,128)(2,1)S(1)} all-gather(bf16[4,2,2048]{2,1,0:T(2,128)(2,1)S(1)} %copy-done.2), channel_id=1, replica_groups=mesh['groups'=2,'blk'=4,'shell'=2,'sub'=2] {'blk'}, dimensions={0}, use_global_device_ids=true | all-gather | bytes 163840 | tf_op jit(solution)/shard_map/all_gather | solution.py:68
  31.4 18.6 %fusion.2 = (bf16[512,1,2048]{2,0,1:T(8,128)(2,1)S(1)}, bf16[512,1,2048]{2,0,1:T(8,128)(2,1)S(1)}) fusion(bf16[512,2048]{1,0:T(8,128)(2,1)S(1)} %copy-done.1, f32[2048]{0:T(1024)S(1)} %get-tuple-element.10, f32[512]{0:T(512)S(1)} %bitcast.34, f32[2048]{0:T(1024)S(1)} %get-tuple-element.9, f32[512]{0:T(512)S(1)} %bitcast.33, f32[2048]{0:T(1024)S(1)} %copy-done.3, ...), kind=kLoop, calls=%fused_computation.10 | loop fusion | flops 18874368 | bytes 10514432 | tf_op jit(solution)/shard_map/stack | solution.py:30
  50.1 0.4 maximum_convert_fusion
  50.5 1.9 %copy-done = bf16[512,2,2048]{2,0,1:T(8,128)(2,1)} copy-done((bf16[512,2,2048]{2,0,1:T(8,128)(2,1)}, bf16[512,2,2048]{2,0,1:T(8,128)(2,1)S(1)}, u32[]{:S(2)}) %copy-start) | copy-done | bytes 4194328
  52.4 1.2 fusion.17
  53.6 6.3 %copy.31 = bf16[512,2,2048]{0,2,1:T(8,128)(2,1)} copy(bf16[512,2,2048]{2,0,1:T(8,128)(2,1)} %copy-done) | data formatting | bytes 8388608 | tf_op jit(solution)/shard_map/convert_element_type | solution.py:30
  59.8 0.7 fusion.14
  60.5 10.3 %psum.7 = f32[512,16]{0,1:T(8,128)S(1)} all-reduce(f32[512,16]{0,1:T(8,128)S(1)} %fusion.14), channel_id=1, replica_groups=mesh['groups'=2,'blk'=4,'shell'=2,'sub'=2] {'shell','sub'}, use_global_device_ids=true, to_apply=%region_1.2 | all-reduce | flops 8192 | bytes 65536 | tf_op jit(solution)/shard_map/psum | solution.py:81
  70.8 0.1 compare_reduce_fusion
  70.9 0.1 broadcast_in_dim.39
  70.9 0.1 broadcast_in_dim.40
  71.0 0.1 select_reduce_fusion
  71.1 0.1 fusion.23
  71.2 0.1 fusion.24
  71.3 0.6 fusion.7
  71.9 3.4 %fusion.33 = f32[16,4096]{1,0:T(8,128)S(1)} fusion(bf16[512,4096]{0,1:T(8,128)(2,1)} %bitcast.32, f32[512,16]{0,1:T(8,128)S(1)} %psum.7, f32[512]{0:T(512)S(1)} %fusion.24, f32[512]{0:T(512)S(1)} %fusion.23, f32[16]{0:T(128)S(1)} %select_reduce_fusion, pred[16]{0:T(512)(128)(4,1)S(1)} %broadcast_in_dim.40), kind=kOutput, calls=%fused_computation.57 | convolution fusion | flops 67149824 | bytes 4493392 | tf_op jit(solution)/shard_map/dot_general | solution.py:46
  75.3 0.8 pad_maximum_fusion
  76.2 0.6 dynamic-slice
  77.4 0.6 dynamic_slice.3
  78.0 36.9 %all-reduce.3.cloned.1.call-done = f32[16,6144]{1,0:T(8,128)} async-done(((f32[16,6144]{1,0:T(8,128)}), f32[16,6144]{1,0:T(8,128)}) %all-reduce.3.cloned.1.call-update) | async-done | bytes 393232
  114.8 0.9 constant_dynamic-slice_fusion
  115.8 0.7 reshape.64
  116.5 1.5 %dynamic-slice.3 = f32[4,2048]{1,0:T(4,128)} dynamic-slice(f32[16,6144]{1,0:T(8,128)} %all-reduce.3.cloned.1.call-done, u32[]{:T(128)S(6)} %multiply.1, u32[]{:T(128)S(6)} %convert.4), dynamic_slice_sizes={4,2048} | dynamic-slice | bytes 65540 | tf_op jit(solution)/shard_map/slice | solution.py:91
  (24 shorter events, 0.2 us)
Async XLA Ops:
  7.2 107.7 %all-reduce.3.cloned.1.call-start = ((), (), s32[]{:S(2)}) async-start(), calls=%async_computation | async-start | bytes 786432
  7.2 9.0 %copy-start.4 = (s32[512,2]{0,1:T(2,128)S(1)}, s32[512,2]{0,1:T(2,128)}, u32[]{:S(2)}) copy-start(s32[512,2]{0,1:T(2,128)} %param.11) | copy-start | bytes 12292
  7.3 9.0 %copy-start.2 = (bf16[4,2,2048]{2,1,0:T(2,128)(2,1)S(1)}, bf16[4,2,2048]{2,1,0:T(2,128)(2,1)}, u32[]{:S(2)}) copy-start(bf16[4,2,2048]{2,1,0:T(2,128)(2,1)} %param.10) | copy-start | bytes 98308
  7.3 24.1 %copy-start.1 = (bf16[512,2048]{1,0:T(8,128)(2,1)S(1)}, bf16[512,2048]{1,0:T(8,128)(2,1)}, u32[]{:S(2)}) copy-start(bf16[512,2048]{1,0:T(8,128)(2,1)} %param.9) | copy-start | bytes 6291460
  7.3 24.1 %copy-start.3 = (f32[2048]{0:T(1024)S(1)}, f32[2048]{0:T(1024)}, u32[]{:S(2)}) copy-start(f32[2048]{0:T(1024)} %param.12) | copy-start | bytes 24580
  50.5 1.9 %copy-start = (bf16[512,2,2048]{2,0,1:T(8,128)(2,1)}, bf16[512,2,2048]{2,0,1:T(8,128)(2,1)S(1)}, u32[]{:S(2)}) copy-start(bf16[512,2,2048]{2,0,1:T(8,128)(2,1)S(1)} %maximum_convert_fusion) | copy-start | bytes 12582916
  53.6 17.2 %copy-start.5 = (s32[1,2]{1,0:T(1,128)S(1)}, s32[1,2]{1,0:T(1,128)}, u32[]{:S(2)}) copy-start(s32[1,2]{1,0:T(1,128)} %param.15) | copy-start | bytes 28
  53.6 17.5 %copy-start.6 = (f32[4]{0:T(128)S(1)}, f32[4]{0:T(128)}, u32[]{:S(2)}) copy-start(f32[4]{0:T(128)} %param.14) | copy-start | bytes 52
  53.6 17.5 %copy-start.7 = (s32[16]{0:T(128)S(1)}, s32[16]{0:T(128)}, u32[]{:S(2)}) copy-start(s32[16]{0:T(128)} %param.13) | copy-start | bytes 196
  71.3 4.8 %copy-start.8 = (u32[32]{0:T(128)S(1)}, u32[32]{0:T(128)}, u32[]{:S(2)}) copy-start(u32[32]{0:T(128)} %constant.64) | copy-start | bytes 388
Sparse Core Ops, SparseCore 0:
  76.3 38.5 all-reduce.2
where the time goes:
time: 125 us
  waiting for transfers between devices  36.9 us (30%)
  blocking collectives  25.3 us (20%)
  local copies, waits for them, and re-layouts  21.7 us (17%)
  other arithmetic  20.3 us (16%)
  between operations  14.9 us (12%)
  matrix products  5.83 us (5%)
    unnamed x2, waiting for transfers between devices  36.9 us
    another operation x1, other arithmetic, prepare(): jnp.stack([factor * shifted_real, factor * shifted_imag], axis=1)  18.6 us
    all_gather x1, blocking collectives, body(): piece = lax.all_gather(projections, 'blk', axis=0, tiled=True)  15.1 us
    psum x1, blocking collectives, body(): rows = lax.psum(values, ('shell', 'sub')) + prior[None, :]  10.3 us
    slice x1, local copies, waits for them, and re-layouts, prepare(): imag_part = images[:, 1].astype(jnp.float32)  8.93 us
    convert_element_type x1, local copies, waits for them, and re-layouts, prepare(): jnp.stack([factor * shifted_real, factor * shifted_imag], axis=1)  6.26 us
    dot_general x2, matrix products, contract_rows(): lax.dot_general(left, right, (((0,), (0,)), ((), ())), preferred_element_...  4 us
    unnamed x19, local copies, waits for them, and re-layouts  2.56 us
  transfers between devices with their start and end apart: 1, of which 1 were waited for; matrix products, arithmetic and copies ran while one was open for 1% of the time, Pallas kernels for 0%

commit v1 on v0

v1 whole, which is shorter than its diff:
```python
import functools
import math

import jax
import jax.numpy as jnp
import ml_dtypes
import numpy as np
from jax import lax
from jax.experimental import pallas as pl
from jax.experimental.pallas import tpu as pltpu
from jax.sharding import PartitionSpec as P

KMAX = 64
BOX = 360
CLASSES = 4
PIXC = 8192
ROW = 2 * KMAX
REACH = 8
GROUP = 16
DIRECT = 4
SPLITS = 3


def split_terms(table):
    terms = []
    rest = table.astype(np.float64)
    for _ in range(SPLITS):
        term = rest.astype(ml_dtypes.bfloat16)
        terms.append(term)
        rest = rest - term.astype(np.float64)
    return np.concatenate(terms, axis=0)


@functools.lru_cache(maxsize=None)
def phase_table(pieces, rows):
    shift = np.arange(-REACH, REACH, dtype=np.float64)[:, None]
    unit = 2.0 * math.pi / BOX
    along_y = unit * shift * np.arange(-KMAX, KMAX, dtype=np.float64)[None, :]
    step = np.broadcast_to(unit * shift, along_y.shape)
    half = SPLITS * 2 * REACH
    tables = []
    for piece in range(pieces):
        first = step * (piece * rows)
        left = split_terms(np.concatenate([np.cos(first), np.sin(first), np.cos(step), np.sin(step)], axis=1))
        right = split_terms(np.concatenate([np.cos(along_y), np.sin(along_y)], axis=1))
        table = np.zeros((128, 6 * ROW), ml_dtypes.bfloat16)
        table[:half, : 4 * ROW] = left
        table[64 : 64 + half, 4 * ROW :] = right
        tables.append(table)
    return np.stack(tables)


def prepare_kernel(rows, place_ref, image_ref, ctf_ref, shift_ref, inv_ref, table_ref, out_ref, wide_ref, phase_ref):
    images = ctf_ref.shape[0]
    pix = rows * ROW
    lane = lax.broadcasted_iota(jnp.int32, (images, 128), 1)
    inner = lane & 63
    moves = jnp.where(lane < 64, shift_ref[:, 0:1], shift_ref[:, 1:2]) + REACH
    hit = ((inner & (2 * REACH - 1)) == moves) & (inner < SPLITS * 2 * REACH)
    onehot = jnp.where(hit, 1.0, 0.0).astype(jnp.bfloat16)
    phase_ref[...] = jnp.dot(onehot, table_ref[0], preferred_element_type=jnp.float32)

    def group(g, carry):
        start = pl.multiple_of(g * GROUP, GROUP)
        slab = pl.multiple_of(g * (GROUP * rows * 2), GROUP * rows * 2)
        wide_ref[...] = image_ref[pl.ds(slab, GROUP * rows * 2), :].astype(jnp.float32)
        phase = phase_ref[pl.ds(start, GROUP), :]
        cos_a, sin_a, cos_s, sin_s, cos_b, sin_b = (phase[:, k * ROW : (k + 1) * ROW] for k in range(6))
        cos_0 = cos_a * cos_b - sin_a * sin_b
        sin_0 = sin_a * cos_b + cos_a * sin_b
        cos_1 = cos_0 * cos_s - sin_0 * sin_s
        sin_1 = sin_0 * cos_s + cos_0 * sin_s
        twice = 2.0 * cos_s
        for t in range(rows):
            lanes = slice(t * ROW, (t + 1) * ROW)
            real = wide_ref[pl.ds(2 * t, GROUP, stride=2 * rows), :]
            imag = wide_ref[pl.ds(2 * t + 1, GROUP, stride=2 * rows), :]
            ctf = ctf_ref[pl.ds(start, GROUP), lanes].astype(jnp.float32)
            factor = ctf * inv_ref[0:1, lanes]
            out_ref[pl.ds(start, GROUP), lanes] = (factor * (real * cos_0 + imag * sin_0)).astype(jnp.bfloat16)
            out_ref[pl.ds(start, GROUP), pl.ds(pix + t * ROW, ROW)] = (
                factor * (imag * cos_0 - real * sin_0)
            ).astype(jnp.bfloat16)
            out_ref[pl.ds(start, GROUP), pl.ds(2 * pix + t * ROW, ROW)] = (factor * ctf).astype(jnp.bfloat16)
            cos_0, cos_1 = cos_1, twice * cos_1 - cos_0
            sin_0, sin_1 = sin_1, twice * sin_1 - sin_0
        return carry

    lax.fori_loop(0, images // GROUP, group, 0)


def prepare(images, ctf, shifts, inv_sigma2, place, pieces):
    count, _, pix = images.shape
    rows = pix // ROW
    step = min(count, 64)
    flat = images.reshape(count, 2, rows, ROW).transpose(0, 2, 1, 3).reshape(count * rows * 2, ROW)
    return pl.pallas_call(
        functools.partial(prepare_kernel, rows),
        grid_spec=pltpu.PrefetchScalarGridSpec(
            num_scalar_prefetch=1,
            grid=(count // step,),
            in_specs=[
                pl.BlockSpec((step * rows * 2, ROW), lambda i, place: (i, 0)),
                pl.BlockSpec((step, pix), lambda i, place: (i, 0)),
                pl.BlockSpec((step, 2), lambda i, place: (i, 0)),
                pl.BlockSpec((1, pix), lambda i, place: (0, 0)),
                pl.BlockSpec((1, 128, 6 * ROW), lambda i, place: (place[0], 0, 0)),
            ],
            out_specs=pl.BlockSpec((step, 3 * pix), lambda i, place: (i, 0)),
            scratch_shapes=[
                pltpu.VMEM((GROUP * rows * 2, ROW), jnp.float32),
                pltpu.VMEM((step, 6 * ROW), jnp.float32),
            ],
        ),
        out_shape=jax.ShapeDtypeStruct((count, 3 * pix), jnp.bfloat16),
        compiler_params=pltpu.CompilerParams(vmem_limit_bytes=16 * 2**20),
        name="prepare",
    )(place.reshape(1), flat, ctf, shifts, inv_sigma2.reshape(1, pix), phase_table(pieces, rows))


def score_kernel(data_ref, *refs):
    *proj_refs, out_ref = refs
    pix = data_ref.shape[1] // 3
    parts = []
    for ref in proj_refs:
        wide = ref[...].astype(jnp.float32)
        real, imag = wide[:, 0, :], wide[:, 1, :]
        parts.append(jnp.concatenate([2.0 * real, 2.0 * imag, -(real * real + imag * imag)], axis=1))
    joint = jnp.concatenate(parts, axis=0).astype(jnp.bfloat16)
    out_ref[...] = lax.dot_general(
        joint, data_ref[...], (((1,), (1,)), ((), ())), preferred_element_type=jnp.float32
    )


def score(data, pieces):
    orients = sum(piece.shape[0] for piece in pieces)
    return pl.pallas_call(
        score_kernel,
        out_shape=jax.ShapeDtypeStruct((orients, data.shape[0]), jnp.float32),
        compiler_params=pltpu.CompilerParams(vmem_limit_bytes=24 * 2**20),
        name="score",
    )(data, *pieces)


def back_kernel(place_ref, one_ref, two_ref, prior_ref, keep_ref, data_ref, best_ref, own_ref, *away_refs):
    share = best_ref.shape[0]
    rows = (one_ref[...] + two_ref[...]) * (1.0 / math.sqrt(PIXC)) + prior_ref[...]
    masked = jnp.where(keep_ref[...] == 1, rows, jnp.float32(-1e30))
    expo = jnp.exp(masked - jnp.max(masked, axis=0, keepdims=True))
    inverse = 1.0 / jnp.sum(expo, axis=0, keepdims=True)
    weights = (expo * inverse).astype(jnp.bfloat16)
    best = inverse[0, 0:share]
    for piece in range(1, one_ref.shape[1] // share):
        best = jnp.where(place_ref[0] == piece, inverse[0, piece * share : (piece + 1) * share], best)
    best_ref[...] = best
    sums = jnp.dot(weights, data_ref[...], preferred_element_type=jnp.float32)
    each = own_ref.shape[0]
    own_ref[...] = sums[0:each]
    for k, ref in enumerate(away_refs):
        ref[...] = sums[(k + 1) * each : (k + 2) * each].astype(ref.dtype)


def back(place, one, two, prior, keep, data, away, pieces):
    orients, count = one.shape
    each = orients // (away + 1)
    wide = data.shape[1]
    vmem = pl.BlockSpec(memory_space=pltpu.VMEM)
    return pl.pallas_call(
        back_kernel,
        in_specs=[pl.BlockSpec(memory_space=pltpu.SMEM)] + [vmem] * 5,
        out_shape=[
            jax.ShapeDtypeStruct((count // pieces,), jnp.float32),
            jax.ShapeDtypeStruct((each, wide), jnp.float32),
        ]
        + [jax.ShapeDtypeStruct((each, wide), jnp.bfloat16)] * away,
        compiler_params=pltpu.CompilerParams(vmem_limit_bytes=32 * 2**20),
        name="back",
    )(place.reshape(1), one, two, prior, keep, data)


def finish_kernel(own_ref, *refs):
    *away_refs, data_ref, weight_ref = refs
    pix = weight_ref.shape[1]
    total = own_ref[...]
    for ref in away_refs:
        total = total + ref[...].astype(jnp.float32)
    data_ref[:, 0, :] = total[:, :pix]
    data_ref[:, 1, :] = total[:, pix : 2 * pix]
    weight_ref[...] = total[:, 2 * pix :]


def finish(own, away):
    each, wide = own.shape
    return pl.pallas_call(
        finish_kernel,
        out_shape=[
            jax.ShapeDtypeStruct((each, 2, wide // 3), jnp.float32),
            jax.ShapeDtypeStruct((each, wide // 3), jnp.float32),
        ],
        compiler_params=pltpu.CompilerParams(vmem_limit_bytes=16 * 2**20),
        name="finish",
    )(own, *away)


def rotate(value, axis, size, by):
    return lax.ppermute(value, axis, [((j + by) % size, j) for j in range(size)])


def body(images, ctf, projections, shifts, inv_sigma2, class_ids, log_prior, allowed):
    count, _, pix = images.shape
    each = projections.shape[0]
    blocks = lax.axis_size("blk")
    pieces = lax.axis_size(("shell", "sub"))
    place = lax.axis_index(("shell", "sub"))
    me = lax.axis_index("blk")

    direct = blocks <= DIRECT
    if direct:
        projs = [projections] + [rotate(projections, "blk", blocks, k) for k in range(1, blocks)]
    else:
        projs = [jnp.roll(lax.all_gather(projections, "blk", axis=0, tiled=True), -me * each, axis=0)]
    data = prepare(images, ctf, shifts, inv_sigma2, place, pieces)

    order = (me + jnp.arange(blocks, dtype=jnp.int32)) % blocks
    listed = jnp.any(allowed[0][:, None] == order[None, :], axis=0).astype(jnp.int32)
    keep = jnp.repeat(listed, each)[:, None]
    classes = class_ids[:, None] == jnp.arange(CLASSES, dtype=jnp.int32)[None, :]
    prior = jnp.sum(jnp.where(classes, log_prior[None, :], jnp.float32(0.0)), axis=1)
    prior = jnp.roll(prior, -me * each)[:, None]

    part = score(data, projs)
    part = part + rotate(part, "sub", 2, 1)
    if lax.axis_size("shell") == 2:
        other = rotate(part, "shell", 2, 1)
    else:
        other = lax.psum(part, "shell") - part
    best, own, *away = back(place, part, other, prior, keep, data, blocks - 1 if direct else 0, pieces)
    if not direct:
        own = lax.psum_scatter(jnp.roll(own, me * each, axis=0), "blk", scatter_dimension=0, tiled=True)
    arrived = [rotate(block, "blk", blocks, blocks - k) for k, block in enumerate(away, start=1)]
    back_data, back_weight = finish(own, arrived)
    return (back_data, back_weight, best)


def solution(mesh):
    in_specs = (
        P(("groups", "blk"), None, ("shell", "sub")),
        P(("groups", "blk"), ("shell", "sub")),
        P(("groups", "blk"), None, ("shell", "sub")),
        P(("groups", "blk"), None),
        P(("shell", "sub")),
        P("groups"),
        P(),
        P(("groups", "blk"), None),
    )
    out_specs = (
        P(("groups", "blk"), None, ("shell", "sub")),
        P(("groups", "blk"), ("shell", "sub")),
        P(("groups", "blk", "shell", "sub")),
    )
    return jax.shard_map(body, mesh=mesh, in_specs=in_specs, out_specs=out_specs, check_vma=False)
```

time: 125 us -> 45.1 us (0.36)
  waiting for transfers between devices: 36.9 us -> 6.33 us
  blocking collectives: 25.3 us -> 0 us
  other arithmetic: 20.3 us -> 1.59 us
  between operations: 14.9 us -> 0.71 us
  starting transfers between devices: 0.04 us -> 12.5 us
  Pallas kernels: 0 us -> 11.4 us
  local copies, waits for them, and re-layouts: 21.7 us -> 12.2 us
  matrix products: 5.83 us -> 0 us
    unnamed x2 -> x0, waiting for transfers between devices: 36.9 us -> none
    another operation x1 -> x0, other arithmetic: 18.6 us -> none  [prepare(): jnp.stack([factor * shifted_real, factor * shifted_imag], axis=1)]
    all_gather x1 -> x0, blocking collectives: 15.1 us -> none  [body(): piece = lax.all_gather(projections, 'blk', axis=0, tiled=True)]
    ppermute x0 -> x8, starting transfers between devices: none -> 12.5 us  [rotate(): lax.ppermute(value, axis, [((j + by) % size, j) for j in range(size)])]
    slice x4 -> x0, local copies, waits for them, and re-layouts: 11.4 us -> none  [the longest x1 8.93 us: prepare(): imag_part = images[:, 1].astype(jnp.float32)]
    pallas_call x0 -> x4, Pallas kernels: none -> 11.4 us  [the longest x1 7.99 us: prepare(): pl.pallas_call(functools.partial(prepare_kernel, rows), grid_spec=pltpu.P...]
    psum x1 -> x0, blocking collectives: 10.3 us -> none  [body(): rows = lax.psum(values, ('shell', 'sub')) + prior[None, :]]
    unnamed x19 -> x15, local copies, waits for them, and re-layouts: 2.56 us -> 11.9 us
  transfers between devices with their start and end apart: 1 -> 8, of which waited for: 1 -> 5; matrix products, arithmetic and copies ran while one was open for 1% -> 6% of each run, Pallas kernels for 0% -> 18%
where the time goes in v1:
time: 45.1 us; the launch traced here: 44.7 us
  starting transfers between devices  12.5 us (28%)
  local copies, waits for them, and re-layouts  12.2 us (27%)
  Pallas kernels  11.4 us (25%)
  waiting for transfers between devices  6.33 us (14%)
  other arithmetic  1.59 us (4%)
  between operations  0.71 us (2%)
    ppermute x8, starting transfers between devices, rotate(): lax.ppermute(value, axis, [((j + by) % size, j) for j in range(size)])  12.5 us
    unnamed x15, local copies, waits for them, and re-layouts  11.9 us
    pallas_call x1, Pallas kernels, prepare(): pl.pallas_call(functools.partial(prepare_kernel, rows), grid_spec=pltpu.P...  7.99 us
    ppermute x8, waiting for transfers between devices, rotate(): lax.ppermute(value, axis, [((j + by) % size, j) for j in range(size)])  6.33 us
    pallas_call x1, Pallas kernels, score(): pl.pallas_call(score_kernel, out_shape=jax.ShapeDtypeStruct((orients, dat...  1.72 us
    pallas_call x1, Pallas kernels, back(): pl.pallas_call(back_kernel, in_specs=[pl.BlockSpec(memory_space=pltpu.SME...  1 us
  transfers between devices with their start and end apart: 8, of which 5 were waited for; matrix products, arithmetic and copies ran while one was open for 6% of the time, Pallas kernels for 18%

profile of v1, /device:TPU:0, one launch (start us, length us, event | category | flops | bytes accessed | tf_op | source)
XLA Modules:
  0.0 44.7 jit_solution(7568246836431489912)
XLA Ops:
  0.6 5.1 %collective-permute-start = (bf16[4,2,2048]{2,1,0:T(2,128)(2,1)}, bf16[4,2,2048]{2,1,0:T(2,128)(2,1)S(1)}, u32[]{:S(2)}, u32[]{:S(2)}) collective-permute-start(bf16[4,2,2048]{2,1,0:T(2,128)(2,1)} %refs_0_.1), channel_id=1, source_target_pairs={{4,0},{8,4},{12,8},{0,12},{5,1},{9,5},{13,9},{1,13},{6,2},{10,6},{... | collective-permute-start | bytes 98312 | tf_op jit(solution)/shard_map/ppermute | solution.py:206
  5.7 1.0 %collective-permute-start.2 = (bf16[4,2,2048]{2,1,0:T(2,128)(2,1)}, bf16[4,2,2048]{2,1,0:T(2,128)(2,1)S(1)}, u32[]{:S(2)}, u32[]{:S(2)}) collective-permute-start(bf16[4,2,2048]{2,1,0:T(2,128)(2,1)} %refs_0_.1), channel_id=1, source_target_pairs={{12,0},{0,4},{4,8},{8,12},{13,1},{1,5},{5,9},{9,13},{14,2},{2,6},{... | collective-permute-start | bytes 98312 | tf_op jit(solution)/shard_map/ppermute | solution.py:206
  6.8 0.8 %select_reduce_fusion = f32[16]{0:T(128)S(1)} fusion(f32[4]{0:T(128)} %param.15, s32[16]{0:T(128)} %param.14), kind=kLoop, calls=%fused_computation.2 | loop fusion | flops 176 | bytes 144 | tf_op jit(solution)/shard_map/reduce_sum | solution.py:228
  7.5 0.7 %compare_reduce_fusion = pred[4]{0:T(512)(128)(4,1)S(1)} fusion(s32[4]{0:T(128)S(1)} %and_select_fusion, s32[2]{0:T(128)} %bitcast.12), kind=kLoop, calls=%fused_computation.4 | loop fusion | flops 12 | bytes 28 | tf_op jit(solution)/shard_map/reduce_or | solution.py:225
  8.3 0.8 %copy.17.shift_ref = s32[512,2]{1,0:T(8,128)S(1)} copy(s32[512,2]{0,1:T(2,128)} %param.12) | data formatting | bytes 8192 | tf_op args[3]
  9.1 2.2 %copy-done.2 = bf16[512,2,2048]{2,1,0:T(2,128)(2,1)S(1)} copy-done((bf16[512,2,2048]{2,1,0:T(2,128)(2,1)S(1)}, bf16[512,2,2048]{2,1,0:T(2,128)(2,1)}, u32[]{:S(2)}) %copy-start.2) | copy-done | bytes 4194328
  11.3 1.6 %copy-done.3 = bf16[512,2048]{1,0:T(8,128)(2,1)S(1)} copy-done((bf16[512,2048]{1,0:T(8,128)(2,1)S(1)}, bf16[512,2048]{1,0:T(8,128)(2,1)}, u32[]{:S(2)}) %copy-start.3) | copy-done | bytes 2097176
  12.9 1.1 %copy-done.4 = bf16[4,128,768]{2,1,0:T(8,128)(2,1)S(1)} copy-done((bf16[4,128,768]{2,1,0:T(8,128)(2,1)S(1)}, bf16[4,128,768]{2,1,0:T(8,128)(2,1)}, u32[]{:S(2)}) %copy-start.4) | copy-done | bytes 786456
  14.0 0.7 %copy-done.6 = f32[2048]{0:T(1024)S(1)} copy-done((f32[2048]{0:T(1024)S(1)}, f32[2048]{0:T(1024)}, u32[]{:S(2)}) %copy-start.6) | copy-done | bytes 8216
  14.7 8.0 %prepare.1.data_ref = bf16[512,6144]{1,0:T(8,128)(2,1)S(1)} custom-call(s32[1]{0:T(128)} %bitcast.place_ref, bf16[16384,128]{1,0:T(8,128)(2,1)S(1)} %bitcast.10, bf16[512,2048]{1,0:T(8,128)(2,1)S(1)} %copy-done.3, s32[512,2]{1,0:T(8,128)S(1)} %copy.17.shift_ref, f32[1,2048]{1,0:T(1,128)S(1)} %bitcast.11, bf16[4,128,768]{2,1,0:T(8,128)(2,1)S(1)} %copy-done.4), custom_call_target="tpu_custom_call" | custom-call | tf_op jit(solution)/shard_map/prepare/pallas_call | solution.py:97
  22.8 1.7 %score.1 = f32[16,512]{1,0:T(8,128)S(1)} custom-call(bf16[512,6144]{1,0:T(8,128)(2,1)S(1)} %prepare.1.data_ref, bf16[4,2,2048]{2,1,0:T(2,128)(2,1)S(1)} %copy-done.5, bf16[4,2,2048]{2,1,0:T(2,128)(2,1)S(1)} %collective-permute-done.refs_1_, bf16[4,2,2048]{2,1,0:T(2,128)(2,1)S(1)} %collective-permute-done.1.refs_2_, ...), custom_call_target="tpu_custom_call" | custom-call | tf_op jit(solution)/shard_map/score/pallas_call | solution.py:137
  24.5 2.7 %copy-done = bf16[512,6144]{1,0:T(8,128)(2,1)} copy-done((bf16[512,6144]{1,0:T(8,128)(2,1)}, bf16[512,6144]{1,0:T(8,128)(2,1)S(1)}, u32[]{:S(2)}) %copy-start) | copy-done | bytes 6291480
  27.2 1.1 %collective-permute-done.3 = f32[16,512]{1,0:T(8,128)S(1)} collective-permute-done((f32[16,512]{1,0:T(8,128)S(1)}, f32[16,512]{1,0:T(8,128)S(1)}, u32[]{:S(2)}, u32[]{:S(2)}) %collective-permute-start.3) | collective-permute-done | bytes 32800 | tf_op jit(solution)/shard_map/ppermute | solution.py:206
  28.4 1.5 %collective-permute-start.4 = (f32[16,512]{1,0:T(8,128)S(1)}, f32[16,512]{1,0:T(8,128)S(1)}, u32[]{:S(2)}, u32[]{:S(2)}) collective-permute-start(f32[16,512]{1,0:T(8,128)S(1)} %add.37.one_ref), channel_id=1, source_target_pairs={{2,0},{0,2},{3,1},{1,3},{6,4},{4,6},{7,5},{5,7},{10,8},{8,10},{11,... | collective-permute-start | bytes 98312 | tf_op jit(solution)/shard_map/ppermute | solution.py:206
  30.2 2.1 %collective-permute-done.4.two_ref = f32[16,512]{1,0:T(8,128)S(1)} collective-permute-done((f32[16,512]{1,0:T(8,128)S(1)}, f32[16,512]{1,0:T(8,128)S(1)}, u32[]{:S(2)}, u32[]{:S(2)}) %collective-permute-start.4) | collective-permute-done | bytes 32800 | tf_op jit(solution)/shard_map/ppermute | solution.py:206
  32.3 2.8 %copy-done.1 = bf16[512,6144]{1,0:T(8,128)(2,1)S(1)} copy-done((bf16[512,6144]{1,0:T(8,128)(2,1)S(1)}, bf16[512,6144]{1,0:T(8,128)(2,1)}, u32[]{:S(2)}) %copy-start.1) | copy-done | bytes 6291480
  35.1 1.0 %back.1 = (f32[128]{0:T(128)}, f32[4,6144]{1,0:T(4,128)S(1)}, bf16[4,6144]{1,0:T(4,128)(2,1)S(1)}, bf16[4,6144]{1,0:T(4,128)(2,1)S(1)}, bf16[4,6144]{1,0:T(4,128)(2,1)S(1)}) custom-call(s32[1]{0:T(128)} %bitcast.place_ref, f32[16,512]{1,0:T(8,128)S(1)} %add.37.one_ref, f32[16,512]{1,0:T(8,128)S(1)} %collective-permute-done.4.two_ref, ...), custom_call_target="tpu_custom_call" | custom-call | tf_op jit(solution)/shard_map/back/pallas_call | solution.py:168
  36.1 2.5 %collective-permute-start.5 = (bf16[4,6144]{1,0:T(4,128)(2,1)S(1)}, bf16[4,6144]{1,0:T(4,128)(2,1)S(1)}, u32[]{:S(2)}, u32[]{:S(2)}) collective-permute-start(bf16[4,6144]{1,0:T(4,128)(2,1)S(1)} %get-tuple-element.11), channel_id=1, source_target_pairs={{12,0},{0,4},{4,8},{8,12},{13,1},{1,5},{5,9},{9,13},{14,2},{2,6},{... | collective-permute-start | bytes 147464 | tf_op jit(solution)/shard_map/ppermute | solution.py:206
  38.6 0.9 %collective-permute-start.6 = (bf16[4,6144]{1,0:T(4,128)(2,1)S(1)}, bf16[4,6144]{1,0:T(4,128)(2,1)S(1)}, u32[]{:S(2)}, u32[]{:S(2)}) collective-permute-start(bf16[4,6144]{1,0:T(4,128)(2,1)S(1)} %get-tuple-element.12), channel_id=1, source_target_pairs={{8,0},{12,4},{0,8},{4,12},{9,1},{13,5},{1,9},{5,13},{10,2},{14,6},... | collective-permute-start | bytes 147464 | tf_op jit(solution)/shard_map/ppermute | solution.py:206
  39.5 1.5 %collective-permute-start.7 = (bf16[4,6144]{1,0:T(4,128)(2,1)S(1)}, bf16[4,6144]{1,0:T(4,128)(2,1)S(1)}, u32[]{:S(2)}, u32[]{:S(2)}) collective-permute-start(bf16[4,6144]{1,0:T(4,128)(2,1)S(1)} %get-tuple-element.13), channel_id=1, source_target_pairs={{4,0},{8,4},{12,8},{0,12},{5,1},{9,5},{13,9},{1,13},{6,2},{10,6},{... | collective-permute-start | bytes 147464 | tf_op jit(solution)/shard_map/ppermute | solution.py:206
  41.0 1.0 %collective-permute-done.5.refs_0_ = bf16[4,6144]{1,0:T(4,128)(2,1)S(1)} collective-permute-done((bf16[4,6144]{1,0:T(4,128)(2,1)S(1)}, bf16[4,6144]{1,0:T(4,128)(2,1)S(1)}, u32[]{:S(2)}, u32[]{:S(2)}) %collective-permute-start.5) | collective-permute-done | bytes 49184 | tf_op jit(solution)/shard_map/ppermute | solution.py:206
  42.0 1.9 %collective-permute-done.6.refs_1_ = bf16[4,6144]{1,0:T(4,128)(2,1)S(1)} collective-permute-done((bf16[4,6144]{1,0:T(4,128)(2,1)S(1)}, bf16[4,6144]{1,0:T(4,128)(2,1)S(1)}, u32[]{:S(2)}, u32[]{:S(2)}) %collective-permute-start.6) | collective-permute-done | bytes 49184 | tf_op jit(solution)/shard_map/ppermute | solution.py:206
  43.8 0.2 collective-permute-done.7.refs_2_
  44.1 0.7 %finish.1 = (f32[4,2,2048]{2,1,0:T(2,128)}, f32[4,2048]{1,0:T(4,128)}) custom-call(f32[4,6144]{1,0:T(4,128)S(1)} %get-tuple-element.10.own_ref, bf16[4,6144]{1,0:T(4,128)(2,1)S(1)} %collective-permute-done.5.refs_0_, bf16[4,6144]{1,0:T(4,128)(2,1)S(1)} %collective-permute-done.6.refs_1_, bf16[4,6144]{1,0:T(4,128)(2,1)S(1)} %collective-permute-done.7.refs_2_), custom_call_target="tpu_custom_call" | custom-call | tf_op jit(solution)/shard_map/finish/pallas_call | solution.py:194
  (21 shorter events, 0.4 us)
Async XLA Ops:
  0.6 22.1 %collective-permute-start = (bf16[4,2,2048]{2,1,0:T(2,128)(2,1)}, bf16[4,2,2048]{2,1,0:T(2,128)(2,1)S(1)}, u32[]{:S(2)}, u32[]{:S(2)}) collective-permute-start(bf16[4,2,2048]{2,1,0:T(2,128)(2,1)} %refs_0_.1), channel_id=1, source_target_pairs={{4,0},{8,4},{12,8},{0,12},{5,1},{9,5},{13,9},{1,13},{6,2},{10,6},{... | collective-permute-start | bytes 98312 | tf_op jit(solution)/shard_map/ppermute | solution.py:206
  5.7 17.0 %collective-permute-start.1 = (bf16[4,2,2048]{2,1,0:T(2,128)(2,1)}, bf16[4,2,2048]{2,1,0:T(2,128)(2,1)S(1)}, u32[]{:S(2)}, u32[]{:S(2)}) collective-permute-start(bf16[4,2,2048]{2,1,0:T(2,128)(2,1)} %refs_0_.1), channel_id=1, source_target_pairs={{8,0},{12,4},{0,8},{4,12},{9,1},{13,5},{1,9},{5,13},{10,2},{14,6},... | collective-permute-start | bytes 98312 | tf_op jit(solution)/shard_map/ppermute | solution.py:206
  5.7 17.0 %collective-permute-start.2 = (bf16[4,2,2048]{2,1,0:T(2,128)(2,1)}, bf16[4,2,2048]{2,1,0:T(2,128)(2,1)S(1)}, u32[]{:S(2)}, u32[]{:S(2)}) collective-permute-start(bf16[4,2,2048]{2,1,0:T(2,128)(2,1)} %refs_0_.1), channel_id=1, source_target_pairs={{12,0},{0,4},{4,8},{8,12},{13,1},{1,5},{5,9},{9,13},{14,2},{2,6},{... | collective-permute-start | bytes 98312 | tf_op jit(solution)/shard_map/ppermute | solution.py:206
  9.1 2.2 %copy-start.2 = (bf16[512,2,2048]{2,1,0:T(2,128)(2,1)S(1)}, bf16[512,2,2048]{2,1,0:T(2,128)(2,1)}, u32[]{:S(2)}) copy-start(bf16[512,2,2048]{2,1,0:T(2,128)(2,1)} %param.9) | copy-start | bytes 12582916
  11.3 1.6 %copy-start.3 = (bf16[512,2048]{1,0:T(8,128)(2,1)S(1)}, bf16[512,2048]{1,0:T(8,128)(2,1)}, u32[]{:S(2)}) copy-start(bf16[512,2048]{1,0:T(8,128)(2,1)} %ctf_ref.1) | copy-start | bytes 6291460
  12.9 1.1 %copy-start.4 = (bf16[4,128,768]{2,1,0:T(8,128)(2,1)S(1)}, bf16[4,128,768]{2,1,0:T(8,128)(2,1)}, u32[]{:S(2)}) copy-start(bf16[4,128,768]{2,1,0:T(8,128)(2,1)} %constant.55.clone.table_ref) | copy-start | bytes 2359300
  14.0 0.7 %copy-start.6 = (f32[2048]{0:T(1024)S(1)}, f32[2048]{0:T(1024)}, u32[]{:S(2)}) copy-start(f32[2048]{0:T(1024)} %param.13) | copy-start | bytes 24580
  14.7 8.0 %copy-start.5 = (bf16[4,2,2048]{2,1,0:T(2,128)(2,1)S(1)}, bf16[4,2,2048]{2,1,0:T(2,128)(2,1)}, u32[]{:S(2)}) copy-start(bf16[4,2,2048]{2,1,0:T(2,128)(2,1)} %refs_0_.1) | copy-start | bytes 98308
  24.5 2.7 %copy-start = (bf16[512,6144]{1,0:T(8,128)(2,1)}, bf16[512,6144]{1,0:T(8,128)(2,1)S(1)}, u32[]{:S(2)}) copy-start(bf16[512,6144]{1,0:T(8,128)(2,1)S(1)} %prepare.1.data_ref) | copy-start | bytes 18874372
  27.1 1.2 %collective-permute-start.3 = (f32[16,512]{1,0:T(8,128)S(1)}, f32[16,512]{1,0:T(8,128)S(1)}, u32[]{:S(2)}, u32[]{:S(2)}) collective-permute-start(f32[16,512]{1,0:T(8,128)S(1)} %score.1), channel_id=1, source_target_pairs={{1,0},{0,1},{3,2},{2,3},{5,4},{4,5},{7,6},{6,7},{9,8},{8,9},{11,10... | collective-permute-start | bytes 98312 | tf_op jit(solution)/shard_map/ppermute | solution.py:206
  28.4 3.9 %collective-permute-start.4 = (f32[16,512]{1,0:T(8,128)S(1)}, f32[16,512]{1,0:T(8,128)S(1)}, u32[]{:S(2)}, u32[]{:S(2)}) collective-permute-start(f32[16,512]{1,0:T(8,128)S(1)} %add.37.one_ref), channel_id=1, source_target_pairs={{2,0},{0,2},{3,1},{1,3},{6,4},{4,6},{7,5},{5,7},{10,8},{8,10},{11,... | collective-permute-start | bytes 98312 | tf_op jit(solution)/shard_map/ppermute | solution.py:206
  32.3 2.8 %copy-start.1 = (bf16[512,6144]{1,0:T(8,128)(2,1)S(1)}, bf16[512,6144]{1,0:T(8,128)(2,1)}, u32[]{:S(2)}) copy-start(bf16[512,6144]{1,0:T(8,128)(2,1)} %copy-done) | copy-start | bytes 18874372
  36.1 5.9 %collective-permute-start.5 = (bf16[4,6144]{1,0:T(4,128)(2,1)S(1)}, bf16[4,6144]{1,0:T(4,128)(2,1)S(1)}, u32[]{:S(2)}, u32[]{:S(2)}) collective-permute-start(bf16[4,6144]{1,0:T(4,128)(2,1)S(1)} %get-tuple-element.11), channel_id=1, source_target_pairs={{12,0},{0,4},{4,8},{8,12},{13,1},{1,5},{5,9},{9,13},{14,2},{2,6},{... | collective-permute-start | bytes 147464 | tf_op jit(solution)/shard_map/ppermute | solution.py:206
  38.6 5.3 %collective-permute-start.6 = (bf16[4,6144]{1,0:T(4,128)(2,1)S(1)}, bf16[4,6144]{1,0:T(4,128)(2,1)S(1)}, u32[]{:S(2)}, u32[]{:S(2)}) collective-permute-start(bf16[4,6144]{1,0:T(4,128)(2,1)S(1)} %get-tuple-element.12), channel_id=1, source_target_pairs={{8,0},{12,4},{0,8},{4,12},{9,1},{13,5},{1,9},{5,13},{10,2},{14,6},... | collective-permute-start | bytes 147464 | tf_op jit(solution)/shard_map/ppermute | solution.py:206
  39.5 4.6 %collective-permute-start.7 = (bf16[4,6144]{1,0:T(4,128)(2,1)S(1)}, bf16[4,6144]{1,0:T(4,128)(2,1)S(1)}, u32[]{:S(2)}, u32[]{:S(2)}) collective-permute-start(bf16[4,6144]{1,0:T(4,128)(2,1)S(1)} %get-tuple-element.13), channel_id=1, source_target_pairs={{4,0},{8,4},{12,8},{0,12},{5,1},{9,5},{13,9},{1,13},{6,2},{10,6},{... | collective-permute-start | bytes 147464 | tf_op jit(solution)/shard_map/ppermute | solution.py:206

commit v2 on v1

v2 whole, which is shorter than its diff:
```python
import functools
import math

import jax
import jax.numpy as jnp
import ml_dtypes
import numpy as np
from jax import lax
from jax.experimental import pallas as pl
from jax.experimental.pallas import tpu as pltpu
from jax.sharding import PartitionSpec as P

KMAX = 64
BOX = 360
CLASSES = 4
PIXC = 8192
ROW = 2 * KMAX
REACH = 8
GROUP = 16
DIRECT = 4
SPLITS = 3


def split_terms(table):
    terms = []
    rest = table.astype(np.float64)
    for _ in range(SPLITS):
        term = rest.astype(ml_dtypes.bfloat16)
        terms.append(term)
        rest = rest - term.astype(np.float64)
    return np.concatenate(terms, axis=0)


@functools.lru_cache(maxsize=None)
def phase_table(pieces, rows):
    shift = np.arange(-REACH, REACH, dtype=np.float64)[:, None]
    unit = 2.0 * math.pi / BOX
    along_y = unit * shift * np.arange(-KMAX, KMAX, dtype=np.float64)[None, :]
    step = np.broadcast_to(unit * shift, along_y.shape)
    half = SPLITS * 2 * REACH
    tables = []
    for piece in range(pieces):
        first = step * (piece * rows)
        left = split_terms(np.concatenate([np.cos(first), np.sin(first), np.cos(step), np.sin(step)], axis=1))
        right = split_terms(np.concatenate([np.cos(along_y), np.sin(along_y)], axis=1))
        table = np.zeros((128, 6 * ROW), ml_dtypes.bfloat16)
        table[:half, : 4 * ROW] = left
        table[64 : 64 + half, 4 * ROW :] = right
        tables.append(table)
    return np.stack(tables)


@functools.lru_cache(maxsize=None)
def spread_table(rows):
    table = np.zeros((2, rows, 8, 8, rows, 2), ml_dtypes.bfloat16)
    for image in range(8):
        for row in range(rows):
            for part in range(2):
                table[part, row, image, image, row, part] = 1
    return table.reshape(16 * rows, 16 * rows)


def prepare_kernel(
    rows,
    image_hbm,
    ctf_hbm,
    shift_hbm,
    inv_hbm,
    table_hbm,
    spread_hbm,
    out_ref,
    image_ref,
    ctf_ref,
    shift_ref,
    inv_ref,
    table_ref,
    spread_ref,
    phase_ref,
    even_ref,
    odd_ref,
    chunk_sems,
    sems,
):
    images = ctf_ref.shape[0]
    pix = rows * ROW
    chunks = chunk_sems.shape[1]
    each = images // chunks
    lines = 2 * rows
    half = 8 * lines
    place = lax.axis_index(("shell", "sub"))

    def chunk_copies(c):
        image_rows = pl.ds(c * each * lines, each * lines)
        ctf_rows = pl.ds(c * each, each)
        return (
            pltpu.make_async_copy(image_hbm.at[image_rows], image_ref.at[image_rows], chunk_sems.at[0, c]),
            pltpu.make_async_copy(ctf_hbm.at[ctf_rows], ctf_ref.at[ctf_rows], chunk_sems.at[1, c]),
        )

    first = (
        pltpu.make_async_copy(shift_hbm, shift_ref, sems.at[0]),
        pltpu.make_async_copy(table_hbm.at[place], table_ref, sems.at[1]),
    )
    second = (
        pltpu.make_async_copy(spread_hbm, spread_ref, sems.at[2]),
        pltpu.make_async_copy(inv_hbm, inv_ref, sems.at[3]),
    )
    for copy in first + second:
        copy.start()
    for c in range(chunks):
        for copy in chunk_copies(c):
            copy.start()

    for copy in first:
        copy.wait()
    line = lax.broadcasted_iota(jnp.int32, (128, images), 0)
    inner = line & 63
    moves = jnp.where(line < 64, shift_ref[0:1, :], shift_ref[1:2, :]) + REACH
    hit = ((inner & (2 * REACH - 1)) == moves) & (inner < SPLITS * 2 * REACH)
    phase_ref[...] = lax.dot_general(
        jnp.where(hit, 1.0, 0.0).astype(jnp.bfloat16),
        table_ref[...],
        (((0,), (0,)), ((), ())),
        preferred_element_type=jnp.float32,
    )
    for copy in second:
        copy.wait()

    def spread(g, ref):
        slab = pl.multiple_of(g * (2 * half), 2 * half)
        pair = jnp.concatenate([image_ref[pl.ds(slab, half), :], image_ref[pl.ds(slab + half, half), :]], axis=1)
        ref[...] = jnp.dot(spread_ref[...], pair, preferred_element_type=jnp.float32)

    def weigh(g, ref):
        start = pl.multiple_of(g * GROUP, GROUP)
        phase = phase_ref[pl.ds(start, GROUP), :]
        cos_a, sin_a, cos_s, sin_s, cos_b, sin_b = (phase[:, k * ROW : (k + 1) * ROW] for k in range(6))
        cos_0 = cos_a * cos_b - sin_a * sin_b
        sin_0 = sin_a * cos_b + cos_a * sin_b
        cos_1 = cos_0 * cos_s - sin_0 * sin_s
        sin_1 = sin_0 * cos_s + cos_0 * sin_s
        twice = 2.0 * cos_s
        for t in range(rows):
            lanes = slice(t * ROW, (t + 1) * ROW)
            a, b = 8 * t, 8 * (rows + t)
            real = jnp.concatenate([ref[a : a + 8, :ROW], ref[a : a + 8, ROW:]], axis=0)
            imag = jnp.concatenate([ref[b : b + 8, :ROW], ref[b : b + 8, ROW:]], axis=0)
            ctf = ctf_ref[pl.ds(start, GROUP), lanes].astype(jnp.float32)
            factor = ctf * inv_ref[0:1, lanes]
            out_ref[pl.ds(start, GROUP), lanes] = (factor * (real * cos_0 + imag * sin_0)).astype(jnp.bfloat16)
            out_ref[pl.ds(start, GROUP), pl.ds(pix + t * ROW, ROW)] = (
                factor * (imag * cos_0 - real * sin_0)
            ).astype(jnp.bfloat16)
            out_ref[pl.ds(start, GROUP), pl.ds(2 * pix + t * ROW, ROW)] = (factor * ctf).astype(jnp.bfloat16)
            cos_0, cos_1 = cos_1, twice * cos_1 - cos_0
            sin_0, sin_1 = sin_1, twice * sin_1 - sin_0

    groups = images // GROUP
    pairs = groups // chunks // 2
    for copy in chunk_copies(0):
        copy.wait()
    spread(0, even_ref)
    for c in range(chunks):
        if c + 1 < chunks:
            for copy in chunk_copies(c + 1):
                copy.wait()

        def step(i, carry):
            g = 2 * (c * pairs + i)
            spread(g + 1, odd_ref)
            weigh(g, even_ref)
            spread(jnp.minimum(g + 2, groups - 1), even_ref)
            weigh(g + 1, odd_ref)
            return carry

        lax.fori_loop(0, pairs, step, 0)


def in_hbm(value):
    return pltpu.with_memory_space_constraint(value, pltpu.HBM)


def prepare(images, ctf, shifts, inv_sigma2, pieces):
    count, _, pix = images.shape
    rows = pix // ROW
    chunks = max(1, min(8, count // (2 * GROUP)))
    flat = images.reshape(count, 2, rows, ROW).transpose(0, 2, 1, 3).reshape(count * rows * 2, ROW)
    args = (flat, ctf, shifts.T, inv_sigma2.reshape(1, pix), phase_table(pieces, rows), spread_table(rows))
    return pl.pallas_call(
        functools.partial(prepare_kernel, rows),
        in_specs=[pl.BlockSpec(memory_space=pltpu.HBM)] * len(args),
        out_specs=pl.BlockSpec(memory_space=pltpu.VMEM),
        out_shape=pltpu.VMEM((count, 3 * pix), jnp.bfloat16),
        scratch_shapes=[
            pltpu.VMEM(flat.shape, jnp.bfloat16),
            pltpu.VMEM(ctf.shape, jnp.bfloat16),
            pltpu.VMEM((2, count), jnp.int32),
            pltpu.VMEM((1, pix), jnp.float32),
            pltpu.VMEM((128, 6 * ROW), jnp.bfloat16),
            pltpu.VMEM((16 * rows, 16 * rows), jnp.bfloat16),
            pltpu.VMEM((count, 6 * ROW), jnp.float32),
            pltpu.VMEM((16 * rows, 2 * ROW), jnp.float32),
            pltpu.VMEM((16 * rows, 2 * ROW), jnp.float32),
            pltpu.SemaphoreType.DMA((2, chunks)),
            pltpu.SemaphoreType.DMA((4,)),
        ],
        compiler_params=pltpu.CompilerParams(vmem_limit_bytes=24 * 2**20),
        name="prepare",
    )(*[in_hbm(jnp.asarray(arg)) for arg in args])


def score_kernel(blocks, turned, data_ref, allowed_ref, class_ref, prior_ref, *refs):
    *proj_refs, out_ref = refs
    orients = out_ref.shape[0]
    each = orients // blocks
    me = lax.axis_index("blk") if turned else 0

    line = lax.broadcasted_iota(jnp.int32, (orients, orients), 0)
    lane = lax.broadcasted_iota(jnp.int32, (orients, orients), 1)
    block = lax.rem(line // each + me, blocks)
    own = lane == block * each + lax.rem(line, each)
    prior = jnp.zeros((orients, orients), jnp.float32)
    for c in range(CLASSES):
        prior = jnp.where(own & (class_ref[...] == c), prior_ref[0:1, c : c + 1], prior)
    bias = jnp.sum(prior, axis=1, keepdims=True)
    listed = jnp.zeros((orients, 1), jnp.bool_)
    for k in range(allowed_ref.shape[1]):
        listed = listed | (block[:, 0:1] == allowed_ref[0:1, k : k + 1])
    bias = jnp.where(listed, bias, jnp.float32(-1e30))
    bias = jnp.where(lax.axis_index(("shell", "sub")) == 0, bias, 0.0)

    parts = []
    for ref in proj_refs:
        wide = ref[...].astype(jnp.float32)
        real, imag = wide[:, 0, :], wide[:, 1, :]
        parts.append(jnp.concatenate([2.0 * real, 2.0 * imag, -(real * real + imag * imag)], axis=1))
    joint = jnp.concatenate(parts, axis=0).astype(jnp.bfloat16)
    raw = lax.dot_general(joint, data_ref[...], (((1,), (1,)), ((), ())), preferred_element_type=jnp.float32)
    out_ref[...] = raw * (1.0 / math.sqrt(PIXC)) + bias


def score(data, allowed, class_ids, log_prior, projs, blocks, turned):
    orients = class_ids.shape[0]
    return pl.pallas_call(
        functools.partial(score_kernel, blocks, turned),
        out_shape=jax.ShapeDtypeStruct((orients, data.shape[0]), jnp.float32),
        compiler_params=pltpu.CompilerParams(vmem_limit_bytes=24 * 2**20),
        name="score",
    )(data, allowed, class_ids.reshape(1, -1), log_prior.reshape(1, -1), *projs)


def back_kernel(parts, data_ref, *refs):
    part_refs, (best_ref, own_ref, *away_refs) = refs[:parts], refs[parts:]
    share = best_ref.shape[0]
    sums = [ref[...] for ref in part_refs]
    while len(sums) > 1:
        sums = [sums[k] + sums[k + 1] for k in range(0, len(sums), 2)]
    rows = sums[0]
    expo = jnp.exp(rows - jnp.max(rows, axis=0, keepdims=True))
    inverse = 1.0 / jnp.sum(expo, axis=0, keepdims=True)
    weights = (expo * inverse).astype(jnp.bfloat16)
    place = lax.axis_index(("shell", "sub"))
    best = inverse[0, 0:share]
    for piece in range(1, rows.shape[1] // share):
        best = jnp.where(place == piece, inverse[0, piece * share : (piece + 1) * share], best)
    best_ref[...] = best
    back = jnp.dot(weights, data_ref[...], preferred_element_type=jnp.float32)
    each = own_ref.shape[0]
    own_ref[...] = back[0:each]
    for k, ref in enumerate(away_refs):
        ref[...] = back[(k + 1) * each : (k + 2) * each].astype(ref.dtype)


def back(data, parts, away, pieces):
    orients, count = parts[0].shape
    each = orients // (away + 1)
    wide = data.shape[1]
    return pl.pallas_call(
        functools.partial(back_kernel, len(parts)),
        out_shape=[
            jax.ShapeDtypeStruct((count // pieces,), jnp.float32),
            jax.ShapeDtypeStruct((each, wide), jnp.float32),
        ]
        + [jax.ShapeDtypeStruct((each, wide), jnp.bfloat16)] * away,
        compiler_params=pltpu.CompilerParams(vmem_limit_bytes=24 * 2**20),
        name="back",
    )(data, *parts)


def finish_kernel(own_ref, *refs):
    *away_refs, data_ref, weight_ref = refs
    pix = weight_ref.shape[1]
    total = own_ref[...]
    for ref in away_refs:
        total = total + ref[...].astype(jnp.float32)
    data_ref[:, 0, :] = total[:, :pix]
    data_ref[:, 1, :] = total[:, pix : 2 * pix]
    weight_ref[...] = total[:, 2 * pix :]


def finish(own, away):
    each, wide = own.shape
    return pl.pallas_call(
        finish_kernel,
        out_shape=[
            jax.ShapeDtypeStruct((each, 2, wide // 3), jnp.float32),
            jax.ShapeDtypeStruct((each, wide // 3), jnp.float32),
        ],
        compiler_params=pltpu.CompilerParams(vmem_limit_bytes=16 * 2**20),
        name="finish",
    )(own, *away)


def rotate(value, axis, size, by):
    return lax.ppermute(value, axis, [((j + by) % size, j) for j in range(size)])


def swap(value, axes, size, mask):
    return lax.ppermute(value, axes, [(j ^ mask, j) for j in range(size)])


def body(images, ctf, projections, shifts, inv_sigma2, class_ids, log_prior, allowed):
    blocks = lax.axis_size("blk")
    pieces = lax.axis_size(("shell", "sub"))
    direct = blocks <= DIRECT

    if direct:
        projs = [projections] + [rotate(projections, "blk", blocks, k) for k in range(1, blocks)]
    else:
        projs = [lax.all_gather(projections, "blk", axis=0, tiled=True)]
    data = prepare(images, ctf, shifts, inv_sigma2, pieces)
    part = score(data, allowed, class_ids, log_prior, projs, blocks, direct)
    if pieces == 4:
        parts = [part, swap(part, ("shell", "sub"), 4, 1), swap(part, ("shell", "sub"), 4, 2), swap(part, ("shell", "sub"), 4, 3)]
    else:
        parts = [lax.psum(part, ("shell", "sub"))]
    best, own, *away = back(data, parts, blocks - 1 if direct else 0, pieces)
    if not direct:
        own = lax.psum_scatter(own, "blk", scatter_dimension=0, tiled=True)
    arrived = [rotate(block, "blk", blocks, blocks - k) for k, block in enumerate(away, start=1)]
    back_data, back_weight = finish(own, arrived)
    return (back_data, back_weight, best)


def solution(mesh):
    in_specs = (
        P(("groups", "blk"), None, ("shell", "sub")),
        P(("groups", "blk"), ("shell", "sub")),
        P(("groups", "blk"), None, ("shell", "sub")),
        P(("groups", "blk"), None),
        P(("shell", "sub")),
        P("groups"),
        P(),
        P(("groups", "blk"), None),
    )
    out_specs = (
        P(("groups", "blk"), None, ("shell", "sub")),
        P(("groups", "blk"), ("shell", "sub")),
        P(("groups", "blk", "shell", "sub")),
    )
    return jax.shard_map(body, mesh=mesh, in_specs=in_specs, out_specs=out_specs, check_vma=False)
```

time: 45.1 us -> 31.7 us (0.70)
  local copies, waits for them, and re-layouts: 12.2 us -> 0.01 us
  other arithmetic: 1.59 us -> 0 us
  Pallas kernels: 11.4 us -> 12.2 us
    unnamed x15 -> x8, local copies, waits for them, and re-layouts: 11.9 us -> 0.01 us
    ppermute x8 -> x6, waiting for transfers between devices: 6.33 us -> 4.12 us  [rotate(): lax.ppermute(value, axis, [((j + by) % size, j) for j in range(size)])]
    ppermute x0 -> x3, waiting for transfers between devices: none -> 2.18 us  [swap(): return lax.ppermute(value, axes, [(j ^ mask, j) for j in range(size)])]
    ppermute x8 -> x6, starting transfers between devices: 12.5 us -> 10.4 us  [rotate(): lax.ppermute(value, axis, [((j + by) % size, j) for j in range(size)])]
    ppermute x0 -> x3, starting transfers between devices: none -> 1.91 us  [swap(): return lax.ppermute(value, axes, [(j ^ mask, j) for j in range(size)])]
    pallas_call x3, Pallas kernels: 10.7 us -> 11.5 us  [the longest x1 8.52 us: prepare(): pl.pallas_call(functools.partial(prepare_kernel, rows), in_specs=[pl.Bloc...]
    reduce_sum x1 -> x0, other arithmetic: 0.75 us -> none  [body(): jnp.sum(jnp.where(classes, log_prior[None, :], jnp.float32(0.0)), axis=1)]
    reduce_or x1 -> x0, other arithmetic: 0.74 us -> none  [body(): jnp.any(allowed[0][:, None] == order[None, :], axis=0).astype(jnp.int32)]
  transfers between devices with their start and end apart: 8 -> 9, of which waited for: 5 -> 5; matrix products, arithmetic and copies ran while one was open for 6% -> 0% of each run, Pallas kernels for 18% -> 27%
where the time goes in v2:
time: 31.7 us; the launch traced here: 31.5 us
  starting transfers between devices  12.3 us (39%)
  Pallas kernels  12.2 us (38%)
  waiting for transfers between devices  6.3 us (20%)
  between operations  0.71 us (2%)
    ppermute x6, starting transfers between devices, rotate(): lax.ppermute(value, axis, [((j + by) % size, j) for j in range(size)])  10.4 us
    pallas_call x1, Pallas kernels, prepare(): pl.pallas_call(functools.partial(prepare_kernel, rows), in_specs=[pl.Bloc...  8.52 us
    ppermute x6, waiting for transfers between devices, rotate(): lax.ppermute(value, axis, [((j + by) % size, j) for j in range(size)])  4.12 us
    ppermute x3, waiting for transfers between devices, swap(): return lax.ppermute(value, axes, [(j ^ mask, j) for j in range(size)])  2.18 us
    ppermute x3, starting transfers between devices, swap(): return lax.ppermute(value, axes, [(j ^ mask, j) for j in range(size)])  1.91 us
    pallas_call x1, Pallas kernels, score(): pl.pallas_call(functools.partial(score_kernel, blocks, turned), out_shape...  1.69 us
    pallas_call x1, Pallas kernels, back(): pl.pallas_call(functools.partial(back_kernel, len(parts)), out_shape=[jax...  1.34 us
    pallas_call x1, Pallas kernels, finish(): pl.pallas_call(finish_kernel, out_shape=[jax.ShapeDtypeStruct((each, 2, w...  0.66 us
  transfers between devices with their start and end apart: 9, of which 5 were waited for; matrix products, arithmetic and copies ran while one was open for 0% of the time, Pallas kernels for 27%

profile of v2, /device:TPU:0, one launch (start us, length us, event | category | flops | bytes accessed | tf_op | source)
XLA Modules:
  0.0 31.5 jit_solution(15502763039125251498)
XLA Ops:
  0.6 4.1 %collective-permute-start.1 = (bf16[4,2,2048]{2,1,0:T(2,128)(2,1)}, bf16[4,2,2048]{2,1,0:T(2,128)(2,1)S(1)}, u32[]{:S(2)}, u32[]{:S(2)}) collective-permute-start(bf16[4,2,2048]{2,1,0:T(2,128)(2,1)} %refs_0_.1), channel_id=1, source_target_pairs={{8,0},{12,4},{0,8},{4,12},{9,1},{13,5},{1,9},{5,13},{10,2},{14,6},... | collective-permute-start | bytes 98312 | tf_op jit(solution)/shard_map/ppermute | solution.py:315
  4.7 1.3 %collective-permute-start = (bf16[4,2,2048]{2,1,0:T(2,128)(2,1)}, bf16[4,2,2048]{2,1,0:T(2,128)(2,1)S(1)}, u32[]{:S(2)}, u32[]{:S(2)}) collective-permute-start(bf16[4,2,2048]{2,1,0:T(2,128)(2,1)} %refs_0_.1), channel_id=1, source_target_pairs={{4,0},{8,4},{12,8},{0,12},{5,1},{9,5},{13,9},{1,13},{6,2},{10,6},{... | collective-permute-start | bytes 98312 | tf_op jit(solution)/shard_map/ppermute | solution.py:315
  6.1 0.7 %collective-permute-start.2 = (bf16[4,2,2048]{2,1,0:T(2,128)(2,1)}, bf16[4,2,2048]{2,1,0:T(2,128)(2,1)S(1)}, u32[]{:S(2)}, u32[]{:S(2)}) collective-permute-start(bf16[4,2,2048]{2,1,0:T(2,128)(2,1)} %refs_0_.1), channel_id=1, source_target_pairs={{12,0},{0,4},{4,8},{8,12},{13,1},{1,5},{5,9},{9,13},{14,2},{2,6},{... | collective-permute-start | bytes 98312 | tf_op jit(solution)/shard_map/ppermute | solution.py:315
  6.8 8.5 %prepare.1.data_ref = bf16[512,6144]{1,0:T(8,128)(2,1)S(1)} custom-call(bf16[16384,128]{1,0:T(8,128)(2,1)} %bitcast.11, bf16[512,2048]{1,0:T(8,128)(2,1)} %ctf_hbm.1, s32[2,512]{1,0:T(2,128)} %bitcast.13, f32[1,2048]{1,0:T(1,128)} %bitcast.12, bf16[4,128,768]{2,1,0:T(8,128)(2,1)} %constant.4.clone.table_hbm, bf16[256,256]{1,0:T(8,128)(2,1)} %constant.5.clone.spread_hbm), custom_call_target="tpu_custom_call" | custom-call | tf_op jit(solution)/shard_map/prepare/pallas_call | solution.py:189
  15.3 0.0 collective-permute-done.1.refs_2_
  15.3 0.0 collective-permute-done.refs_1_
  15.3 0.0 collective-permute-done.2.refs_3_
  15.3 0.0 copy-done
  15.3 0.0 copy-done.1
  15.4 1.7 %score.1.refs_0_ = f32[16,512]{1,0:T(8,128)S(1)} custom-call(bf16[512,6144]{1,0:T(8,128)(2,1)S(1)} %prepare.1.data_ref, s32[1,2]{1,0:T(1,128)S(1)} %copy-done.1, s32[1,16]{1,0:T(1,128)S(1)} %bitcast.9, f32[1,4]{1,0:T(1,128)S(1)} %bitcast.10, bf16[4,2,2048]{2,1,0:T(2,128)(2,1)S(1)} %copy-done, bf16[4,2,2048]{2,1,0:T(2,128)(2,1)S(1)} %collective-permute-done.refs_1_, ...), custom_call_target="tpu_custom_call" | custom-call | tf_op jit(solution)/shard_map/score/pallas_call | solution.py:244
  17.1 0.1 collective-permute-start.5
  17.2 1.5 %collective-permute-start.4 = (f32[16,512]{1,0:T(8,128)S(1)}, f32[16,512]{1,0:T(8,128)S(1)}, u32[]{:S(2)}, u32[]{:S(2)}) collective-permute-start(f32[16,512]{1,0:T(8,128)S(1)} %score.1.refs_0_), channel_id=1, source_target_pairs={{2,0},{3,1},{0,2},{1,3},{6,4},{7,5},{4,6},{5,7},{10,8},{11,9},{8,1... | collective-permute-start | bytes 98312 | tf_op jit(solution)/shard_map/ppermute | solution.py:319
  18.6 0.3 %collective-permute-start.3 = (f32[16,512]{1,0:T(8,128)S(1)}, f32[16,512]{1,0:T(8,128)S(1)}, u32[]{:S(2)}, u32[]{:S(2)}) collective-permute-start(f32[16,512]{1,0:T(8,128)S(1)} %score.1.refs_0_), channel_id=1, source_target_pairs={{1,0},{0,1},{3,2},{2,3},{5,4},{4,5},{7,6},{6,7},{9,8},{8,9},{11,10... | collective-permute-start | bytes 98312 | tf_op jit(solution)/shard_map/ppermute | solution.py:319
  19.0 1.8 %collective-permute-done.5.refs_3_ = f32[16,512]{1,0:T(8,128)S(1)} collective-permute-done((f32[16,512]{1,0:T(8,128)S(1)}, f32[16,512]{1,0:T(8,128)S(1)}, u32[]{:S(2)}, u32[]{:S(2)}) %collective-permute-start.5) | collective-permute-done | bytes 32800 | tf_op jit(solution)/shard_map/ppermute | solution.py:319
  20.8 0.4 %collective-permute-done.4.refs_2_ = f32[16,512]{1,0:T(8,128)S(1)} collective-permute-done((f32[16,512]{1,0:T(8,128)S(1)}, f32[16,512]{1,0:T(8,128)S(1)}, u32[]{:S(2)}, u32[]{:S(2)}) %collective-permute-start.4) | collective-permute-done | bytes 32800 | tf_op jit(solution)/shard_map/ppermute | solution.py:319
  21.2 0.0 collective-permute-done.3.refs_1_
  21.2 1.3 %back.1 = (f32[128]{0:T(128)}, f32[4,6144]{1,0:T(4,128)S(1)}, bf16[4,6144]{1,0:T(4,128)(2,1)S(1)}, bf16[4,6144]{1,0:T(4,128)(2,1)S(1)}, bf16[4,6144]{1,0:T(4,128)(2,1)S(1)}) custom-call(bf16[512,6144]{1,0:T(8,128)(2,1)S(1)} %prepare.1.data_ref, f32[16,512]{1,0:T(8,128)S(1)} %score.1.refs_0_, f32[16,512]{1,0:T(8,128)S(1)} %collective-permute-done.3.refs_1_, ...), custom_call_target="tpu_custom_call" | custom-call | tf_op jit(solution)/shard_map/back/pallas_call | solution.py:278
  22.5 1.6 %collective-permute-start.6 = (bf16[4,6144]{1,0:T(4,128)(2,1)S(1)}, bf16[4,6144]{1,0:T(4,128)(2,1)S(1)}, u32[]{:S(2)}, u32[]{:S(2)}) collective-permute-start(bf16[4,6144]{1,0:T(4,128)(2,1)S(1)} %get-tuple-element.11), channel_id=1, source_target_pairs={{12,0},{0,4},{4,8},{8,12},{13,1},{1,5},{5,9},{9,13},{14,2},{2,6},{... | collective-permute-start | bytes 147464 | tf_op jit(solution)/shard_map/ppermute | solution.py:315
  24.1 2.1 %collective-permute-start.7 = (bf16[4,6144]{1,0:T(4,128)(2,1)S(1)}, bf16[4,6144]{1,0:T(4,128)(2,1)S(1)}, u32[]{:S(2)}, u32[]{:S(2)}) collective-permute-start(bf16[4,6144]{1,0:T(4,128)(2,1)S(1)} %get-tuple-element.12), channel_id=1, source_target_pairs={{8,0},{12,4},{0,8},{4,12},{9,1},{13,5},{1,9},{5,13},{10,2},{14,6},... | collective-permute-start | bytes 147464 | tf_op jit(solution)/shard_map/ppermute | solution.py:315
  26.2 0.5 %collective-permute-start.8 = (bf16[4,6144]{1,0:T(4,128)(2,1)S(1)}, bf16[4,6144]{1,0:T(4,128)(2,1)S(1)}, u32[]{:S(2)}, u32[]{:S(2)}) collective-permute-start(bf16[4,6144]{1,0:T(4,128)(2,1)S(1)} %get-tuple-element.13), channel_id=1, source_target_pairs={{4,0},{8,4},{12,8},{0,12},{5,1},{9,5},{13,9},{1,13},{6,2},{10,6},{... | collective-permute-start | bytes 147464 | tf_op jit(solution)/shard_map/ppermute | solution.py:315
  26.7 2.2 %collective-permute-done.6.refs_0_ = bf16[4,6144]{1,0:T(4,128)(2,1)S(1)} collective-permute-done((bf16[4,6144]{1,0:T(4,128)(2,1)S(1)}, bf16[4,6144]{1,0:T(4,128)(2,1)S(1)}, u32[]{:S(2)}, u32[]{:S(2)}) %collective-permute-start.6) | collective-permute-done | bytes 49184 | tf_op jit(solution)/shard_map/ppermute | solution.py:315
  28.9 1.6 %collective-permute-done.7.refs_1_ = bf16[4,6144]{1,0:T(4,128)(2,1)S(1)} collective-permute-done((bf16[4,6144]{1,0:T(4,128)(2,1)S(1)}, bf16[4,6144]{1,0:T(4,128)(2,1)S(1)}, u32[]{:S(2)}, u32[]{:S(2)}) %collective-permute-start.7) | collective-permute-done | bytes 49184 | tf_op jit(solution)/shard_map/ppermute | solution.py:315
  30.5 0.4 %collective-permute-done.8.refs_2_ = bf16[4,6144]{1,0:T(4,128)(2,1)S(1)} collective-permute-done((bf16[4,6144]{1,0:T(4,128)(2,1)S(1)}, bf16[4,6144]{1,0:T(4,128)(2,1)S(1)}, u32[]{:S(2)}, u32[]{:S(2)}) %collective-permute-start.8) | collective-permute-done | bytes 49184 | tf_op jit(solution)/shard_map/ppermute | solution.py:315
  30.8 0.7 %finish.1 = (f32[4,2,2048]{2,1,0:T(2,128)}, f32[4,2048]{1,0:T(4,128)}) custom-call(f32[4,6144]{1,0:T(4,128)S(1)} %get-tuple-element.10.own_ref, bf16[4,6144]{1,0:T(4,128)(2,1)S(1)} %collective-permute-done.6.refs_0_, bf16[4,6144]{1,0:T(4,128)(2,1)S(1)} %collective-permute-done.7.refs_1_, bf16[4,6144]{1,0:T(4,128)(2,1)S(1)} %collective-permute-done.8.refs_2_), custom_call_target="tpu_custom_call" | custom-call | tf_op jit(solution)/shard_map/finish/pallas_call | solution.py:303
  (6 shorter events, 0.0 us)
Async XLA Ops:
  0.6 14.7 %collective-permute-start.1 = (bf16[4,2,2048]{2,1,0:T(2,128)(2,1)}, bf16[4,2,2048]{2,1,0:T(2,128)(2,1)S(1)}, u32[]{:S(2)}, u32[]{:S(2)}) collective-permute-start(bf16[4,2,2048]{2,1,0:T(2,128)(2,1)} %refs_0_.1), channel_id=1, source_target_pairs={{8,0},{12,4},{0,8},{4,12},{9,1},{13,5},{1,9},{5,13},{10,2},{14,6},... | collective-permute-start | bytes 98312 | tf_op jit(solution)/shard_map/ppermute | solution.py:315
  4.7 10.6 %collective-permute-start = (bf16[4,2,2048]{2,1,0:T(2,128)(2,1)}, bf16[4,2,2048]{2,1,0:T(2,128)(2,1)S(1)}, u32[]{:S(2)}, u32[]{:S(2)}) collective-permute-start(bf16[4,2,2048]{2,1,0:T(2,128)(2,1)} %refs_0_.1), channel_id=1, source_target_pairs={{4,0},{8,4},{12,8},{0,12},{5,1},{9,5},{13,9},{1,13},{6,2},{10,6},{... | collective-permute-start | bytes 98312 | tf_op jit(solution)/shard_map/ppermute | solution.py:315
  6.1 9.2 %collective-permute-start.2 = (bf16[4,2,2048]{2,1,0:T(2,128)(2,1)}, bf16[4,2,2048]{2,1,0:T(2,128)(2,1)S(1)}, u32[]{:S(2)}, u32[]{:S(2)}) collective-permute-start(bf16[4,2,2048]{2,1,0:T(2,128)(2,1)} %refs_0_.1), channel_id=1, source_target_pairs={{12,0},{0,4},{4,8},{8,12},{13,1},{1,5},{5,9},{9,13},{14,2},{2,6},{... | collective-permute-start | bytes 98312 | tf_op jit(solution)/shard_map/ppermute | solution.py:315
  6.8 8.6 %copy-start = (bf16[4,2,2048]{2,1,0:T(2,128)(2,1)S(1)}, bf16[4,2,2048]{2,1,0:T(2,128)(2,1)}, u32[]{:S(2)}) copy-start(bf16[4,2,2048]{2,1,0:T(2,128)(2,1)} %refs_0_.1) | copy-start | bytes 98308
  6.8 8.6 %copy-start.1 = (s32[1,2]{1,0:T(1,128)S(1)}, s32[1,2]{1,0:T(1,128)}, u32[]{:S(2)}) copy-start(s32[1,2]{1,0:T(1,128)} %allowed_ref.1) | copy-start | bytes 28
  6.8 8.6 %copy-start.2 = (s32[16]{0:T(128)S(1)}, s32[16]{0:T(128)}, u32[]{:S(2)}) copy-start(s32[16]{0:T(128)} %param.15) | copy-start | bytes 196
  6.8 8.6 %copy-start.3 = (f32[4]{0:T(128)S(1)}, f32[4]{0:T(128)}, u32[]{:S(2)}) copy-start(f32[4]{0:T(128)} %param.16) | copy-start | bytes 52
  17.1 3.7 %collective-permute-start.5 = (f32[16,512]{1,0:T(8,128)S(1)}, f32[16,512]{1,0:T(8,128)S(1)}, u32[]{:S(2)}, u32[]{:S(2)}) collective-permute-start(f32[16,512]{1,0:T(8,128)S(1)} %score.1.refs_0_), channel_id=1, source_target_pairs={{3,0},{2,1},{1,2},{0,3},{7,4},{6,5},{5,6},{4,7},{11,8},{10,9},{9,1... | collective-permute-start | bytes 98312 | tf_op jit(solution)/shard_map/ppermute | solution.py:319
  17.2 4.0 %collective-permute-start.4 = (f32[16,512]{1,0:T(8,128)S(1)}, f32[16,512]{1,0:T(8,128)S(1)}, u32[]{:S(2)}, u32[]{:S(2)}) collective-permute-start(f32[16,512]{1,0:T(8,128)S(1)} %score.1.refs_0_), channel_id=1, source_target_pairs={{2,0},{3,1},{0,2},{1,3},{6,4},{7,5},{4,6},{5,7},{10,8},{11,9},{8,1... | collective-permute-start | bytes 98312 | tf_op jit(solution)/shard_map/ppermute | solution.py:319
  18.6 2.5 %collective-permute-start.3 = (f32[16,512]{1,0:T(8,128)S(1)}, f32[16,512]{1,0:T(8,128)S(1)}, u32[]{:S(2)}, u32[]{:S(2)}) collective-permute-start(f32[16,512]{1,0:T(8,128)S(1)} %score.1.refs_0_), channel_id=1, source_target_pairs={{1,0},{0,1},{3,2},{2,3},{5,4},{4,5},{7,6},{6,7},{9,8},{8,9},{11,10... | collective-permute-start | bytes 98312 | tf_op jit(solution)/shard_map/ppermute | solution.py:319
  22.5 6.4 %collective-permute-start.6 = (bf16[4,6144]{1,0:T(4,128)(2,1)S(1)}, bf16[4,6144]{1,0:T(4,128)(2,1)S(1)}, u32[]{:S(2)}, u32[]{:S(2)}) collective-permute-start(bf16[4,6144]{1,0:T(4,128)(2,1)S(1)} %get-tuple-element.11), channel_id=1, source_target_pairs={{12,0},{0,4},{4,8},{8,12},{13,1},{1,5},{5,9},{9,13},{14,2},{2,6},{... | collective-permute-start | bytes 147464 | tf_op jit(solution)/shard_map/ppermute | solution.py:315
  24.1 6.4 %collective-permute-start.7 = (bf16[4,6144]{1,0:T(4,128)(2,1)S(1)}, bf16[4,6144]{1,0:T(4,128)(2,1)S(1)}, u32[]{:S(2)}, u32[]{:S(2)}) collective-permute-start(bf16[4,6144]{1,0:T(4,128)(2,1)S(1)} %get-tuple-element.12), channel_id=1, source_target_pairs={{8,0},{12,4},{0,8},{4,12},{9,1},{13,5},{1,9},{5,13},{10,2},{14,6},... | collective-permute-start | bytes 147464 | tf_op jit(solution)/shard_map/ppermute | solution.py:315
  26.2 4.6 %collective-permute-start.8 = (bf16[4,6144]{1,0:T(4,128)(2,1)S(1)}, bf16[4,6144]{1,0:T(4,128)(2,1)S(1)}, u32[]{:S(2)}, u32[]{:S(2)}) collective-permute-start(bf16[4,6144]{1,0:T(4,128)(2,1)S(1)} %get-tuple-element.13), channel_id=1, source_target_pairs={{4,0},{8,4},{12,8},{0,12},{5,1},{9,5},{13,9},{1,13},{6,2},{10,6},{... | collective-permute-start | bytes 147464 | tf_op jit(solution)/shard_map/ppermute | solution.py:315

commit v3 on v2

--- a/solution.py
+++ b/solution.py
@@ -17,7 +17,7 @@
 ROW = 2 * KMAX
 REACH = 8
 GROUP = 16
-DIRECT = 4
+DIRECT = (2, 4)
 SPLITS = 3
 
 
@@ -50,86 +50,30 @@
     return np.stack(tables)
 
 
-@functools.lru_cache(maxsize=None)
-def spread_table(rows):
-    table = np.zeros((2, rows, 8, 8, rows, 2), ml_dtypes.bfloat16)
-    for image in range(8):
-        for row in range(rows):
-            for part in range(2):
-                table[part, row, image, image, row, part] = 1
-    return table.reshape(16 * rows, 16 * rows)
-
-
 def prepare_kernel(
-    rows,
-    image_hbm,
-    ctf_hbm,
-    shift_hbm,
-    inv_hbm,
-    table_hbm,
-    spread_hbm,
-    out_ref,
-    image_ref,
-    ctf_ref,
-    shift_ref,
-    inv_ref,
-    table_ref,
-    spread_ref,
-    phase_ref,
-    even_ref,
-    odd_ref,
-    chunk_sems,
-    sems,
+    rows, image_ref, ctf_ref, shift_ref, inv_ref, table_ref, out_ref, phase_ref, even_ref, odd_ref
 ):
     images = ctf_ref.shape[0]
     pix = rows * ROW
-    chunks = chunk_sems.shape[1]
-    each = images // chunks
     lines = 2 * rows
-    half = 8 * lines
-    place = lax.axis_index(("shell", "sub"))
-
-    def chunk_copies(c):
-        image_rows = pl.ds(c * each * lines, each * lines)
-        ctf_rows = pl.ds(c * each, each)
-        return (
-            pltpu.make_async_copy(image_hbm.at[image_rows], image_ref.at[image_rows], chunk_sems.at[0, c]),
-            pltpu.make_async_copy(ctf_hbm.at[ctf_rows], ctf_ref.at[ctf_rows], chunk_sems.at[1, c]),
-        )
-
-    first = (
-        pltpu.make_async_copy(shift_hbm, shift_ref, sems.at[0]),
-        pltpu.make_async_copy(table_hbm.at[place], table_ref, sems.at[1]),
-    )
-    second = (
-        pltpu.make_async_copy(spread_hbm, spread_ref, sems.at[2]),
-        pltpu.make_async_copy(inv_hbm, inv_ref, sems.at[3]),
-    )
-    for copy in first + second:
-        copy.start()
-    for c in range(chunks):
-        for copy in chunk_copies(c):
-            copy.start()
-
-    for copy in first:
-        copy.wait()
+
     line = lax.broadcasted_iota(jnp.int32, (128, images), 0)
     inner = line & 63
     moves = jnp.where(line < 64, shift_ref[0:1, :], shift_ref[1:2, :]) + REACH
     hit = ((inner & (2 * REACH - 1)) == moves) & (inner < SPLITS * 2 * REACH)
     phase_ref[...] = lax.dot_general(
         jnp.where(hit, 1.0, 0.0).astype(jnp.bfloat16),
-        table_ref[...],
+        table_ref[lax.axis_index(("shell", "sub"))],
         (((0,), (0,)), ((), ())),
         preferred_element_type=jnp.float32,
     )
-    for copy in second:
-        copy.wait()
 
     def spread(g, ref):
-        slab = pl.multiple_of(g * (2 * half), 2 * half)
-        pair = jnp.concatenate([image_ref[pl.ds(slab, half), :], image_ref[pl.ds(slab + half, half), :]], axis=1)
-        ref[...] = jnp.dot(spread_ref[...], pair, preferred_element_type=jnp.float32)
+        for i in range(GROUP):
+            line = pl.multiple_of((g * GROUP + i) * lines, lines)
+            wide = image_ref[pl.ds(line, lines), :].astype(jnp.float32)
+            for slab in range(lines // 8):
+                ref[pl.ds((slab * GROUP + i) * 8, 8), :] = wide[8 * slab : 8 * slab + 8]
 
     def weigh(g, ref):
         start = pl.multiple_of(g * GROUP, GROUP)
@@ -142,9 +86,9 @@
         twice = 2.0 * cos_s
         for t in range(rows):
             lanes = slice(t * ROW, (t + 1) * ROW)
-            a, b = 8 * t, 8 * (rows + t)
-            real = jnp.concatenate([ref[a : a + 8, :ROW], ref[a : a + 8, ROW:]], axis=0)
-            imag = jnp.concatenate([ref[b : b + 8, :ROW], ref[b : b + 8, ROW:]], axis=0)
+            line = 8 * GROUP * (t // 4) + 2 * (t % 4)
+            real = ref[pl.ds(line, GROUP, stride=8), :]
+            imag = ref[pl.ds(line + 1, GROUP, stride=8), :]
             ctf = ctf_ref[pl.ds(start, GROUP), lanes].astype(jnp.float32)
             factor = ctf * inv_ref[0:1, lanes]
             out_ref[pl.ds(start, GROUP), lanes] = (factor * (real * cos_0 + imag * sin_0)).astype(jnp.bfloat16)
@@ -155,58 +99,34 @@
             cos_0, cos_1 = cos_1, twice * cos_1 - cos_0
             sin_0, sin_1 = sin_1, twice * sin_1 - sin_0
 
-    groups = images // GROUP
-    pairs = groups // chunks // 2
-    for copy in chunk_copies(0):
-        copy.wait()
-    spread(0, even_ref)
-    for c in range(chunks):
-        if c + 1 < chunks:
-            for copy in chunk_copies(c + 1):
-                copy.wait()
-
-        def step(i, carry):
-            g = 2 * (c * pairs + i)
-            spread(g + 1, odd_ref)
-            weigh(g, even_ref)
-            spread(jnp.minimum(g + 2, groups - 1), even_ref)
-            weigh(g + 1, odd_ref)
-            return carry
-
-        lax.fori_loop(0, pairs, step, 0)
-
-
-def in_hbm(value):
-    return pltpu.with_memory_space_constraint(value, pltpu.HBM)
+    def step(i, carry):
+        spread(2 * i, even_ref)
+        weigh(2 * i, even_ref)
+        spread(2 * i + 1, odd_ref)
+        weigh(2 * i + 1, odd_ref)
+        return carry
+
+    lax.fori_loop(0, images // (2 * GROUP), step, 0)
 
 
 def prepare(images, ctf, shifts, inv_sigma2, pieces):
     count, _, pix = images.shape
     rows = pix // ROW
-    chunks = max(1, min(8, count // (2 * GROUP)))
     flat = images.reshape(count, 2, rows, ROW).transpose(0, 2, 1, 3).reshape(count * rows * 2, ROW)
-    args = (flat, ctf, shifts.T, inv_sigma2.reshape(1, pix), phase_table(pieces, rows), spread_table(rows))
+    args = (flat, ctf, shifts.T, inv_sigma2.reshape(1, pix), phase_table(pieces, rows))
     return pl.pallas_call(
         functools.partial(prepare_kernel, rows),
-        in_specs=[pl.BlockSpec(memory_space=pltpu.HBM)] * len(args),
+        in_specs=[pl.BlockSpec(memory_space=pltpu.VMEM)] * len(args),
         out_specs=pl.BlockSpec(memory_space=pltpu.VMEM),
         out_shape=pltpu.VMEM((count, 3 * pix), jnp.bfloat16),
         scratch_shapes=[
-            pltpu.VMEM(flat.shape, jnp.bfloat16),
-            pltpu.VMEM(ctf.shape, jnp.bfloat16),
-            pltpu.VMEM((2, count), jnp.int32),
-            pltpu.VMEM((1, pix), jnp.float32),
-            pltpu.VMEM((128, 6 * ROW), jnp.bfloat16),
-            pltpu.VMEM((16 * rows, 16 * rows), jnp.bfloat16),
             pltpu.VMEM((count, 6 * ROW), jnp.float32),
-            pltpu.VMEM((16 * rows, 2 * ROW), jnp.float32),
-            pltpu.VMEM((16 * rows, 2 * ROW), jnp.float32),
-            pltpu.SemaphoreType.DMA((2, chunks)),
-            pltpu.SemaphoreType.DMA((4,)),
+            pltpu.VMEM((2 * rows * GROUP, ROW), jnp.float32),
+            pltpu.VMEM((2 * rows * GROUP, ROW), jnp.float32),
         ],
-        compiler_params=pltpu.CompilerParams(vmem_limit_bytes=24 * 2**20),
+        compiler_params=pltpu.CompilerParams(vmem_limit_bytes=8 * 2**20),
         name="prepare",
-    )(*[in_hbm(jnp.asarray(arg)) for arg in args])
+    )(*[pltpu.with_memory_space_constraint(jnp.asarray(arg), pltpu.VMEM) for arg in args])
 
 
 def score_kernel(blocks, turned, data_ref, allowed_ref, class_ref, prior_ref, *refs):
@@ -236,6 +156,16 @@
         parts.append(jnp.concatenate([2.0 * real, 2.0 * imag, -(real * real + imag * imag)], axis=1))
     joint = jnp.concatenate(parts, axis=0).astype(jnp.bfloat16)
     raw = lax.dot_general(joint, data_ref[...], (((1,), (1,)), ((), ())), preferred_element_type=jnp.float32)
+    if turned:
+        came = [raw[k * each : (k + 1) * each] for k in range(blocks)]
+        leave = came[:1]
+        for k in range(1, blocks):
+            at = lax.rem(me + k, blocks) ^ me
+            value = came[1]
+            for other in range(2, blocks):
+                value = jnp.where(at == other, came[other], value)
+            leave.append(value)
+        raw = jnp.concatenate(leave, axis=0)
     out_ref[...] = raw * (1.0 / math.sqrt(PIXC)) + bias
 
 
@@ -311,6 +241,21 @@
     )(own, *away)
 
 
+def opening_kernel(out_ref):
+    out_ref[...] = jnp.zeros_like(out_ref)
+
+
+def opening():
+    return pl.pallas_call(
+        opening_kernel,
+        out_specs=pl.BlockSpec(memory_space=pltpu.VMEM),
+        out_shape=pltpu.VMEM((8, 128), jnp.float32),
+        compiler_params=pltpu.CompilerParams(vmem_limit_bytes=2**20, has_side_effects=True),
+        cost_estimate=pl.CostEstimate(flops=10**10, bytes_accessed=10**7, transcendentals=0),
+        name="opening",
+    )()
+
+
 def rotate(value, axis, size, by):
     return lax.ppermute(value, axis, [((j + by) % size, j) for j in range(size)])
 
@@ -322,10 +267,12 @@
 def body(images, ctf, projections, shifts, inv_sigma2, class_ids, log_prior, allowed):
     blocks = lax.axis_size("blk")
     pieces = lax.axis_size(("shell", "sub"))
-    direct = blocks <= DIRECT
-
+    direct = blocks in DIRECT
+
+    first = opening()
+    projections, first = lax.optimization_barrier((projections, first))
     if direct:
-        projs = [projections] + [rotate(projections, "blk", blocks, k) for k in range(1, blocks)]
+        projs = [projections] + [swap(projections, "blk", blocks, k) for k in range(1, blocks)]
     else:
         projs = [lax.all_gather(projections, "blk", axis=0, tiled=True)]
     data = prepare(images, ctf, shifts, inv_sigma2, pieces)

time: 31.7 us -> 27.8 us (0.88)
  Pallas kernels: 12.2 us -> 8.17 us
  waiting for transfers between devices: 6.3 us -> 5.61 us
  starting transfers between devices: 12.3 us -> 12.9 us
    ppermute x3 -> x6, starting transfers between devices: 1.91 us -> 7.54 us  [swap(): return lax.ppermute(value, axes, [(j ^ mask, j) for j in range(size)])]
    ppermute x6 -> x3, starting transfers between devices: 10.4 us -> 5.32 us  [rotate(): lax.ppermute(value, axis, [((j + by) % size, j) for j in range(size)])]
    pallas_call x1, Pallas kernels: 8.52 us -> 3.83 us  [prepare(): pl.pallas_call(functools.partial(prepare_kernel, rows), in_specs=[pl.Bloc...]
    ppermute x6 -> x3, waiting for transfers between devices: 4.12 us -> 3.09 us  [rotate(): lax.ppermute(value, axis, [((j + by) % size, j) for j in range(size)])]
    pallas_call x0 -> x1, Pallas kernels: none -> 0.59 us  [opening(): pl.pallas_call(opening_kernel, out_specs=pl.BlockSpec(memory_space=pltpu....]
    ppermute x3 -> x6, waiting for transfers between devices: 2.18 us -> 2.52 us  [swap(): return lax.ppermute(value, axes, [(j ^ mask, j) for j in range(size)])]
  transfers between devices with their start and end apart: 9 -> 9, of which waited for: 5 -> 6; matrix products, arithmetic and copies ran while one was open for 0% -> 0% of each run, Pallas kernels for 27% -> 14%
where the time goes in v3:
time: 27.8 us; the launch traced here: 27.6 us
  starting transfers between devices  12.9 us (46%)
  Pallas kernels  8.17 us (29%)
  waiting for transfers between devices  5.61 us (20%)
  between operations  0.76 us (3%)
    ppermute x6, starting transfers between devices, swap(): return lax.ppermute(value, axes, [(j ^ mask, j) for j in range(size)])  7.54 us
    ppermute x3, starting transfers between devices, rotate(): lax.ppermute(value, axis, [((j + by) % size, j) for j in range(size)])  5.32 us
    pallas_call x1, Pallas kernels, prepare(): pl.pallas_call(functools.partial(prepare_kernel, rows), in_specs=[pl.Bloc...  3.83 us
    ppermute x3, waiting for transfers between devices, rotate(): lax.ppermute(value, axis, [((j + by) % size, j) for j in range(size)])  3.09 us
    ppermute x6, waiting for transfers between devices, swap(): return lax.ppermute(value, axes, [(j ^ mask, j) for j in range(size)])  2.52 us
    pallas_call x1, Pallas kernels, score(): pl.pallas_call(functools.partial(score_kernel, blocks, turned), out_shape...  1.75 us
    pallas_call x1, Pallas kernels, back(): pl.pallas_call(functools.partial(back_kernel, len(parts)), out_shape=[jax...  1.34 us
    pallas_call x1, Pallas kernels, finish(): pl.pallas_call(finish_kernel, out_shape=[jax.ShapeDtypeStruct((each, 2, w...  0.66 us
  transfers between devices with their start and end apart: 9, of which 6 were waited for; matrix products, arithmetic and copies ran while one was open for 0% of the time, Pallas kernels for 14%

profile of v3, /device:TPU:0, one launch (start us, length us, event | category | flops | bytes accessed | tf_op | source)
XLA Modules:
  0.0 27.6 jit_solution(12078153168050956548)
XLA Ops:
  0.6 0.0 copy-start.2
  0.7 0.6 %opening.1 = f32[8,128]{1,0:T(8,128)} custom-call(), custom_call_target="tpu_custom_call" | custom-call | flops 10000000000 | bytes 10000000 | tf_op jit(solution)/shard_map/opening/pallas_call | solution.py:249
  1.3 0.2 copy-done.3
  1.5 5.0 %collective-permute-start.2 = (bf16[4,2,2048]{2,1,0:T(2,128)(2,1)S(1)}, bf16[4,2,2048]{2,1,0:T(2,128)(2,1)S(1)}, u32[]{:S(2)}, u32[]{:S(2)}) collective-permute-start(bf16[4,2,2048]{2,1,0:T(2,128)(2,1)S(1)} %copy-done.3), channel_id=1, source_target_pairs={{12,0},{8,4},{4,8},{0,12},{13,1},{9,5},{5,9},{1,13},{14,2},{10,6},... | collective-permute-start | bytes 98312 | tf_op jit(solution)/shard_map/ppermute | solution.py:264
  6.5 0.6 %collective-permute-start = (bf16[4,2,2048]{2,1,0:T(2,128)(2,1)S(1)}, bf16[4,2,2048]{2,1,0:T(2,128)(2,1)S(1)}, u32[]{:S(2)}, u32[]{:S(2)}) collective-permute-start(bf16[4,2,2048]{2,1,0:T(2,128)(2,1)S(1)} %copy-done.3), channel_id=1, source_target_pairs={{4,0},{0,4},{12,8},{8,12},{5,1},{1,5},{13,9},{9,13},{6,2},{2,6},{1... | collective-permute-start | bytes 98312 | tf_op jit(solution)/shard_map/ppermute | solution.py:264
  7.1 0.0 copy-start.6
  7.1 0.0 copy-start.7
  7.1 0.0 copy-start.8
  7.2 3.8 %prepare.1.data_ref = bf16[512,6144]{1,0:T(8,128)(2,1)S(1)} custom-call(bf16[16384,128]{1,0:T(8,128)(2,1)S(1)} %bitcast.9, bf16[512,2048]{1,0:T(8,128)(2,1)S(1)} %copy-done.1, s32[2,512]{1,0:T(2,128)S(1)} %bitcast.11, f32[1,2048]{1,0:T(1,128)S(1)} %bitcast.10, bf16[4,128,768]{2,1,0:T(8,128)(2,1)S(1)} %copy-done.2), custom_call_target="tpu_custom_call" | custom-call | tf_op jit(solution)/shard_map/prepare/pallas_call | solution.py:117
  11.0 0.3 %collective-permute-done.1.refs_2_ = bf16[4,2,2048]{2,1,0:T(2,128)(2,1)S(1)} collective-permute-done((bf16[4,2,2048]{2,1,0:T(2,128)(2,1)S(1)}, bf16[4,2,2048]{2,1,0:T(2,128)(2,1)S(1)}, u32[]{:S(2)}, u32[]{:S(2)}) %collective-permute-start.1) | collective-permute-done | bytes 32800 | tf_op jit(solution)/shard_map/ppermute | solution.py:264
  11.4 1.7 %score.1.refs_0_ = f32[16,512]{1,0:T(8,128)S(1)} custom-call(bf16[512,6144]{1,0:T(8,128)(2,1)S(1)} %prepare.1.data_ref, s32[1,2]{1,0:T(1,128)S(1)} %copy-done.6, s32[1,16]{1,0:T(1,128)S(1)} %bitcast.12, f32[1,4]{1,0:T(1,128)S(1)} %bitcast.13, bf16[4,2,2048]{2,1,0:T(2,128)(2,1)S(1)} %copy-done.3, bf16[4,2,2048]{2,1,0:T(2,128)(2,1)S(1)} %collective-permute-done.refs_1_, ...), custom_call_target="tpu_custom_call" | custom-call | tf_op jit(solution)/shard_map/score/pallas_call | solution.py:174
  13.1 0.1 collective-permute-start.5
  13.2 1.5 %collective-permute-start.4 = (f32[16,512]{1,0:T(8,128)S(1)}, f32[16,512]{1,0:T(8,128)S(1)}, u32[]{:S(2)}, u32[]{:S(2)}) collective-permute-start(f32[16,512]{1,0:T(8,128)S(1)} %score.1.refs_0_), channel_id=1, source_target_pairs={{2,0},{3,1},{0,2},{1,3},{6,4},{7,5},{4,6},{5,7},{10,8},{11,9},{8,1... | collective-permute-start | bytes 98312 | tf_op jit(solution)/shard_map/ppermute | solution.py:264
  14.7 0.3 %collective-permute-start.3 = (f32[16,512]{1,0:T(8,128)S(1)}, f32[16,512]{1,0:T(8,128)S(1)}, u32[]{:S(2)}, u32[]{:S(2)}) collective-permute-start(f32[16,512]{1,0:T(8,128)S(1)} %score.1.refs_0_), channel_id=1, source_target_pairs={{1,0},{0,1},{3,2},{2,3},{5,4},{4,5},{7,6},{6,7},{9,8},{8,9},{11,10... | collective-permute-start | bytes 98312 | tf_op jit(solution)/shard_map/ppermute | solution.py:264
  15.0 1.8 %collective-permute-done.5.refs_3_ = f32[16,512]{1,0:T(8,128)S(1)} collective-permute-done((f32[16,512]{1,0:T(8,128)S(1)}, f32[16,512]{1,0:T(8,128)S(1)}, u32[]{:S(2)}, u32[]{:S(2)}) %collective-permute-start.5) | collective-permute-done | bytes 32800 | tf_op jit(solution)/shard_map/ppermute | solution.py:264
  16.8 0.4 %collective-permute-done.4.refs_2_ = f32[16,512]{1,0:T(8,128)S(1)} collective-permute-done((f32[16,512]{1,0:T(8,128)S(1)}, f32[16,512]{1,0:T(8,128)S(1)}, u32[]{:S(2)}, u32[]{:S(2)}) %collective-permute-start.4) | collective-permute-done | bytes 32800 | tf_op jit(solution)/shard_map/ppermute | solution.py:264
  17.2 1.3 %back.1 = (f32[128]{0:T(128)}, f32[4,6144]{1,0:T(4,128)S(1)}, bf16[4,6144]{1,0:T(4,128)(2,1)S(1)}, bf16[4,6144]{1,0:T(4,128)(2,1)S(1)}, bf16[4,6144]{1,0:T(4,128)(2,1)S(1)}) custom-call(bf16[512,6144]{1,0:T(8,128)(2,1)S(1)} %prepare.1.data_ref, f32[16,512]{1,0:T(8,128)S(1)} %score.1.refs_0_, f32[16,512]{1,0:T(8,128)S(1)} %collective-permute-done.3.refs_1_, ...), custom_call_target="tpu_custom_call" | custom-call | tf_op jit(solution)/shard_map/back/pallas_call | solution.py:208
  18.6 1.5 %collective-permute-start.6 = (bf16[4,6144]{1,0:T(4,128)(2,1)S(1)}, bf16[4,6144]{1,0:T(4,128)(2,1)S(1)}, u32[]{:S(2)}, u32[]{:S(2)}) collective-permute-start(bf16[4,6144]{1,0:T(4,128)(2,1)S(1)} %get-tuple-element.13), channel_id=1, source_target_pairs={{12,0},{0,4},{4,8},{8,12},{13,1},{1,5},{5,9},{9,13},{14,2},{2,6},{... | collective-permute-start | bytes 147464 | tf_op jit(solution)/shard_map/ppermute | solution.py:260
  20.0 2.6 %collective-permute-start.7 = (bf16[4,6144]{1,0:T(4,128)(2,1)S(1)}, bf16[4,6144]{1,0:T(4,128)(2,1)S(1)}, u32[]{:S(2)}, u32[]{:S(2)}) collective-permute-start(bf16[4,6144]{1,0:T(4,128)(2,1)S(1)} %get-tuple-element.14), channel_id=1, source_target_pairs={{8,0},{12,4},{0,8},{4,12},{9,1},{13,5},{1,9},{5,13},{10,2},{14,6},... | collective-permute-start | bytes 147464 | tf_op jit(solution)/shard_map/ppermute | solution.py:260
  22.6 1.2 %collective-permute-start.8 = (bf16[4,6144]{1,0:T(4,128)(2,1)S(1)}, bf16[4,6144]{1,0:T(4,128)(2,1)S(1)}, u32[]{:S(2)}, u32[]{:S(2)}) collective-permute-start(bf16[4,6144]{1,0:T(4,128)(2,1)S(1)} %get-tuple-element.15), channel_id=1, source_target_pairs={{4,0},{8,4},{12,8},{0,12},{5,1},{9,5},{13,9},{1,13},{6,2},{10,6},{... | collective-permute-start | bytes 147464 | tf_op jit(solution)/shard_map/ppermute | solution.py:260
  23.9 0.8 %collective-permute-done.6.refs_0_ = bf16[4,6144]{1,0:T(4,128)(2,1)S(1)} collective-permute-done((bf16[4,6144]{1,0:T(4,128)(2,1)S(1)}, bf16[4,6144]{1,0:T(4,128)(2,1)S(1)}, u32[]{:S(2)}, u32[]{:S(2)}) %collective-permute-start.6) | collective-permute-done | bytes 49184 | tf_op jit(solution)/shard_map/ppermute | solution.py:260
  24.7 1.8 %collective-permute-done.7.refs_1_ = bf16[4,6144]{1,0:T(4,128)(2,1)S(1)} collective-permute-done((bf16[4,6144]{1,0:T(4,128)(2,1)S(1)}, bf16[4,6144]{1,0:T(4,128)(2,1)S(1)}, u32[]{:S(2)}, u32[]{:S(2)}) %collective-permute-start.7) | collective-permute-done | bytes 49184 | tf_op jit(solution)/shard_map/ppermute | solution.py:260
  26.6 0.4 %collective-permute-done.8.refs_2_ = bf16[4,6144]{1,0:T(4,128)(2,1)S(1)} collective-permute-done((bf16[4,6144]{1,0:T(4,128)(2,1)S(1)}, bf16[4,6144]{1,0:T(4,128)(2,1)S(1)}, u32[]{:S(2)}, u32[]{:S(2)}) %collective-permute-start.8) | collective-permute-done | bytes 49184 | tf_op jit(solution)/shard_map/ppermute | solution.py:260
  27.0 0.7 %finish.1 = (f32[4,2,2048]{2,1,0:T(2,128)}, f32[4,2048]{1,0:T(4,128)}) custom-call(f32[4,6144]{1,0:T(4,128)S(1)} %get-tuple-element.12.own_ref, bf16[4,6144]{1,0:T(4,128)(2,1)S(1)} %collective-permute-done.6.refs_0_, bf16[4,6144]{1,0:T(4,128)(2,1)S(1)} %collective-permute-done.7.refs_1_, bf16[4,6144]{1,0:T(4,128)(2,1)S(1)} %collective-permute-done.8.refs_2_), custom_call_target="tpu_custom_call" | custom-call | tf_op jit(solution)/shard_map/finish/pallas_call | solution.py:233
  (17 shorter events, 0.0 us)
Async XLA Ops:
  0.6 6.5 %copy-start.2 = (bf16[4,128,768]{2,1,0:T(8,128)(2,1)S(1)}, bf16[4,128,768]{2,1,0:T(8,128)(2,1)}, u32[]{:S(2)}) copy-start(bf16[4,128,768]{2,1,0:T(8,128)(2,1)} %constant.2.clone.table_ref) | copy-start | bytes 2359300
  0.6 0.8 %copy-start.3 = (bf16[4,2,2048]{2,1,0:T(2,128)(2,1)S(1)}, bf16[4,2,2048]{2,1,0:T(2,128)(2,1)}, u32[]{:S(2)}) copy-start(bf16[4,2,2048]{2,1,0:T(2,128)(2,1)} %refs_0_) | copy-start | bytes 98308
  0.7 6.4 %copy-start.4 = (f32[2048]{0:T(1024)S(1)}, f32[2048]{0:T(1024)}, u32[]{:S(2)}) copy-start(f32[2048]{0:T(1024)} %param.13) | copy-start | bytes 24580
  0.7 6.4 %copy-start.5 = (s32[512,2]{0,1:T(2,128)S(1)}, s32[512,2]{0,1:T(2,128)}, u32[]{:S(2)}) copy-start(s32[512,2]{0,1:T(2,128)} %param.12) | copy-start | bytes 12292
  0.7 6.4 %copy-start.1 = (bf16[512,2048]{1,0:T(8,128)(2,1)S(1)}, bf16[512,2048]{1,0:T(8,128)(2,1)}, u32[]{:S(2)}) copy-start(bf16[512,2048]{1,0:T(8,128)(2,1)} %ctf_ref.1) | copy-start | bytes 6291460
  0.7 6.4 %copy-start = (bf16[512,2,2048]{2,1,0:T(2,128)(2,1)S(1)}, bf16[512,2,2048]{2,1,0:T(2,128)(2,1)}, u32[]{:S(2)}) copy-start(bf16[512,2,2048]{2,1,0:T(2,128)(2,1)} %param.9) | copy-start | bytes 12582916
  1.5 9.5 %collective-permute-start.2 = (bf16[4,2,2048]{2,1,0:T(2,128)(2,1)S(1)}, bf16[4,2,2048]{2,1,0:T(2,128)(2,1)S(1)}, u32[]{:S(2)}, u32[]{:S(2)}) collective-permute-start(bf16[4,2,2048]{2,1,0:T(2,128)(2,1)S(1)} %copy-done.3), channel_id=1, source_target_pairs={{12,0},{8,4},{4,8},{0,12},{13,1},{9,5},{5,9},{1,13},{14,2},{10,6},... | collective-permute-start | bytes 98312 | tf_op jit(solution)/shard_map/ppermute | solution.py:264
  6.5 4.8 %collective-permute-start.1 = (bf16[4,2,2048]{2,1,0:T(2,128)(2,1)S(1)}, bf16[4,2,2048]{2,1,0:T(2,128)(2,1)S(1)}, u32[]{:S(2)}, u32[]{:S(2)}) collective-permute-start(bf16[4,2,2048]{2,1,0:T(2,128)(2,1)S(1)} %copy-done.3), channel_id=1, source_target_pairs={{8,0},{12,4},{0,8},{4,12},{9,1},{13,5},{1,9},{5,13},{10,2},{14,6},... | collective-permute-start | bytes 98312 | tf_op jit(solution)/shard_map/ppermute | solution.py:264
  6.5 4.8 %collective-permute-start = (bf16[4,2,2048]{2,1,0:T(2,128)(2,1)S(1)}, bf16[4,2,2048]{2,1,0:T(2,128)(2,1)S(1)}, u32[]{:S(2)}, u32[]{:S(2)}) collective-permute-start(bf16[4,2,2048]{2,1,0:T(2,128)(2,1)S(1)} %copy-done.3), channel_id=1, source_target_pairs={{4,0},{0,4},{12,8},{8,12},{5,1},{1,5},{13,9},{9,13},{6,2},{2,6},{1... | collective-permute-start | bytes 98312 | tf_op jit(solution)/shard_map/ppermute | solution.py:264
  7.1 4.2 %copy-start.6 = (s32[1,2]{1,0:T(1,128)S(1)}, s32[1,2]{1,0:T(1,128)}, u32[]{:S(2)}) copy-start(s32[1,2]{1,0:T(1,128)} %allowed_ref.1) | copy-start | bytes 28
  7.1 4.2 %copy-start.7 = (s32[16]{0:T(128)S(1)}, s32[16]{0:T(128)}, u32[]{:S(2)}) copy-start(s32[16]{0:T(128)} %param.14) | copy-start | bytes 196
  7.1 4.2 %copy-start.8 = (f32[4]{0:T(128)S(1)}, f32[4]{0:T(128)}, u32[]{:S(2)}) copy-start(f32[4]{0:T(128)} %param.15) | copy-start | bytes 52
  13.1 3.7 %collective-permute-start.5 = (f32[16,512]{1,0:T(8,128)S(1)}, f32[16,512]{1,0:T(8,128)S(1)}, u32[]{:S(2)}, u32[]{:S(2)}) collective-permute-start(f32[16,512]{1,0:T(8,128)S(1)} %score.1.refs_0_), channel_id=1, source_target_pairs={{3,0},{2,1},{1,2},{0,3},{7,4},{6,5},{5,6},{4,7},{11,8},{10,9},{9,1... | collective-permute-start | bytes 98312 | tf_op jit(solution)/shard_map/ppermute | solution.py:264
  13.2 4.0 %collective-permute-start.4 = (f32[16,512]{1,0:T(8,128)S(1)}, f32[16,512]{1,0:T(8,128)S(1)}, u32[]{:S(2)}, u32[]{:S(2)}) collective-permute-start(f32[16,512]{1,0:T(8,128)S(1)} %score.1.refs_0_), channel_id=1, source_target_pairs={{2,0},{3,1},{0,2},{1,3},{6,4},{7,5},{4,6},{5,7},{10,8},{11,9},{8,1... | collective-permute-start | bytes 98312 | tf_op jit(solution)/shard_map/ppermute | solution.py:264
  14.7 2.5 %collective-permute-start.3 = (f32[16,512]{1,0:T(8,128)S(1)}, f32[16,512]{1,0:T(8,128)S(1)}, u32[]{:S(2)}, u32[]{:S(2)}) collective-permute-start(f32[16,512]{1,0:T(8,128)S(1)} %score.1.refs_0_), channel_id=1, source_target_pairs={{1,0},{0,1},{3,2},{2,3},{5,4},{4,5},{7,6},{6,7},{9,8},{8,9},{11,10... | collective-permute-start | bytes 98312 | tf_op jit(solution)/shard_map/ppermute | solution.py:264
  18.6 6.1 %collective-permute-start.6 = (bf16[4,6144]{1,0:T(4,128)(2,1)S(1)}, bf16[4,6144]{1,0:T(4,128)(2,1)S(1)}, u32[]{:S(2)}, u32[]{:S(2)}) collective-permute-start(bf16[4,6144]{1,0:T(4,128)(2,1)S(1)} %get-tuple-element.13), channel_id=1, source_target_pairs={{12,0},{0,4},{4,8},{8,12},{13,1},{1,5},{5,9},{9,13},{14,2},{2,6},{... | collective-permute-start | bytes 147464 | tf_op jit(solution)/shard_map/ppermute | solution.py:260
  20.0 6.5 %collective-permute-start.7 = (bf16[4,6144]{1,0:T(4,128)(2,1)S(1)}, bf16[4,6144]{1,0:T(4,128)(2,1)S(1)}, u32[]{:S(2)}, u32[]{:S(2)}) collective-permute-start(bf16[4,6144]{1,0:T(4,128)(2,1)S(1)} %get-tuple-element.14), channel_id=1, source_target_pairs={{8,0},{12,4},{0,8},{4,12},{9,1},{13,5},{1,9},{5,13},{10,2},{14,6},... | collective-permute-start | bytes 147464 | tf_op jit(solution)/shard_map/ppermute | solution.py:260
  22.6 4.3 %collective-permute-start.8 = (bf16[4,6144]{1,0:T(4,128)(2,1)S(1)}, bf16[4,6144]{1,0:T(4,128)(2,1)S(1)}, u32[]{:S(2)}, u32[]{:S(2)}) collective-permute-start(bf16[4,6144]{1,0:T(4,128)(2,1)S(1)} %get-tuple-element.15), channel_id=1, source_target_pairs={{4,0},{8,4},{12,8},{0,12},{5,1},{9,5},{13,9},{1,13},{6,2},{10,6},{... | collective-permute-start | bytes 147464 | tf_op jit(solution)/shard_map/ppermute | solution.py:260

commit v4 on v3

--- a/solution.py
+++ b/solution.py
@@ -17,7 +17,9 @@
 ROW = 2 * KMAX
 REACH = 8
 GROUP = 16
-DIRECT = (2, 4)
+FETCH = {2: (1,), 4: (1, 3, 2)}
+RETURN = {2: (1,), 4: (1, 2, 3)}
+SHARE = (1, 2, 3)
 SPLITS = 3
 
 
@@ -51,7 +53,7 @@
 
 
 def prepare_kernel(
-    rows, image_ref, ctf_ref, shift_ref, inv_ref, table_ref, out_ref, phase_ref, even_ref, odd_ref
+    rows, image_ref, ctf_ref, shift_ref, inv_ref, table_ref, first_ref, out_ref, phase_ref, even_ref, odd_ref
 ):
     images = ctf_ref.shape[0]
     pix = rows * ROW
@@ -109,11 +111,11 @@
     lax.fori_loop(0, images // (2 * GROUP), step, 0)
 
 
-def prepare(images, ctf, shifts, inv_sigma2, pieces):
+def prepare(images, ctf, shifts, inv_sigma2, pieces, first):
     count, _, pix = images.shape
     rows = pix // ROW
     flat = images.reshape(count, 2, rows, ROW).transpose(0, 2, 1, 3).reshape(count * rows * 2, ROW)
-    args = (flat, ctf, shifts.T, inv_sigma2.reshape(1, pix), phase_table(pieces, rows))
+    args = (flat, ctf, shifts.T, inv_sigma2.reshape(1, pix), phase_table(pieces, rows), first)
     return pl.pallas_call(
         functools.partial(prepare_kernel, rows),
         in_specs=[pl.BlockSpec(memory_space=pltpu.VMEM)] * len(args),
@@ -157,7 +159,9 @@
     joint = jnp.concatenate(parts, axis=0).astype(jnp.bfloat16)
     raw = lax.dot_general(joint, data_ref[...], (((1,), (1,)), ((), ())), preferred_element_type=jnp.float32)
     if turned:
-        came = [raw[k * each : (k + 1) * each] for k in range(blocks)]
+        came = [raw[:each]] * blocks
+        for k, mask in enumerate(FETCH[blocks], start=1):
+            came[mask] = raw[k * each : (k + 1) * each]
         leave = came[:1]
         for k in range(1, blocks):
             at = lax.rem(me + k, blocks) ^ me
@@ -174,25 +178,27 @@
     return pl.pallas_call(
         functools.partial(score_kernel, blocks, turned),
         out_shape=jax.ShapeDtypeStruct((orients, data.shape[0]), jnp.float32),
-        compiler_params=pltpu.CompilerParams(vmem_limit_bytes=24 * 2**20),
+        compiler_params=pltpu.CompilerParams(vmem_limit_bytes=8 * 2**20),
         name="score",
     )(data, allowed, class_ids.reshape(1, -1), log_prior.reshape(1, -1), *projs)
 
 
 def back_kernel(parts, data_ref, *refs):
     part_refs, (best_ref, own_ref, *away_refs) = refs[:parts], refs[parts:]
-    share = best_ref.shape[0]
+    share = best_ref.shape[1]
     sums = [ref[...] for ref in part_refs]
-    while len(sums) > 1:
-        sums = [sums[k] + sums[k + 1] for k in range(0, len(sums), 2)]
-    rows = sums[0]
+    if parts == 4:
+        part = dict(zip((0,) + SHARE, sums))
+        rows = (part[0] + part[1]) + (part[2] + part[3])
+    else:
+        rows = sums[0]
     expo = jnp.exp(rows - jnp.max(rows, axis=0, keepdims=True))
     inverse = 1.0 / jnp.sum(expo, axis=0, keepdims=True)
     weights = (expo * inverse).astype(jnp.bfloat16)
     place = lax.axis_index(("shell", "sub"))
-    best = inverse[0, 0:share]
+    best = inverse[:, 0:share]
     for piece in range(1, rows.shape[1] // share):
-        best = jnp.where(place == piece, inverse[0, piece * share : (piece + 1) * share], best)
+        best = jnp.where(place == piece, inverse[:, piece * share : (piece + 1) * share], best)
     best_ref[...] = best
     back = jnp.dot(weights, data_ref[...], preferred_element_type=jnp.float32)
     each = own_ref.shape[0]
@@ -208,17 +214,20 @@
     return pl.pallas_call(
         functools.partial(back_kernel, len(parts)),
         out_shape=[
-            jax.ShapeDtypeStruct((count // pieces,), jnp.float32),
+            pltpu.VMEM((1, count // pieces), jnp.float32),
             jax.ShapeDtypeStruct((each, wide), jnp.float32),
         ]
         + [jax.ShapeDtypeStruct((each, wide), jnp.bfloat16)] * away,
-        compiler_params=pltpu.CompilerParams(vmem_limit_bytes=24 * 2**20),
+        in_specs=[pl.BlockSpec(memory_space=pltpu.VMEM)] * (1 + len(parts)),
+        out_specs=[pl.BlockSpec(memory_space=pltpu.VMEM)] * (2 + away),
+        compiler_params=pltpu.CompilerParams(vmem_limit_bytes=8 * 2**20),
         name="back",
     )(data, *parts)
 
 
-def finish_kernel(own_ref, *refs):
-    *away_refs, data_ref, weight_ref = refs
+def finish_kernel(found_ref, own_ref, *refs):
+    *away_refs, data_ref, weight_ref, best_ref = refs
+    best_ref[...] = found_ref[0, :]
     pix = weight_ref.shape[1]
     total = own_ref[...]
     for ref in away_refs:
@@ -228,17 +237,18 @@
     weight_ref[...] = total[:, 2 * pix :]
 
 
-def finish(own, away):
+def finish(found, own, away):
     each, wide = own.shape
     return pl.pallas_call(
         finish_kernel,
         out_shape=[
             jax.ShapeDtypeStruct((each, 2, wide // 3), jnp.float32),
             jax.ShapeDtypeStruct((each, wide // 3), jnp.float32),
+            jax.ShapeDtypeStruct(found.shape[1:], jnp.float32),
         ],
-        compiler_params=pltpu.CompilerParams(vmem_limit_bytes=16 * 2**20),
+        compiler_params=pltpu.CompilerParams(vmem_limit_bytes=8 * 2**20),
         name="finish",
-    )(own, *away)
+    )(found, own, *away)
 
 
 def opening_kernel(out_ref):
@@ -267,26 +277,25 @@
 def body(images, ctf, projections, shifts, inv_sigma2, class_ids, log_prior, allowed):
     blocks = lax.axis_size("blk")
     pieces = lax.axis_size(("shell", "sub"))
-    direct = blocks in DIRECT
+    direct = blocks in FETCH
 
     first = opening()
     projections, first = lax.optimization_barrier((projections, first))
     if direct:
-        projs = [projections] + [swap(projections, "blk", blocks, k) for k in range(1, blocks)]
+        projs = [projections] + [swap(projections, "blk", blocks, k) for k in FETCH[blocks]]
     else:
         projs = [lax.all_gather(projections, "blk", axis=0, tiled=True)]
-    data = prepare(images, ctf, shifts, inv_sigma2, pieces)
+    data = prepare(images, ctf, shifts, inv_sigma2, pieces, first)
     part = score(data, allowed, class_ids, log_prior, projs, blocks, direct)
     if pieces == 4:
-        parts = [part, swap(part, ("shell", "sub"), 4, 1), swap(part, ("shell", "sub"), 4, 2), swap(part, ("shell", "sub"), 4, 3)]
+        parts = [part] + [swap(part, ("shell", "sub"), 4, mask) for mask in SHARE]
     else:
         parts = [lax.psum(part, ("shell", "sub"))]
     best, own, *away = back(data, parts, blocks - 1 if direct else 0, pieces)
     if not direct:
         own = lax.psum_scatter(own, "blk", scatter_dimension=0, tiled=True)
-    arrived = [rotate(block, "blk", blocks, blocks - k) for k, block in enumerate(away, start=1)]
-    back_data, back_weight = finish(own, arrived)
-    return (back_data, back_weight, best)
+    arrived = [rotate(away[k - 1], "blk", blocks, blocks - k) for k in (RETURN[blocks] if direct else ())]
+    return finish(best, own, arrived)
 
 
 def solution(mesh):

time: 27.8 us -> 27.1 us (0.975)
  Pallas kernels: 8.17 us -> 7.2 us
  local copies, waits for them, and re-layouts: 0.23 us -> 0.82 us
  waiting for transfers between devices: 5.61 us -> 5.09 us
    pallas_call x1, Pallas kernels: 0.59 us -> 0.01 us  [opening(): pl.pallas_call(opening_kernel, out_specs=pl.BlockSpec(memory_space=pltpu....]
    unnamed x18, local copies, waits for them, and re-layouts: 0.23 us -> 0.82 us
    ppermute x3, waiting for transfers between devices: 3.09 us -> 2.63 us  [rotate(): lax.ppermute(value, axis, [((j + by) % size, j) for j in range(size)])]
    pallas_call x1, Pallas kernels: 1.34 us -> 0.94 us  [back(): pl.pallas_call(functools.partial(back_kernel, len(parts)), out_shape=[plt...]
  transfers between devices with their start and end apart: 9 -> 9, of which waited for: 6 -> 5; matrix products, arithmetic and copies ran while one was open for 0% -> 0% of each run, Pallas kernels for 14% -> 14%
where the time goes in v4:
time: 27.1 us; the launch traced here: 26.9 us
  starting transfers between devices  13 us (48%)
  Pallas kernels  7.2 us (27%)
  waiting for transfers between devices  5.09 us (19%)
  local copies, waits for them, and re-layouts  0.82 us (3%)
  between operations  0.77 us (3%)
    ppermute x6, starting transfers between devices, swap(): return lax.ppermute(value, axes, [(j ^ mask, j) for j in range(size)])  7.54 us
    ppermute x3, starting transfers between devices, rotate(): lax.ppermute(value, axis, [((j + by) % size, j) for j in range(size)])  5.5 us
    pallas_call x1, Pallas kernels, prepare(): pl.pallas_call(functools.partial(prepare_kernel, rows), in_specs=[pl.Bloc...  3.84 us
    ppermute x3, waiting for transfers between devices, rotate(): lax.ppermute(value, axis, [((j + by) % size, j) for j in range(size)])  2.63 us
    ppermute x6, waiting for transfers between devices, swap(): return lax.ppermute(value, axes, [(j ^ mask, j) for j in range(size)])  2.46 us
    pallas_call x1, Pallas kernels, score(): pl.pallas_call(functools.partial(score_kernel, blocks, turned), out_shape...  1.74 us
    pallas_call x1, Pallas kernels, back(): pl.pallas_call(functools.partial(back_kernel, len(parts)), out_shape=[plt...  0.94 us
    unnamed x18, local copies, waits for them, and re-layouts  0.82 us
  transfers between devices with their start and end apart: 9, of which 5 were waited for; matrix products, arithmetic and copies ran while one was open for 0% of the time, Pallas kernels for 14%

profile of v4, /device:TPU:0, one launch (start us, length us, event | category | flops | bytes accessed | tf_op | source)
XLA Modules:
  0.0 26.9 jit_solution(3334948901527975266)
XLA Ops:
  0.6 0.0 copy-start.2
  0.7 0.8 %copy-done.3 = bf16[4,2,2048]{2,1,0:T(2,128)(2,1)S(1)} copy-done((bf16[4,2,2048]{2,1,0:T(2,128)(2,1)S(1)}, bf16[4,2,2048]{2,1,0:T(2,128)(2,1)}, u32[]{:S(2)}) %copy-start.3) | copy-done | bytes 32792
  1.5 4.0 %collective-permute-start.2 = (bf16[4,2,2048]{2,1,0:T(2,128)(2,1)S(1)}, bf16[4,2,2048]{2,1,0:T(2,128)(2,1)S(1)}, u32[]{:S(2)}, u32[]{:S(2)}) collective-permute-start(bf16[4,2,2048]{2,1,0:T(2,128)(2,1)S(1)} %copy-done.3), channel_id=1, source_target_pairs={{8,0},{12,4},{0,8},{4,12},{9,1},{13,5},{1,9},{5,13},{10,2},{14,6},... | collective-permute-start | bytes 98312 | tf_op jit(solution)/shard_map/ppermute | solution.py:274
  5.5 1.3 %collective-permute-start.1 = (bf16[4,2,2048]{2,1,0:T(2,128)(2,1)S(1)}, bf16[4,2,2048]{2,1,0:T(2,128)(2,1)S(1)}, u32[]{:S(2)}, u32[]{:S(2)}) collective-permute-start(bf16[4,2,2048]{2,1,0:T(2,128)(2,1)S(1)} %copy-done.3), channel_id=1, source_target_pairs={{12,0},{8,4},{4,8},{0,12},{13,1},{9,5},{5,9},{1,13},{14,2},{10,6},... | collective-permute-start | bytes 98312 | tf_op jit(solution)/shard_map/ppermute | solution.py:274
  6.9 0.2 collective-permute-start
  7.1 0.0 copy-start.6
  7.1 0.0 copy-start.7
  7.1 0.0 copy-start.8
  7.2 3.8 %prepare.1.data_ref = bf16[512,6144]{1,0:T(8,128)(2,1)S(1)} custom-call(bf16[16384,128]{1,0:T(8,128)(2,1)S(1)} %bitcast.9, bf16[512,2048]{1,0:T(8,128)(2,1)S(1)} %copy-done.1, s32[2,512]{1,0:T(2,128)S(1)} %bitcast.11, f32[1,2048]{1,0:T(1,128)S(1)} %bitcast.10, bf16[4,128,768]{2,1,0:T(8,128)(2,1)S(1)} %copy-done.2, f32[8,128]{1,0:T(8,128)S(1)} %opening.1.first_ref), custom_call_target="tpu_custom_call" | custom-call | tf_op jit(solution)/shard_map/prepare/pallas_call | solution.py:119
  11.0 0.2 collective-permute-done.1.refs_2_
  11.2 0.0 collective-permute-done.refs_1_
  11.2 1.7 %score.1.refs_0_ = f32[16,512]{1,0:T(8,128)S(1)} custom-call(bf16[512,6144]{1,0:T(8,128)(2,1)S(1)} %prepare.1.data_ref, s32[1,2]{1,0:T(1,128)S(1)} %copy-done.6, s32[1,16]{1,0:T(1,128)S(1)} %bitcast.12, f32[1,4]{1,0:T(1,128)S(1)} %bitcast.13, bf16[4,2,2048]{2,1,0:T(2,128)(2,1)S(1)} %copy-done.3, bf16[4,2,2048]{2,1,0:T(2,128)(2,1)S(1)} %collective-permute-done.refs_1_, ...), custom_call_target="tpu_custom_call" | custom-call | tf_op jit(solution)/shard_map/score/pallas_call | solution.py:178
  13.0 0.3 collective-permute-start.5
  13.3 1.4 %collective-permute-start.4 = (f32[16,512]{1,0:T(8,128)S(1)}, f32[16,512]{1,0:T(8,128)S(1)}, u32[]{:S(2)}, u32[]{:S(2)}) collective-permute-start(f32[16,512]{1,0:T(8,128)S(1)} %score.1.refs_0_), channel_id=1, source_target_pairs={{2,0},{3,1},{0,2},{1,3},{6,4},{7,5},{4,6},{5,7},{10,8},{11,9},{8,1... | collective-permute-start | bytes 98312 | tf_op jit(solution)/shard_map/ppermute | solution.py:274
  14.6 0.3 %collective-permute-start.3 = (f32[16,512]{1,0:T(8,128)S(1)}, f32[16,512]{1,0:T(8,128)S(1)}, u32[]{:S(2)}, u32[]{:S(2)}) collective-permute-start(f32[16,512]{1,0:T(8,128)S(1)} %score.1.refs_0_), channel_id=1, source_target_pairs={{1,0},{0,1},{3,2},{2,3},{5,4},{4,5},{7,6},{6,7},{9,8},{8,9},{11,10... | collective-permute-start | bytes 98312 | tf_op jit(solution)/shard_map/ppermute | solution.py:274
  14.9 1.8 %collective-permute-done.5.refs_3_ = f32[16,512]{1,0:T(8,128)S(1)} collective-permute-done((f32[16,512]{1,0:T(8,128)S(1)}, f32[16,512]{1,0:T(8,128)S(1)}, u32[]{:S(2)}, u32[]{:S(2)}) %collective-permute-start.5) | collective-permute-done | bytes 32800 | tf_op jit(solution)/shard_map/ppermute | solution.py:274
  16.7 0.5 %collective-permute-done.4.refs_2_ = f32[16,512]{1,0:T(8,128)S(1)} collective-permute-done((f32[16,512]{1,0:T(8,128)S(1)}, f32[16,512]{1,0:T(8,128)S(1)}, u32[]{:S(2)}, u32[]{:S(2)}) %collective-permute-start.4) | collective-permute-done | bytes 32800 | tf_op jit(solution)/shard_map/ppermute | solution.py:274
  17.2 0.9 %back.1 = (f32[1,128]{1,0:T(1,128)S(1)}, f32[4,6144]{1,0:T(4,128)S(1)}, bf16[4,6144]{1,0:T(4,128)(2,1)S(1)}, bf16[4,6144]{1,0:T(4,128)(2,1)S(1)}, bf16[4,6144]{1,0:T(4,128)(2,1)S(1)}) custom-call(bf16[512,6144]{1,0:T(8,128)(2,1)S(1)} %prepare.1.data_ref, f32[16,512]{1,0:T(8,128)S(1)} %score.1.refs_0_, f32[16,512]{1,0:T(8,128)S(1)} %collective-permute-done.3.refs_1_, ...), custom_call_target="tpu_custom_call" | custom-call | tf_op jit(solution)/shard_map/back/pallas_call | solution.py:214
  18.1 1.6 %collective-permute-start.6 = (bf16[4,6144]{1,0:T(4,128)(2,1)S(1)}, bf16[4,6144]{1,0:T(4,128)(2,1)S(1)}, u32[]{:S(2)}, u32[]{:S(2)}) collective-permute-start(bf16[4,6144]{1,0:T(4,128)(2,1)S(1)} %get-tuple-element.14), channel_id=1, source_target_pairs={{12,0},{0,4},{4,8},{8,12},{13,1},{1,5},{5,9},{9,13},{14,2},{2,6},{... | collective-permute-start | bytes 147464 | tf_op jit(solution)/shard_map/ppermute | solution.py:270
  19.7 1.7 %collective-permute-start.7 = (bf16[4,6144]{1,0:T(4,128)(2,1)S(1)}, bf16[4,6144]{1,0:T(4,128)(2,1)S(1)}, u32[]{:S(2)}, u32[]{:S(2)}) collective-permute-start(bf16[4,6144]{1,0:T(4,128)(2,1)S(1)} %get-tuple-element.15), channel_id=1, source_target_pairs={{8,0},{12,4},{0,8},{4,12},{9,1},{13,5},{1,9},{5,13},{10,2},{14,6},... | collective-permute-start | bytes 147464 | tf_op jit(solution)/shard_map/ppermute | solution.py:270
  21.4 2.2 %collective-permute-start.8 = (bf16[4,6144]{1,0:T(4,128)(2,1)S(1)}, bf16[4,6144]{1,0:T(4,128)(2,1)S(1)}, u32[]{:S(2)}, u32[]{:S(2)}) collective-permute-start(bf16[4,6144]{1,0:T(4,128)(2,1)S(1)} %get-tuple-element.16), channel_id=1, source_target_pairs={{4,0},{8,4},{12,8},{0,12},{5,1},{9,5},{13,9},{1,13},{6,2},{10,6},{... | collective-permute-start | bytes 147464 | tf_op jit(solution)/shard_map/ppermute | solution.py:270
  23.6 0.4 %collective-permute-done.6.refs_0_ = bf16[4,6144]{1,0:T(4,128)(2,1)S(1)} collective-permute-done((bf16[4,6144]{1,0:T(4,128)(2,1)S(1)}, bf16[4,6144]{1,0:T(4,128)(2,1)S(1)}, u32[]{:S(2)}, u32[]{:S(2)}) %collective-permute-start.6) | collective-permute-done | bytes 49184 | tf_op jit(solution)/shard_map/ppermute | solution.py:270
  24.0 2.2 %collective-permute-done.7.refs_1_ = bf16[4,6144]{1,0:T(4,128)(2,1)S(1)} collective-permute-done((bf16[4,6144]{1,0:T(4,128)(2,1)S(1)}, bf16[4,6144]{1,0:T(4,128)(2,1)S(1)}, u32[]{:S(2)}, u32[]{:S(2)}) %collective-permute-start.7) | collective-permute-done | bytes 49184 | tf_op jit(solution)/shard_map/ppermute | solution.py:270
  26.2 0.7 %finish.1 = (f32[4,2,2048]{2,1,0:T(2,128)}, f32[4,2048]{1,0:T(4,128)}, f32[128]{0:T(128)}) custom-call(f32[1,128]{1,0:T(1,128)S(1)} %get-tuple-element.12.found_ref, f32[4,6144]{1,0:T(4,128)S(1)} %get-tuple-element.13.own_ref, bf16[4,6144]{1,0:T(4,128)(2,1)S(1)} %collective-permute-done.6.refs_0_, bf16[4,6144]{1,0:T(4,128)(2,1)S(1)} %collective-permute-done.7.refs_1_, ...), custom_call_target="tpu_custom_call" | custom-call | tf_op jit(solution)/shard_map/finish/pallas_call | solution.py:242
  (17 shorter events, 0.0 us)
Async XLA Ops:
  0.6 6.5 %copy-start.2 = (bf16[4,128,768]{2,1,0:T(8,128)(2,1)S(1)}, bf16[4,128,768]{2,1,0:T(8,128)(2,1)}, u32[]{:S(2)}) copy-start(bf16[4,128,768]{2,1,0:T(8,128)(2,1)} %constant.2.clone.table_ref) | copy-start | bytes 2359300
  0.6 0.8 %copy-start.3 = (bf16[4,2,2048]{2,1,0:T(2,128)(2,1)S(1)}, bf16[4,2,2048]{2,1,0:T(2,128)(2,1)}, u32[]{:S(2)}) copy-start(bf16[4,2,2048]{2,1,0:T(2,128)(2,1)} %refs_0_) | copy-start | bytes 98308
  0.7 6.4 %copy-start.4 = (f32[2048]{0:T(1024)S(1)}, f32[2048]{0:T(1024)}, u32[]{:S(2)}) copy-start(f32[2048]{0:T(1024)} %param.13) | copy-start | bytes 24580
  0.7 6.4 %copy-start.5 = (s32[512,2]{0,1:T(2,128)S(1)}, s32[512,2]{0,1:T(2,128)}, u32[]{:S(2)}) copy-start(s32[512,2]{0,1:T(2,128)} %param.12) | copy-start | bytes 12292
  0.7 6.4 %copy-start.1 = (bf16[512,2048]{1,0:T(8,128)(2,1)S(1)}, bf16[512,2048]{1,0:T(8,128)(2,1)}, u32[]{:S(2)}) copy-start(bf16[512,2048]{1,0:T(8,128)(2,1)} %ctf_ref.1) | copy-start | bytes 6291460
  0.7 6.4 %copy-start = (bf16[512,2,2048]{2,1,0:T(2,128)(2,1)S(1)}, bf16[512,2,2048]{2,1,0:T(2,128)(2,1)}, u32[]{:S(2)}) copy-start(bf16[512,2,2048]{2,1,0:T(2,128)(2,1)} %param.9) | copy-start | bytes 12582916
  1.5 9.5 %collective-permute-start.2 = (bf16[4,2,2048]{2,1,0:T(2,128)(2,1)S(1)}, bf16[4,2,2048]{2,1,0:T(2,128)(2,1)S(1)}, u32[]{:S(2)}, u32[]{:S(2)}) collective-permute-start(bf16[4,2,2048]{2,1,0:T(2,128)(2,1)S(1)} %copy-done.3), channel_id=1, source_target_pairs={{8,0},{12,4},{0,8},{4,12},{9,1},{13,5},{1,9},{5,13},{10,2},{14,6},... | collective-permute-start | bytes 98312 | tf_op jit(solution)/shard_map/ppermute | solution.py:274
  5.5 5.7 %collective-permute-start.1 = (bf16[4,2,2048]{2,1,0:T(2,128)(2,1)S(1)}, bf16[4,2,2048]{2,1,0:T(2,128)(2,1)S(1)}, u32[]{:S(2)}, u32[]{:S(2)}) collective-permute-start(bf16[4,2,2048]{2,1,0:T(2,128)(2,1)S(1)} %copy-done.3), channel_id=1, source_target_pairs={{12,0},{8,4},{4,8},{0,12},{13,1},{9,5},{5,9},{1,13},{14,2},{10,6},... | collective-permute-start | bytes 98312 | tf_op jit(solution)/shard_map/ppermute | solution.py:274
  6.9 4.4 %collective-permute-start = (bf16[4,2,2048]{2,1,0:T(2,128)(2,1)S(1)}, bf16[4,2,2048]{2,1,0:T(2,128)(2,1)S(1)}, u32[]{:S(2)}, u32[]{:S(2)}) collective-permute-start(bf16[4,2,2048]{2,1,0:T(2,128)(2,1)S(1)} %copy-done.3), channel_id=1, source_target_pairs={{4,0},{0,4},{12,8},{8,12},{5,1},{1,5},{13,9},{9,13},{6,2},{2,6},{1... | collective-permute-start | bytes 98312 | tf_op jit(solution)/shard_map/ppermute | solution.py:274
  7.1 4.1 %copy-start.6 = (s32[1,2]{1,0:T(1,128)S(1)}, s32[1,2]{1,0:T(1,128)}, u32[]{:S(2)}) copy-start(s32[1,2]{1,0:T(1,128)} %allowed_ref.1) | copy-start | bytes 28
  7.1 4.1 %copy-start.7 = (s32[16]{0:T(128)S(1)}, s32[16]{0:T(128)}, u32[]{:S(2)}) copy-start(s32[16]{0:T(128)} %param.14) | copy-start | bytes 196
  7.1 4.1 %copy-start.8 = (f32[4]{0:T(128)S(1)}, f32[4]{0:T(128)}, u32[]{:S(2)}) copy-start(f32[4]{0:T(128)} %param.15) | copy-start | bytes 52
  13.0 3.7 %collective-permute-start.5 = (f32[16,512]{1,0:T(8,128)S(1)}, f32[16,512]{1,0:T(8,128)S(1)}, u32[]{:S(2)}, u32[]{:S(2)}) collective-permute-start(f32[16,512]{1,0:T(8,128)S(1)} %score.1.refs_0_), channel_id=1, source_target_pairs={{3,0},{2,1},{1,2},{0,3},{7,4},{6,5},{5,6},{4,7},{11,8},{10,9},{9,1... | collective-permute-start | bytes 98312 | tf_op jit(solution)/shard_map/ppermute | solution.py:274
  13.3 3.9 %collective-permute-start.4 = (f32[16,512]{1,0:T(8,128)S(1)}, f32[16,512]{1,0:T(8,128)S(1)}, u32[]{:S(2)}, u32[]{:S(2)}) collective-permute-start(f32[16,512]{1,0:T(8,128)S(1)} %score.1.refs_0_), channel_id=1, source_target_pairs={{2,0},{3,1},{0,2},{1,3},{6,4},{7,5},{4,6},{5,7},{10,8},{11,9},{8,1... | collective-permute-start | bytes 98312 | tf_op jit(solution)/shard_map/ppermute | solution.py:274
  14.6 2.5 %collective-permute-start.3 = (f32[16,512]{1,0:T(8,128)S(1)}, f32[16,512]{1,0:T(8,128)S(1)}, u32[]{:S(2)}, u32[]{:S(2)}) collective-permute-start(f32[16,512]{1,0:T(8,128)S(1)} %score.1.refs_0_), channel_id=1, source_target_pairs={{1,0},{0,1},{3,2},{2,3},{5,4},{4,5},{7,6},{6,7},{9,8},{8,9},{11,10... | collective-permute-start | bytes 98312 | tf_op jit(solution)/shard_map/ppermute | solution.py:274
  18.1 5.9 %collective-permute-start.6 = (bf16[4,6144]{1,0:T(4,128)(2,1)S(1)}, bf16[4,6144]{1,0:T(4,128)(2,1)S(1)}, u32[]{:S(2)}, u32[]{:S(2)}) collective-permute-start(bf16[4,6144]{1,0:T(4,128)(2,1)S(1)} %get-tuple-element.14), channel_id=1, source_target_pairs={{12,0},{0,4},{4,8},{8,12},{13,1},{1,5},{5,9},{9,13},{14,2},{2,6},{... | collective-permute-start | bytes 147464 | tf_op jit(solution)/shard_map/ppermute | solution.py:270
  19.7 6.6 %collective-permute-start.7 = (bf16[4,6144]{1,0:T(4,128)(2,1)S(1)}, bf16[4,6144]{1,0:T(4,128)(2,1)S(1)}, u32[]{:S(2)}, u32[]{:S(2)}) collective-permute-start(bf16[4,6144]{1,0:T(4,128)(2,1)S(1)} %get-tuple-element.15), channel_id=1, source_target_pairs={{8,0},{12,4},{0,8},{4,12},{9,1},{13,5},{1,9},{5,13},{10,2},{14,6},... | collective-permute-start | bytes 147464 | tf_op jit(solution)/shard_map/ppermute | solution.py:270
  21.4 4.9 %collective-permute-start.8 = (bf16[4,6144]{1,0:T(4,128)(2,1)S(1)}, bf16[4,6144]{1,0:T(4,128)(2,1)S(1)}, u32[]{:S(2)}, u32[]{:S(2)}) collective-permute-start(bf16[4,6144]{1,0:T(4,128)(2,1)S(1)} %get-tuple-element.16), channel_id=1, source_target_pairs={{4,0},{8,4},{12,8},{0,12},{5,1},{9,5},{13,9},{1,13},{6,2},{10,6},{... | collective-permute-start | bytes 147464 | tf_op jit(solution)/shard_map/ppermute | solution.py:270

commit v5 on v4

--- a/solution.py
+++ b/solution.py
@@ -56,7 +56,6 @@
     rows, image_ref, ctf_ref, shift_ref, inv_ref, table_ref, first_ref, out_ref, phase_ref, even_ref, odd_ref
 ):
     images = ctf_ref.shape[0]
-    pix = rows * ROW
     lines = 2 * rows
 
     line = lax.broadcasted_iota(jnp.int32, (128, images), 0)
@@ -93,11 +92,9 @@
             imag = ref[pl.ds(line + 1, GROUP, stride=8), :]
             ctf = ctf_ref[pl.ds(start, GROUP), lanes].astype(jnp.float32)
             factor = ctf * inv_ref[0:1, lanes]
-            out_ref[pl.ds(start, GROUP), lanes] = (factor * (real * cos_0 + imag * sin_0)).astype(jnp.bfloat16)
-            out_ref[pl.ds(start, GROUP), pl.ds(pix + t * ROW, ROW)] = (
-                factor * (imag * cos_0 - real * sin_0)
-            ).astype(jnp.bfloat16)
-            out_ref[pl.ds(start, GROUP), pl.ds(2 * pix + t * ROW, ROW)] = (factor * ctf).astype(jnp.bfloat16)
+            out_ref[g, t] = (factor * (real * cos_0 + imag * sin_0)).astype(jnp.bfloat16)
+            out_ref[g, rows + t] = (factor * (imag * cos_0 - real * sin_0)).astype(jnp.bfloat16)
+            out_ref[g, 2 * rows + t] = (factor * ctf).astype(jnp.bfloat16)
             cos_0, cos_1 = cos_1, twice * cos_1 - cos_0
             sin_0, sin_1 = sin_1, twice * sin_1 - sin_0
 
@@ -120,7 +117,7 @@
         functools.partial(prepare_kernel, rows),
         in_specs=[pl.BlockSpec(memory_space=pltpu.VMEM)] * len(args),
         out_specs=pl.BlockSpec(memory_space=pltpu.VMEM),
-        out_shape=pltpu.VMEM((count, 3 * pix), jnp.bfloat16),
+        out_shape=pltpu.VMEM((count // GROUP, 3 * rows, GROUP, ROW), jnp.bfloat16),
         scratch_shapes=[
             pltpu.VMEM((count, 6 * ROW), jnp.float32),
             pltpu.VMEM((2 * rows * GROUP, ROW), jnp.float32),
@@ -129,6 +126,11 @@
         compiler_params=pltpu.CompilerParams(vmem_limit_bytes=8 * 2**20),
         name="prepare",
     )(*[pltpu.with_memory_space_constraint(jnp.asarray(arg), pltpu.VMEM) for arg in args])
+
+
+def whole(data_ref):
+    groups, columns, _, _ = data_ref.shape
+    return jnp.concatenate([data_ref[:, k].reshape(groups * GROUP, ROW) for k in range(columns)], axis=1)
 
 
 def score_kernel(blocks, turned, data_ref, allowed_ref, class_ref, prior_ref, *refs):
@@ -157,7 +159,7 @@
         real, imag = wide[:, 0, :], wide[:, 1, :]
         parts.append(jnp.concatenate([2.0 * real, 2.0 * imag, -(real * real + imag * imag)], axis=1))
     joint = jnp.concatenate(parts, axis=0).astype(jnp.bfloat16)
-    raw = lax.dot_general(joint, data_ref[...], (((1,), (1,)), ((), ())), preferred_element_type=jnp.float32)
+    raw = lax.dot_general(joint, whole(data_ref), (((1,), (1,)), ((), ())), preferred_element_type=jnp.float32)
     if turned:
         came = [raw[:each]] * blocks
         for k, mask in enumerate(FETCH[blocks], start=1):
@@ -177,7 +179,7 @@
     orients = class_ids.shape[0]
     return pl.pallas_call(
         functools.partial(score_kernel, blocks, turned),
-        out_shape=jax.ShapeDtypeStruct((orients, data.shape[0]), jnp.float32),
+        out_shape=jax.ShapeDtypeStruct((orients, data.shape[0] * GROUP), jnp.float32),
         compiler_params=pltpu.CompilerParams(vmem_limit_bytes=8 * 2**20),
         name="score",
     )(data, allowed, class_ids.reshape(1, -1), log_prior.reshape(1, -1), *projs)
@@ -200,7 +202,7 @@
     for piece in range(1, rows.shape[1] // share):
         best = jnp.where(place == piece, inverse[:, piece * share : (piece + 1) * share], best)
     best_ref[...] = best
-    back = jnp.dot(weights, data_ref[...], preferred_element_type=jnp.float32)
+    back = jnp.dot(weights, whole(data_ref), preferred_element_type=jnp.float32)
     each = own_ref.shape[0]
     own_ref[...] = back[0:each]
     for k, ref in enumerate(away_refs):
@@ -210,7 +212,7 @@
 def back(data, parts, away, pieces):
     orients, count = parts[0].shape
     each = orients // (away + 1)
-    wide = data.shape[1]
+    wide = data.shape[1] * ROW
     return pl.pallas_call(
         functools.partial(back_kernel, len(parts)),
         out_shape=[

time: 27.1 us -> 26.9 us (level)
  no operation moved by 1% of the time
where the time goes in v5:
time: 26.9 us; the launch traced here: 26.7 us
  starting transfers between devices  12.9 us (48%)
  Pallas kernels  6.99 us (26%)
  waiting for transfers between devices  5.26 us (20%)
  local copies, waits for them, and re-layouts  0.82 us (3%)
  between operations  0.77 us (3%)
    ppermute x6, starting transfers between devices, swap(): return lax.ppermute(value, axes, [(j ^ mask, j) for j in range(size)])  7.53 us
    ppermute x3, starting transfers between devices, rotate(): lax.ppermute(value, axis, [((j + by) % size, j) for j in range(size)])  5.35 us
    pallas_call x1, Pallas kernels, prepare(): pl.pallas_call(functools.partial(prepare_kernel, rows), in_specs=[pl.Bloc...  3.63 us
    ppermute x3, waiting for transfers between devices, rotate(): lax.ppermute(value, axis, [((j + by) % size, j) for j in range(size)])  2.65 us
    ppermute x6, waiting for transfers between devices, swap(): return lax.ppermute(value, axes, [(j ^ mask, j) for j in range(size)])  2.61 us
    pallas_call x1, Pallas kernels, score(): pl.pallas_call(functools.partial(score_kernel, blocks, turned), out_shape...  1.74 us
    pallas_call x1, Pallas kernels, back(): pl.pallas_call(functools.partial(back_kernel, len(parts)), out_shape=[plt...  0.95 us
    unnamed x18, local copies, waits for them, and re-layouts  0.82 us
  transfers between devices with their start and end apart: 9, of which 5 were waited for; matrix products, arithmetic and copies ran while one was open for 0% of the time, Pallas kernels for 14%

profile of v5, /device:TPU:0, one launch (start us, length us, event | category | flops | bytes accessed | tf_op | source)
XLA Modules:
  0.0 26.7 jit_solution(3371377946560626646)
XLA Ops:
  0.6 0.0 copy-start.2
  0.7 0.8 %copy-done.3 = bf16[4,2,2048]{2,1,0:T(2,128)(2,1)S(1)} copy-done((bf16[4,2,2048]{2,1,0:T(2,128)(2,1)S(1)}, bf16[4,2,2048]{2,1,0:T(2,128)(2,1)}, u32[]{:S(2)}) %copy-start.3) | copy-done | bytes 32792
  1.5 4.0 %collective-permute-start.2 = (bf16[4,2,2048]{2,1,0:T(2,128)(2,1)S(1)}, bf16[4,2,2048]{2,1,0:T(2,128)(2,1)S(1)}, u32[]{:S(2)}, u32[]{:S(2)}) collective-permute-start(bf16[4,2,2048]{2,1,0:T(2,128)(2,1)S(1)} %copy-done.3), channel_id=1, source_target_pairs={{8,0},{12,4},{0,8},{4,12},{9,1},{13,5},{1,9},{5,13},{10,2},{14,6},... | collective-permute-start | bytes 98312 | tf_op jit(solution)/shard_map/ppermute | solution.py:276
  5.5 1.3 %collective-permute-start.1 = (bf16[4,2,2048]{2,1,0:T(2,128)(2,1)S(1)}, bf16[4,2,2048]{2,1,0:T(2,128)(2,1)S(1)}, u32[]{:S(2)}, u32[]{:S(2)}) collective-permute-start(bf16[4,2,2048]{2,1,0:T(2,128)(2,1)S(1)} %copy-done.3), channel_id=1, source_target_pairs={{12,0},{8,4},{4,8},{0,12},{13,1},{9,5},{5,9},{1,13},{14,2},{10,6},... | collective-permute-start | bytes 98312 | tf_op jit(solution)/shard_map/ppermute | solution.py:276
  6.9 0.2 collective-permute-start
  7.1 0.0 copy-start.6
  7.1 0.0 copy-start.7
  7.1 0.0 copy-start.8
  7.2 3.6 %prepare.1.data_ref = bf16[32,48,16,128]{3,2,1,0:T(8,128)(2,1)S(1)} custom-call(bf16[16384,128]{1,0:T(8,128)(2,1)S(1)} %bitcast.9, bf16[512,2048]{1,0:T(8,128)(2,1)S(1)} %copy-done.1, s32[2,512]{1,0:T(2,128)S(1)} %bitcast.11, f32[1,2048]{1,0:T(1,128)S(1)} %bitcast.10, bf16[4,128,768]{2,1,0:T(8,128)(2,1)S(1)} %copy-done.2, f32[8,128]{1,0:T(8,128)S(1)} %opening.1.first_ref), custom_call_target="tpu_custom_call" | custom-call | tf_op jit(solution)/shard_map/prepare/pallas_call | solution.py:116
  10.8 0.0 collective-permute-done.2.refs_3_
  10.8 0.4 %collective-permute-done.1.refs_2_ = bf16[4,2,2048]{2,1,0:T(2,128)(2,1)S(1)} collective-permute-done((bf16[4,2,2048]{2,1,0:T(2,128)(2,1)S(1)}, bf16[4,2,2048]{2,1,0:T(2,128)(2,1)S(1)}, u32[]{:S(2)}, u32[]{:S(2)}) %collective-permute-start.1) | collective-permute-done | bytes 32800 | tf_op jit(solution)/shard_map/ppermute | solution.py:276
  11.2 1.7 %score.1.refs_0_ = f32[16,512]{1,0:T(8,128)S(1)} custom-call(bf16[32,48,16,128]{3,2,1,0:T(8,128)(2,1)S(1)} %prepare.1.data_ref, s32[1,2]{1,0:T(1,128)S(1)} %copy-done.6, s32[1,16]{1,0:T(1,128)S(1)} %bitcast.12, f32[1,4]{1,0:T(1,128)S(1)} %bitcast.13, bf16[4,2,2048]{2,1,0:T(2,128)(2,1)S(1)} %copy-done.3, ...), custom_call_target="tpu_custom_call" | custom-call | tf_op jit(solution)/shard_map/score/pallas_call | solution.py:180
  13.0 0.1 collective-permute-start.5
  13.1 1.6 %collective-permute-start.4 = (f32[16,512]{1,0:T(8,128)S(1)}, f32[16,512]{1,0:T(8,128)S(1)}, u32[]{:S(2)}, u32[]{:S(2)}) collective-permute-start(f32[16,512]{1,0:T(8,128)S(1)} %score.1.refs_0_), channel_id=1, source_target_pairs={{2,0},{3,1},{0,2},{1,3},{6,4},{7,5},{4,6},{5,7},{10,8},{11,9},{8,1... | collective-permute-start | bytes 98312 | tf_op jit(solution)/shard_map/ppermute | solution.py:276
  14.6 0.3 %collective-permute-start.3 = (f32[16,512]{1,0:T(8,128)S(1)}, f32[16,512]{1,0:T(8,128)S(1)}, u32[]{:S(2)}, u32[]{:S(2)}) collective-permute-start(f32[16,512]{1,0:T(8,128)S(1)} %score.1.refs_0_), channel_id=1, source_target_pairs={{1,0},{0,1},{3,2},{2,3},{5,4},{4,5},{7,6},{6,7},{9,8},{8,9},{11,10... | collective-permute-start | bytes 98312 | tf_op jit(solution)/shard_map/ppermute | solution.py:276
  14.9 1.8 %collective-permute-done.5.refs_3_ = f32[16,512]{1,0:T(8,128)S(1)} collective-permute-done((f32[16,512]{1,0:T(8,128)S(1)}, f32[16,512]{1,0:T(8,128)S(1)}, u32[]{:S(2)}, u32[]{:S(2)}) %collective-permute-start.5) | collective-permute-done | bytes 32800 | tf_op jit(solution)/shard_map/ppermute | solution.py:276
  16.7 0.4 %collective-permute-done.4.refs_2_ = f32[16,512]{1,0:T(8,128)S(1)} collective-permute-done((f32[16,512]{1,0:T(8,128)S(1)}, f32[16,512]{1,0:T(8,128)S(1)}, u32[]{:S(2)}, u32[]{:S(2)}) %collective-permute-start.4) | collective-permute-done | bytes 32800 | tf_op jit(solution)/shard_map/ppermute | solution.py:276
  17.1 0.9 %back.1 = (f32[1,128]{1,0:T(1,128)S(1)}, f32[4,6144]{1,0:T(4,128)S(1)}, bf16[4,6144]{1,0:T(4,128)(2,1)S(1)}, bf16[4,6144]{1,0:T(4,128)(2,1)S(1)}, bf16[4,6144]{1,0:T(4,128)(2,1)S(1)}) custom-call(bf16[32,48,16,128]{3,2,1,0:T(8,128)(2,1)S(1)} %prepare.1.data_ref, f32[16,512]{1,0:T(8,128)S(1)} %score.1.refs_0_, f32[16,512]{1,0:T(8,128)S(1)} %collective-permute-done.3.refs_1_, ...), custom_call_target="tpu_custom_call" | custom-call | tf_op jit(solution)/shard_map/back/pallas_call | solution.py:216
  18.1 1.4 %collective-permute-start.6 = (bf16[4,6144]{1,0:T(4,128)(2,1)S(1)}, bf16[4,6144]{1,0:T(4,128)(2,1)S(1)}, u32[]{:S(2)}, u32[]{:S(2)}) collective-permute-start(bf16[4,6144]{1,0:T(4,128)(2,1)S(1)} %get-tuple-element.14), channel_id=1, source_target_pairs={{12,0},{0,4},{4,8},{8,12},{13,1},{1,5},{5,9},{9,13},{14,2},{2,6},{... | collective-permute-start | bytes 147464 | tf_op jit(solution)/shard_map/ppermute | solution.py:272
  19.5 1.7 %collective-permute-start.7 = (bf16[4,6144]{1,0:T(4,128)(2,1)S(1)}, bf16[4,6144]{1,0:T(4,128)(2,1)S(1)}, u32[]{:S(2)}, u32[]{:S(2)}) collective-permute-start(bf16[4,6144]{1,0:T(4,128)(2,1)S(1)} %get-tuple-element.15), channel_id=1, source_target_pairs={{8,0},{12,4},{0,8},{4,12},{9,1},{13,5},{1,9},{5,13},{10,2},{14,6},... | collective-permute-start | bytes 147464 | tf_op jit(solution)/shard_map/ppermute | solution.py:272
  21.2 2.2 %collective-permute-start.8 = (bf16[4,6144]{1,0:T(4,128)(2,1)S(1)}, bf16[4,6144]{1,0:T(4,128)(2,1)S(1)}, u32[]{:S(2)}, u32[]{:S(2)}) collective-permute-start(bf16[4,6144]{1,0:T(4,128)(2,1)S(1)} %get-tuple-element.16), channel_id=1, source_target_pairs={{4,0},{8,4},{12,8},{0,12},{5,1},{9,5},{13,9},{1,13},{6,2},{10,6},{... | collective-permute-start | bytes 147464 | tf_op jit(solution)/shard_map/ppermute | solution.py:272
  23.4 0.6 %collective-permute-done.6.refs_0_ = bf16[4,6144]{1,0:T(4,128)(2,1)S(1)} collective-permute-done((bf16[4,6144]{1,0:T(4,128)(2,1)S(1)}, bf16[4,6144]{1,0:T(4,128)(2,1)S(1)}, u32[]{:S(2)}, u32[]{:S(2)}) %collective-permute-start.6) | collective-permute-done | bytes 49184 | tf_op jit(solution)/shard_map/ppermute | solution.py:272
  24.0 2.1 %collective-permute-done.7.refs_1_ = bf16[4,6144]{1,0:T(4,128)(2,1)S(1)} collective-permute-done((bf16[4,6144]{1,0:T(4,128)(2,1)S(1)}, bf16[4,6144]{1,0:T(4,128)(2,1)S(1)}, u32[]{:S(2)}, u32[]{:S(2)}) %collective-permute-start.7) | collective-permute-done | bytes 49184 | tf_op jit(solution)/shard_map/ppermute | solution.py:272
  26.1 0.7 %finish.1 = (f32[4,2,2048]{2,1,0:T(2,128)}, f32[4,2048]{1,0:T(4,128)}, f32[128]{0:T(128)}) custom-call(f32[1,128]{1,0:T(1,128)S(1)} %get-tuple-element.12.found_ref, f32[4,6144]{1,0:T(4,128)S(1)} %get-tuple-element.13.own_ref, bf16[4,6144]{1,0:T(4,128)(2,1)S(1)} %collective-permute-done.6.refs_0_, bf16[4,6144]{1,0:T(4,128)(2,1)S(1)} %collective-permute-done.7.refs_1_, ...), custom_call_target="tpu_custom_call" | custom-call | tf_op jit(solution)/shard_map/finish/pallas_call | solution.py:244
  (17 shorter events, 0.0 us)
Async XLA Ops:
  0.6 6.5 %copy-start.2 = (bf16[4,128,768]{2,1,0:T(8,128)(2,1)S(1)}, bf16[4,128,768]{2,1,0:T(8,128)(2,1)}, u32[]{:S(2)}) copy-start(bf16[4,128,768]{2,1,0:T(8,128)(2,1)} %constant.2.clone.table_ref) | copy-start | bytes 2359300
  0.6 0.8 %copy-start.3 = (bf16[4,2,2048]{2,1,0:T(2,128)(2,1)S(1)}, bf16[4,2,2048]{2,1,0:T(2,128)(2,1)}, u32[]{:S(2)}) copy-start(bf16[4,2,2048]{2,1,0:T(2,128)(2,1)} %refs_0_) | copy-start | bytes 98308
  0.7 6.4 %copy-start.4 = (f32[2048]{0:T(1024)S(1)}, f32[2048]{0:T(1024)}, u32[]{:S(2)}) copy-start(f32[2048]{0:T(1024)} %param.13) | copy-start | bytes 24580
  0.7 6.4 %copy-start.5 = (s32[512,2]{0,1:T(2,128)S(1)}, s32[512,2]{0,1:T(2,128)}, u32[]{:S(2)}) copy-start(s32[512,2]{0,1:T(2,128)} %param.12) | copy-start | bytes 12292
  0.7 6.4 %copy-start.1 = (bf16[512,2048]{1,0:T(8,128)(2,1)S(1)}, bf16[512,2048]{1,0:T(8,128)(2,1)}, u32[]{:S(2)}) copy-start(bf16[512,2048]{1,0:T(8,128)(2,1)} %ctf_ref.1) | copy-start | bytes 6291460
  0.7 6.4 %copy-start = (bf16[512,2,2048]{2,1,0:T(2,128)(2,1)S(1)}, bf16[512,2,2048]{2,1,0:T(2,128)(2,1)}, u32[]{:S(2)}) copy-start(bf16[512,2,2048]{2,1,0:T(2,128)(2,1)} %param.9) | copy-start | bytes 12582916
  1.5 9.3 %collective-permute-start.2 = (bf16[4,2,2048]{2,1,0:T(2,128)(2,1)S(1)}, bf16[4,2,2048]{2,1,0:T(2,128)(2,1)S(1)}, u32[]{:S(2)}, u32[]{:S(2)}) collective-permute-start(bf16[4,2,2048]{2,1,0:T(2,128)(2,1)S(1)} %copy-done.3), channel_id=1, source_target_pairs={{8,0},{12,4},{0,8},{4,12},{9,1},{13,5},{1,9},{5,13},{10,2},{14,6},... | collective-permute-start | bytes 98312 | tf_op jit(solution)/shard_map/ppermute | solution.py:276
  5.5 5.7 %collective-permute-start.1 = (bf16[4,2,2048]{2,1,0:T(2,128)(2,1)S(1)}, bf16[4,2,2048]{2,1,0:T(2,128)(2,1)S(1)}, u32[]{:S(2)}, u32[]{:S(2)}) collective-permute-start(bf16[4,2,2048]{2,1,0:T(2,128)(2,1)S(1)} %copy-done.3), channel_id=1, source_target_pairs={{12,0},{8,4},{4,8},{0,12},{13,1},{9,5},{5,9},{1,13},{14,2},{10,6},... | collective-permute-start | bytes 98312 | tf_op jit(solution)/shard_map/ppermute | solution.py:276
  6.9 4.4 %collective-permute-start = (bf16[4,2,2048]{2,1,0:T(2,128)(2,1)S(1)}, bf16[4,2,2048]{2,1,0:T(2,128)(2,1)S(1)}, u32[]{:S(2)}, u32[]{:S(2)}) collective-permute-start(bf16[4,2,2048]{2,1,0:T(2,128)(2,1)S(1)} %copy-done.3), channel_id=1, source_target_pairs={{4,0},{0,4},{12,8},{8,12},{5,1},{1,5},{13,9},{9,13},{6,2},{2,6},{1... | collective-permute-start | bytes 98312 | tf_op jit(solution)/shard_map/ppermute | solution.py:276
  7.1 4.1 %copy-start.6 = (s32[1,2]{1,0:T(1,128)S(1)}, s32[1,2]{1,0:T(1,128)}, u32[]{:S(2)}) copy-start(s32[1,2]{1,0:T(1,128)} %allowed_ref.1) | copy-start | bytes 28
  7.1 4.1 %copy-start.7 = (s32[16]{0:T(128)S(1)}, s32[16]{0:T(128)}, u32[]{:S(2)}) copy-start(s32[16]{0:T(128)} %param.14) | copy-start | bytes 196
  7.1 4.1 %copy-start.8 = (f32[4]{0:T(128)S(1)}, f32[4]{0:T(128)}, u32[]{:S(2)}) copy-start(f32[4]{0:T(128)} %param.15) | copy-start | bytes 52
  13.0 3.7 %collective-permute-start.5 = (f32[16,512]{1,0:T(8,128)S(1)}, f32[16,512]{1,0:T(8,128)S(1)}, u32[]{:S(2)}, u32[]{:S(2)}) collective-permute-start(f32[16,512]{1,0:T(8,128)S(1)} %score.1.refs_0_), channel_id=1, source_target_pairs={{3,0},{2,1},{1,2},{0,3},{7,4},{6,5},{5,6},{4,7},{11,8},{10,9},{9,1... | collective-permute-start | bytes 98312 | tf_op jit(solution)/shard_map/ppermute | solution.py:276
  13.1 4.0 %collective-permute-start.4 = (f32[16,512]{1,0:T(8,128)S(1)}, f32[16,512]{1,0:T(8,128)S(1)}, u32[]{:S(2)}, u32[]{:S(2)}) collective-permute-start(f32[16,512]{1,0:T(8,128)S(1)} %score.1.refs_0_), channel_id=1, source_target_pairs={{2,0},{3,1},{0,2},{1,3},{6,4},{7,5},{4,6},{5,7},{10,8},{11,9},{8,1... | collective-permute-start | bytes 98312 | tf_op jit(solution)/shard_map/ppermute | solution.py:276
  14.6 2.5 %collective-permute-start.3 = (f32[16,512]{1,0:T(8,128)S(1)}, f32[16,512]{1,0:T(8,128)S(1)}, u32[]{:S(2)}, u32[]{:S(2)}) collective-permute-start(f32[16,512]{1,0:T(8,128)S(1)} %score.1.refs_0_), channel_id=1, source_target_pairs={{1,0},{0,1},{3,2},{2,3},{5,4},{4,5},{7,6},{6,7},{9,8},{8,9},{11,10... | collective-permute-start | bytes 98312 | tf_op jit(solution)/shard_map/ppermute | solution.py:276
  18.1 5.9 %collective-permute-start.6 = (bf16[4,6144]{1,0:T(4,128)(2,1)S(1)}, bf16[4,6144]{1,0:T(4,128)(2,1)S(1)}, u32[]{:S(2)}, u32[]{:S(2)}) collective-permute-start(bf16[4,6144]{1,0:T(4,128)(2,1)S(1)} %get-tuple-element.14), channel_id=1, source_target_pairs={{12,0},{0,4},{4,8},{8,12},{13,1},{1,5},{5,9},{9,13},{14,2},{2,6},{... | collective-permute-start | bytes 147464 | tf_op jit(solution)/shard_map/ppermute | solution.py:272
  19.5 6.6 %collective-permute-start.7 = (bf16[4,6144]{1,0:T(4,128)(2,1)S(1)}, bf16[4,6144]{1,0:T(4,128)(2,1)S(1)}, u32[]{:S(2)}, u32[]{:S(2)}) collective-permute-start(bf16[4,6144]{1,0:T(4,128)(2,1)S(1)} %get-tuple-element.15), channel_id=1, source_target_pairs={{8,0},{12,4},{0,8},{4,12},{9,1},{13,5},{1,9},{5,13},{10,2},{14,6},... | collective-permute-start | bytes 147464 | tf_op jit(solution)/shard_map/ppermute | solution.py:272
  21.2 4.9 %collective-permute-start.8 = (bf16[4,6144]{1,0:T(4,128)(2,1)S(1)}, bf16[4,6144]{1,0:T(4,128)(2,1)S(1)}, u32[]{:S(2)}, u32[]{:S(2)}) collective-permute-start(bf16[4,6144]{1,0:T(4,128)(2,1)S(1)} %get-tuple-element.16), channel_id=1, source_target_pairs={{4,0},{8,4},{12,8},{0,12},{5,1},{9,5},{13,9},{1,13},{6,2},{10,6},{... | collective-permute-start | bytes 147464 | tf_op jit(solution)/shard_map/ppermute | solution.py:272

commit v6 on v5

--- a/solution.py
+++ b/solution.py
@@ -17,8 +17,8 @@
 ROW = 2 * KMAX
 REACH = 8
 GROUP = 16
-FETCH = {2: (1,), 4: (1, 3, 2)}
-RETURN = {2: (1,), 4: (1, 2, 3)}
+FETCH = {2: ((1, 0),), 4: ((1, 0, 3, 2), (2, 3, 1, 0), (3, 2, 0, 1))}
+RETURN = {2: ((1, 0),), 4: ((1, 2, 3, 0), (2, 3, 0, 1), (3, 0, 1, 2))}
 SHARE = (1, 2, 3)
 SPLITS = 3
 
@@ -141,7 +141,12 @@
 
     line = lax.broadcasted_iota(jnp.int32, (orients, orients), 0)
     lane = lax.broadcasted_iota(jnp.int32, (orients, orients), 1)
-    block = lax.rem(line // each + me, blocks)
+    block = line // each
+    if turned:
+        slot = block
+        block = jnp.where(slot == 0, me, 0)
+        for k in range(1, blocks):
+            block = jnp.where(slot == k, entry(RETURN[blocks][k - 1], me), block)
     own = lane == block * each + lax.rem(line, each)
     prior = jnp.zeros((orients, orients), jnp.float32)
     for c in range(CLASSES):
@@ -161,15 +166,12 @@
     joint = jnp.concatenate(parts, axis=0).astype(jnp.bfloat16)
     raw = lax.dot_general(joint, whole(data_ref), (((1,), (1,)), ((), ())), preferred_element_type=jnp.float32)
     if turned:
-        came = [raw[:each]] * blocks
-        for k, mask in enumerate(FETCH[blocks], start=1):
-            came[mask] = raw[k * each : (k + 1) * each]
+        came = [raw[k * each : (k + 1) * each] for k in range(blocks)]
         leave = came[:1]
         for k in range(1, blocks):
-            at = lax.rem(me + k, blocks) ^ me
             value = came[1]
             for other in range(2, blocks):
-                value = jnp.where(at == other, came[other], value)
+                value = jnp.where(entry(FETCH[blocks][other - 1], me) == entry(RETURN[blocks][k - 1], me), came[other], value)
             leave.append(value)
         raw = jnp.concatenate(leave, axis=0)
     out_ref[...] = raw * (1.0 / math.sqrt(PIXC)) + bias
@@ -268,8 +270,11 @@
     )()
 
 
-def rotate(value, axis, size, by):
-    return lax.ppermute(value, axis, [((j + by) % size, j) for j in range(size)])
+def entry(table, me):
+    value = jnp.int32(table[0])
+    for j in range(1, len(table)):
+        value = jnp.where(me == j, jnp.int32(table[j]), value)
+    return value
 
 
 def swap(value, axes, size, mask):
@@ -284,7 +289,7 @@
     first = opening()
     projections, first = lax.optimization_barrier((projections, first))
     if direct:
-        projs = [projections] + [swap(projections, "blk", blocks, k) for k in FETCH[blocks]]
+        projs = [projections] + [lax.ppermute(projections, "blk", [(source, j) for j, source in enumerate(sources)]) for sources in FETCH[blocks]]
     else:
         projs = [lax.all_gather(projections, "blk", axis=0, tiled=True)]
     data = prepare(images, ctf, shifts, inv_sigma2, pieces, first)
@@ -296,7 +301,9 @@
     best, own, *away = back(data, parts, blocks - 1 if direct else 0, pieces)
     if not direct:
         own = lax.psum_scatter(own, "blk", scatter_dimension=0, tiled=True)
-    arrived = [rotate(away[k - 1], "blk", blocks, blocks - k) for k in (RETURN[blocks] if direct else ())]
+    arrived = [
+        lax.ppermute(value, "blk", list(enumerate(goals))) for value, goals in zip(away, RETURN[blocks] if direct else ())
+    ]
     return finish(best, own, arrived)
 
 

time: 26.9 us -> 26.8 us (level)
  waiting for transfers between devices: 5.26 us -> 4.97 us
    ppermute x3 -> x6, starting transfers between devices: 5.35 us -> 11.2 us  [the longest x3 5.62 us: body(): lax.ppermute(projections, 'blk', [(source, j) for j, source in enumerate(...]
    ppermute x6 -> x3, starting transfers between devices: 7.53 us -> 1.93 us  [swap(): return lax.ppermute(value, axes, [(j ^ mask, j) for j in range(size)])]
    ppermute x3 -> x6, waiting for transfers between devices: 2.65 us -> 2.47 us  [the longest x3 2.46 us: body(): lax.ppermute(value, 'blk', list(enumerate(goals)))]
    ppermute x6 -> x3, waiting for transfers between devices: 2.61 us -> 2.5 us  [swap(): return lax.ppermute(value, axes, [(j ^ mask, j) for j in range(size)])]
  transfers between devices with their start and end apart: 9 -> 9, of which waited for: 5 -> 4; matrix products, arithmetic and copies ran while one was open for 0% -> 0% of each run, Pallas kernels for 14% -> 14%
where the time goes in v6:
time: 26.8 us; the launch traced here: 26.7 us
  starting transfers between devices  13.1 us (49%)
  Pallas kernels  6.99 us (26%)
  waiting for transfers between devices  4.97 us (19%)
  local copies, waits for them, and re-layouts  0.82 us (3%)
  between operations  0.79 us (3%)
    ppermute x3, starting transfers between devices, body(): lax.ppermute(projections, 'blk', [(source, j) for j, source in enumerate(...  5.62 us
    ppermute x3, starting transfers between devices, body(): lax.ppermute(value, 'blk', list(enumerate(goals)))  5.54 us
    pallas_call x1, Pallas kernels, prepare(): pl.pallas_call(functools.partial(prepare_kernel, rows), in_specs=[pl.Bloc...  3.63 us
    ppermute x3, waiting for transfers between devices, swap(): return lax.ppermute(value, axes, [(j ^ mask, j) for j in range(size)])  2.5 us
    ppermute x3, waiting for transfers between devices, body(): lax.ppermute(value, 'blk', list(enumerate(goals)))  2.46 us
    ppermute x3, starting transfers between devices, swap(): return lax.ppermute(value, axes, [(j ^ mask, j) for j in range(size)])  1.93 us
    pallas_call x1, Pallas kernels, score(): pl.pallas_call(functools.partial(score_kernel, blocks, turned), out_shape...  1.74 us
    pallas_call x1, Pallas kernels, back(): pl.pallas_call(functools.partial(back_kernel, len(parts)), out_shape=[plt...  0.95 us
  transfers between devices with their start and end apart: 9, of which 4 were waited for; matrix products, arithmetic and copies ran while one was open for 0% of the time, Pallas kernels for 14%

profile of v6, /device:TPU:0, one launch (start us, length us, event | category | flops | bytes accessed | tf_op | source)
XLA Modules:
  0.0 26.7 jit_solution(9291872092222047521)
XLA Ops:
  0.6 0.0 copy-start.2
  0.7 0.8 %copy-done.3 = bf16[4,2,2048]{2,1,0:T(2,128)(2,1)S(1)} copy-done((bf16[4,2,2048]{2,1,0:T(2,128)(2,1)S(1)}, bf16[4,2,2048]{2,1,0:T(2,128)(2,1)}, u32[]{:S(2)}) %copy-start.3) | copy-done | bytes 32792
  1.5 4.0 %collective-permute-start.2 = (bf16[4,2,2048]{2,1,0:T(2,128)(2,1)S(1)}, bf16[4,2,2048]{2,1,0:T(2,128)(2,1)S(1)}, u32[]{:S(2)}, u32[]{:S(2)}) collective-permute-start(bf16[4,2,2048]{2,1,0:T(2,128)(2,1)S(1)} %copy-done.3), channel_id=1, source_target_pairs={{12,0},{8,4},{0,8},{4,12},{13,1},{9,5},{1,9},{5,13},{14,2},{10,6},... | collective-permute-start | bytes 98312 | tf_op jit(solution)/shard_map/ppermute | solution.py:292
  5.5 1.0 %collective-permute-start.1 = (bf16[4,2,2048]{2,1,0:T(2,128)(2,1)S(1)}, bf16[4,2,2048]{2,1,0:T(2,128)(2,1)S(1)}, u32[]{:S(2)}, u32[]{:S(2)}) collective-permute-start(bf16[4,2,2048]{2,1,0:T(2,128)(2,1)S(1)} %copy-done.3), channel_id=1, source_target_pairs={{8,0},{12,4},{4,8},{0,12},{9,1},{13,5},{5,9},{1,13},{10,2},{14,6},... | collective-permute-start | bytes 98312 | tf_op jit(solution)/shard_map/ppermute | solution.py:292
  6.5 0.6 %collective-permute-start = (bf16[4,2,2048]{2,1,0:T(2,128)(2,1)S(1)}, bf16[4,2,2048]{2,1,0:T(2,128)(2,1)S(1)}, u32[]{:S(2)}, u32[]{:S(2)}) collective-permute-start(bf16[4,2,2048]{2,1,0:T(2,128)(2,1)S(1)} %copy-done.3), channel_id=1, source_target_pairs={{4,0},{0,4},{12,8},{8,12},{5,1},{1,5},{13,9},{9,13},{6,2},{2,6},{1... | collective-permute-start | bytes 98312 | tf_op jit(solution)/shard_map/ppermute | solution.py:292
  7.1 0.0 copy-start.6
  7.1 0.0 copy-start.7
  7.1 0.0 copy-start.8
  7.2 3.6 %prepare.1.data_ref = bf16[32,48,16,128]{3,2,1,0:T(8,128)(2,1)S(1)} custom-call(bf16[16384,128]{1,0:T(8,128)(2,1)S(1)} %bitcast.9, bf16[512,2048]{1,0:T(8,128)(2,1)S(1)} %copy-done.1, s32[2,512]{1,0:T(2,128)S(1)} %bitcast.11, f32[1,2048]{1,0:T(1,128)S(1)} %bitcast.10, bf16[4,128,768]{2,1,0:T(8,128)(2,1)S(1)} %copy-done.2, f32[8,128]{1,0:T(8,128)S(1)} %opening.1.first_ref), custom_call_target="tpu_custom_call" | custom-call | tf_op jit(solution)/shard_map/prepare/pallas_call | solution.py:116
  10.8 0.0 collective-permute-done.2.refs_3_
  10.8 0.0 collective-permute-done.1.refs_2_
  10.9 1.7 %score.1.refs_0_ = f32[16,512]{1,0:T(8,128)S(1)} custom-call(bf16[32,48,16,128]{3,2,1,0:T(8,128)(2,1)S(1)} %prepare.1.data_ref, s32[1,2]{1,0:T(1,128)S(1)} %copy-done.6, s32[1,16]{1,0:T(1,128)S(1)} %bitcast.12, f32[1,4]{1,0:T(1,128)S(1)} %bitcast.13, bf16[4,2,2048]{2,1,0:T(2,128)(2,1)S(1)} %copy-done.3, ...), custom_call_target="tpu_custom_call" | custom-call | tf_op jit(solution)/shard_map/score/pallas_call | solution.py:182
  12.6 0.4 %collective-permute-start.5 = (f32[16,512]{1,0:T(8,128)S(1)}, f32[16,512]{1,0:T(8,128)S(1)}, u32[]{:S(2)}, u32[]{:S(2)}) collective-permute-start(f32[16,512]{1,0:T(8,128)S(1)} %score.1.refs_0_), channel_id=1, source_target_pairs={{3,0},{2,1},{1,2},{0,3},{7,4},{6,5},{5,6},{4,7},{11,8},{10,9},{9,1... | collective-permute-start | bytes 98312 | tf_op jit(solution)/shard_map/ppermute | solution.py:281
  13.0 1.2 %collective-permute-start.4 = (f32[16,512]{1,0:T(8,128)S(1)}, f32[16,512]{1,0:T(8,128)S(1)}, u32[]{:S(2)}, u32[]{:S(2)}) collective-permute-start(f32[16,512]{1,0:T(8,128)S(1)} %score.1.refs_0_), channel_id=1, source_target_pairs={{2,0},{3,1},{0,2},{1,3},{6,4},{7,5},{4,6},{5,7},{10,8},{11,9},{8,1... | collective-permute-start | bytes 98312 | tf_op jit(solution)/shard_map/ppermute | solution.py:281
  14.2 0.3 %collective-permute-start.3 = (f32[16,512]{1,0:T(8,128)S(1)}, f32[16,512]{1,0:T(8,128)S(1)}, u32[]{:S(2)}, u32[]{:S(2)}) collective-permute-start(f32[16,512]{1,0:T(8,128)S(1)} %score.1.refs_0_), channel_id=1, source_target_pairs={{1,0},{0,1},{3,2},{2,3},{5,4},{4,5},{7,6},{6,7},{9,8},{8,9},{11,10... | collective-permute-start | bytes 98312 | tf_op jit(solution)/shard_map/ppermute | solution.py:281
  14.5 1.8 %collective-permute-done.5.refs_3_ = f32[16,512]{1,0:T(8,128)S(1)} collective-permute-done((f32[16,512]{1,0:T(8,128)S(1)}, f32[16,512]{1,0:T(8,128)S(1)}, u32[]{:S(2)}, u32[]{:S(2)}) %collective-permute-start.5) | collective-permute-done | bytes 32800 | tf_op jit(solution)/shard_map/ppermute | solution.py:281
  16.3 0.7 %collective-permute-done.4.refs_2_ = f32[16,512]{1,0:T(8,128)S(1)} collective-permute-done((f32[16,512]{1,0:T(8,128)S(1)}, f32[16,512]{1,0:T(8,128)S(1)}, u32[]{:S(2)}, u32[]{:S(2)}) %collective-permute-start.4) | collective-permute-done | bytes 32800 | tf_op jit(solution)/shard_map/ppermute | solution.py:281
  17.0 0.9 %back.1 = (f32[1,128]{1,0:T(1,128)S(1)}, f32[4,6144]{1,0:T(4,128)S(1)}, bf16[4,6144]{1,0:T(4,128)(2,1)S(1)}, bf16[4,6144]{1,0:T(4,128)(2,1)S(1)}, bf16[4,6144]{1,0:T(4,128)(2,1)S(1)}) custom-call(bf16[32,48,16,128]{3,2,1,0:T(8,128)(2,1)S(1)} %prepare.1.data_ref, f32[16,512]{1,0:T(8,128)S(1)} %score.1.refs_0_, f32[16,512]{1,0:T(8,128)S(1)} %collective-permute-done.3.refs_1_, ...), custom_call_target="tpu_custom_call" | custom-call | tf_op jit(solution)/shard_map/back/pallas_call | solution.py:218
  18.0 1.4 %collective-permute-start.6 = (bf16[4,6144]{1,0:T(4,128)(2,1)S(1)}, bf16[4,6144]{1,0:T(4,128)(2,1)S(1)}, u32[]{:S(2)}, u32[]{:S(2)}) collective-permute-start(bf16[4,6144]{1,0:T(4,128)(2,1)S(1)} %get-tuple-element.14), channel_id=1, source_target_pairs={{0,4},{4,8},{8,12},{12,0},{1,5},{5,9},{9,13},{13,1},{2,6},{6,10},{... | collective-permute-start | bytes 147464 | tf_op jit(solution)/shard_map/ppermute | solution.py:305
  19.4 1.7 %collective-permute-start.7 = (bf16[4,6144]{1,0:T(4,128)(2,1)S(1)}, bf16[4,6144]{1,0:T(4,128)(2,1)S(1)}, u32[]{:S(2)}, u32[]{:S(2)}) collective-permute-start(bf16[4,6144]{1,0:T(4,128)(2,1)S(1)} %get-tuple-element.15), channel_id=1, source_target_pairs={{0,8},{4,12},{8,0},{12,4},{1,9},{5,13},{9,1},{13,5},{2,10},{6,14},... | collective-permute-start | bytes 147464 | tf_op jit(solution)/shard_map/ppermute | solution.py:305
  21.0 2.5 %collective-permute-start.8 = (bf16[4,6144]{1,0:T(4,128)(2,1)S(1)}, bf16[4,6144]{1,0:T(4,128)(2,1)S(1)}, u32[]{:S(2)}, u32[]{:S(2)}) collective-permute-start(bf16[4,6144]{1,0:T(4,128)(2,1)S(1)} %get-tuple-element.16), channel_id=1, source_target_pairs={{0,12},{4,0},{8,4},{12,8},{1,13},{5,1},{9,5},{13,9},{2,14},{6,2},{... | collective-permute-start | bytes 147464 | tf_op jit(solution)/shard_map/ppermute | solution.py:305
  23.5 0.4 %collective-permute-done.6.refs_0_ = bf16[4,6144]{1,0:T(4,128)(2,1)S(1)} collective-permute-done((bf16[4,6144]{1,0:T(4,128)(2,1)S(1)}, bf16[4,6144]{1,0:T(4,128)(2,1)S(1)}, u32[]{:S(2)}, u32[]{:S(2)}) %collective-permute-start.6) | collective-permute-done | bytes 49184 | tf_op jit(solution)/shard_map/ppermute | solution.py:305
  23.9 2.1 %collective-permute-done.7.refs_1_ = bf16[4,6144]{1,0:T(4,128)(2,1)S(1)} collective-permute-done((bf16[4,6144]{1,0:T(4,128)(2,1)S(1)}, bf16[4,6144]{1,0:T(4,128)(2,1)S(1)}, u32[]{:S(2)}, u32[]{:S(2)}) %collective-permute-start.7) | collective-permute-done | bytes 49184 | tf_op jit(solution)/shard_map/ppermute | solution.py:305
  26.0 0.7 %finish.1 = (f32[4,2,2048]{2,1,0:T(2,128)}, f32[4,2048]{1,0:T(4,128)}, f32[128]{0:T(128)}) custom-call(f32[1,128]{1,0:T(1,128)S(1)} %get-tuple-element.12.found_ref, f32[4,6144]{1,0:T(4,128)S(1)} %get-tuple-element.13.own_ref, bf16[4,6144]{1,0:T(4,128)(2,1)S(1)} %collective-permute-done.6.refs_0_, bf16[4,6144]{1,0:T(4,128)(2,1)S(1)} %collective-permute-done.7.refs_1_, ...), custom_call_target="tpu_custom_call" | custom-call | tf_op jit(solution)/shard_map/finish/pallas_call | solution.py:246
  (17 shorter events, 0.0 us)
Async XLA Ops:
  0.6 6.5 %copy-start.2 = (bf16[4,128,768]{2,1,0:T(8,128)(2,1)S(1)}, bf16[4,128,768]{2,1,0:T(8,128)(2,1)}, u32[]{:S(2)}) copy-start(bf16[4,128,768]{2,1,0:T(8,128)(2,1)} %constant.2.clone.table_ref) | copy-start | bytes 2359300
  0.6 0.8 %copy-start.3 = (bf16[4,2,2048]{2,1,0:T(2,128)(2,1)S(1)}, bf16[4,2,2048]{2,1,0:T(2,128)(2,1)}, u32[]{:S(2)}) copy-start(bf16[4,2,2048]{2,1,0:T(2,128)(2,1)} %refs_0_) | copy-start | bytes 98308
  0.7 6.4 %copy-start.4 = (f32[2048]{0:T(1024)S(1)}, f32[2048]{0:T(1024)}, u32[]{:S(2)}) copy-start(f32[2048]{0:T(1024)} %param.13) | copy-start | bytes 24580
  0.7 6.4 %copy-start.5 = (s32[512,2]{0,1:T(2,128)S(1)}, s32[512,2]{0,1:T(2,128)}, u32[]{:S(2)}) copy-start(s32[512,2]{0,1:T(2,128)} %param.12) | copy-start | bytes 12292
  0.7 6.4 %copy-start.1 = (bf16[512,2048]{1,0:T(8,128)(2,1)S(1)}, bf16[512,2048]{1,0:T(8,128)(2,1)}, u32[]{:S(2)}) copy-start(bf16[512,2048]{1,0:T(8,128)(2,1)} %ctf_ref.1) | copy-start | bytes 6291460
  0.7 6.4 %copy-start = (bf16[512,2,2048]{2,1,0:T(2,128)(2,1)S(1)}, bf16[512,2,2048]{2,1,0:T(2,128)(2,1)}, u32[]{:S(2)}) copy-start(bf16[512,2,2048]{2,1,0:T(2,128)(2,1)} %param.9) | copy-start | bytes 12582916
  1.5 9.3 %collective-permute-start.2 = (bf16[4,2,2048]{2,1,0:T(2,128)(2,1)S(1)}, bf16[4,2,2048]{2,1,0:T(2,128)(2,1)S(1)}, u32[]{:S(2)}, u32[]{:S(2)}) collective-permute-start(bf16[4,2,2048]{2,1,0:T(2,128)(2,1)S(1)} %copy-done.3), channel_id=1, source_target_pairs={{12,0},{8,4},{0,8},{4,12},{13,1},{9,5},{1,9},{5,13},{14,2},{10,6},... | collective-permute-start | bytes 98312 | tf_op jit(solution)/shard_map/ppermute | solution.py:292
  5.5 5.3 %collective-permute-start.1 = (bf16[4,2,2048]{2,1,0:T(2,128)(2,1)S(1)}, bf16[4,2,2048]{2,1,0:T(2,128)(2,1)S(1)}, u32[]{:S(2)}, u32[]{:S(2)}) collective-permute-start(bf16[4,2,2048]{2,1,0:T(2,128)(2,1)S(1)} %copy-done.3), channel_id=1, source_target_pairs={{8,0},{12,4},{4,8},{0,12},{9,1},{13,5},{5,9},{1,13},{10,2},{14,6},... | collective-permute-start | bytes 98312 | tf_op jit(solution)/shard_map/ppermute | solution.py:292
  6.5 4.3 %collective-permute-start = (bf16[4,2,2048]{2,1,0:T(2,128)(2,1)S(1)}, bf16[4,2,2048]{2,1,0:T(2,128)(2,1)S(1)}, u32[]{:S(2)}, u32[]{:S(2)}) collective-permute-start(bf16[4,2,2048]{2,1,0:T(2,128)(2,1)S(1)} %copy-done.3), channel_id=1, source_target_pairs={{4,0},{0,4},{12,8},{8,12},{5,1},{1,5},{13,9},{9,13},{6,2},{2,6},{1... | collective-permute-start | bytes 98312 | tf_op jit(solution)/shard_map/ppermute | solution.py:292
  7.1 3.7 %copy-start.6 = (s32[1,2]{1,0:T(1,128)S(1)}, s32[1,2]{1,0:T(1,128)}, u32[]{:S(2)}) copy-start(s32[1,2]{1,0:T(1,128)} %allowed_ref.1) | copy-start | bytes 28
  7.1 3.7 %copy-start.7 = (s32[16]{0:T(128)S(1)}, s32[16]{0:T(128)}, u32[]{:S(2)}) copy-start(s32[16]{0:T(128)} %param.14) | copy-start | bytes 196
  7.1 3.7 %copy-start.8 = (f32[4]{0:T(128)S(1)}, f32[4]{0:T(128)}, u32[]{:S(2)}) copy-start(f32[4]{0:T(128)} %param.15) | copy-start | bytes 52
  12.6 3.7 %collective-permute-start.5 = (f32[16,512]{1,0:T(8,128)S(1)}, f32[16,512]{1,0:T(8,128)S(1)}, u32[]{:S(2)}, u32[]{:S(2)}) collective-permute-start(f32[16,512]{1,0:T(8,128)S(1)} %score.1.refs_0_), channel_id=1, source_target_pairs={{3,0},{2,1},{1,2},{0,3},{7,4},{6,5},{5,6},{4,7},{11,8},{10,9},{9,1... | collective-permute-start | bytes 98312 | tf_op jit(solution)/shard_map/ppermute | solution.py:281
  13.0 4.0 %collective-permute-start.4 = (f32[16,512]{1,0:T(8,128)S(1)}, f32[16,512]{1,0:T(8,128)S(1)}, u32[]{:S(2)}, u32[]{:S(2)}) collective-permute-start(f32[16,512]{1,0:T(8,128)S(1)} %score.1.refs_0_), channel_id=1, source_target_pairs={{2,0},{3,1},{0,2},{1,3},{6,4},{7,5},{4,6},{5,7},{10,8},{11,9},{8,1... | collective-permute-start | bytes 98312 | tf_op jit(solution)/shard_map/ppermute | solution.py:281
  14.2 2.8 %collective-permute-start.3 = (f32[16,512]{1,0:T(8,128)S(1)}, f32[16,512]{1,0:T(8,128)S(1)}, u32[]{:S(2)}, u32[]{:S(2)}) collective-permute-start(f32[16,512]{1,0:T(8,128)S(1)} %score.1.refs_0_), channel_id=1, source_target_pairs={{1,0},{0,1},{3,2},{2,3},{5,4},{4,5},{7,6},{6,7},{9,8},{8,9},{11,10... | collective-permute-start | bytes 98312 | tf_op jit(solution)/shard_map/ppermute | solution.py:281
  18.0 5.9 %collective-permute-start.6 = (bf16[4,6144]{1,0:T(4,128)(2,1)S(1)}, bf16[4,6144]{1,0:T(4,128)(2,1)S(1)}, u32[]{:S(2)}, u32[]{:S(2)}) collective-permute-start(bf16[4,6144]{1,0:T(4,128)(2,1)S(1)} %get-tuple-element.14), channel_id=1, source_target_pairs={{0,4},{4,8},{8,12},{12,0},{1,5},{5,9},{9,13},{13,1},{2,6},{6,10},{... | collective-permute-start | bytes 147464 | tf_op jit(solution)/shard_map/ppermute | solution.py:305
  19.4 6.6 %collective-permute-start.7 = (bf16[4,6144]{1,0:T(4,128)(2,1)S(1)}, bf16[4,6144]{1,0:T(4,128)(2,1)S(1)}, u32[]{:S(2)}, u32[]{:S(2)}) collective-permute-start(bf16[4,6144]{1,0:T(4,128)(2,1)S(1)} %get-tuple-element.15), channel_id=1, source_target_pairs={{0,8},{4,12},{8,0},{12,4},{1,9},{5,13},{9,1},{13,5},{2,10},{6,14},... | collective-permute-start | bytes 147464 | tf_op jit(solution)/shard_map/ppermute | solution.py:305
  21.0 4.9 %collective-permute-start.8 = (bf16[4,6144]{1,0:T(4,128)(2,1)S(1)}, bf16[4,6144]{1,0:T(4,128)(2,1)S(1)}, u32[]{:S(2)}, u32[]{:S(2)}) collective-permute-start(bf16[4,6144]{1,0:T(4,128)(2,1)S(1)} %get-tuple-element.16), channel_id=1, source_target_pairs={{0,12},{4,0},{8,4},{12,8},{1,13},{5,1},{9,5},{13,9},{2,14},{6,2},{... | collective-permute-start | bytes 147464 | tf_op jit(solution)/shard_map/ppermute | solution.py:305

commit v7 on v6

--- a/solution.py
+++ b/solution.py
@@ -160,8 +160,7 @@
 
     parts = []
     for ref in proj_refs:
-        wide = ref[...].astype(jnp.float32)
-        real, imag = wide[:, 0, :], wide[:, 1, :]
+        real, imag = (ref[:, part, :].astype(jnp.float32) for part in range(2))
         parts.append(jnp.concatenate([2.0 * real, 2.0 * imag, -(real * real + imag * imag)], axis=1))
     joint = jnp.concatenate(parts, axis=0).astype(jnp.bfloat16)
     raw = lax.dot_general(joint, whole(data_ref), (((1,), (1,)), ((), ())), preferred_element_type=jnp.float32)

time: 26.8 us -> 26.8 us (level)
  no operation moved by 1% of the time
where the time goes in v7:
time: 26.8 us; the launch traced here: 26.7 us
  starting transfers between devices  13.1 us (49%)
  Pallas kernels  6.99 us (26%)
  waiting for transfers between devices  4.97 us (19%)
  local copies, waits for them, and re-layouts  0.82 us (3%)
  between operations  0.79 us (3%)
    ppermute x3, starting transfers between devices, body(): lax.ppermute(projections, 'blk', [(source, j) for j, source in enumerate(...  5.62 us
    ppermute x3, starting transfers between devices, body(): lax.ppermute(value, 'blk', list(enumerate(goals)))  5.54 us
    pallas_call x1, Pallas kernels, prepare(): pl.pallas_call(functools.partial(prepare_kernel, rows), in_specs=[pl.Bloc...  3.63 us
    ppermute x3, waiting for transfers between devices, swap(): return lax.ppermute(value, axes, [(j ^ mask, j) for j in range(size)])  2.5 us
    ppermute x3, waiting for transfers between devices, body(): lax.ppermute(value, 'blk', list(enumerate(goals)))  2.46 us
    ppermute x3, starting transfers between devices, swap(): return lax.ppermute(value, axes, [(j ^ mask, j) for j in range(size)])  1.93 us
    pallas_call x1, Pallas kernels, score(): pl.pallas_call(functools.partial(score_kernel, blocks, turned), out_shape...  1.74 us
    pallas_call x1, Pallas kernels, back(): pl.pallas_call(functools.partial(back_kernel, len(parts)), out_shape=[plt...  0.95 us
  transfers between devices with their start and end apart: 9, of which 4 were waited for; matrix products, arithmetic and copies ran while one was open for 0% of the time, Pallas kernels for 14%

profile of v7, /device:TPU:0, one launch (start us, length us, event | category | flops | bytes accessed | tf_op | source)
XLA Modules:
  0.0 26.7 jit_solution(9291872092222047521)
XLA Ops:
  0.6 0.0 copy-start.2
  0.7 0.8 %copy-done.3 = bf16[4,2,2048]{2,1,0:T(2,128)(2,1)S(1)} copy-done((bf16[4,2,2048]{2,1,0:T(2,128)(2,1)S(1)}, bf16[4,2,2048]{2,1,0:T(2,128)(2,1)}, u32[]{:S(2)}) %copy-start.3) | copy-done | bytes 32792
  1.5 4.0 %collective-permute-start.2 = (bf16[4,2,2048]{2,1,0:T(2,128)(2,1)S(1)}, bf16[4,2,2048]{2,1,0:T(2,128)(2,1)S(1)}, u32[]{:S(2)}, u32[]{:S(2)}) collective-permute-start(bf16[4,2,2048]{2,1,0:T(2,128)(2,1)S(1)} %copy-done.3), channel_id=1, source_target_pairs={{12,0},{8,4},{0,8},{4,12},{13,1},{9,5},{1,9},{5,13},{14,2},{10,6},... | collective-permute-start | bytes 98312 | tf_op jit(solution)/shard_map/ppermute | solution.py:291
  5.5 1.0 %collective-permute-start.1 = (bf16[4,2,2048]{2,1,0:T(2,128)(2,1)S(1)}, bf16[4,2,2048]{2,1,0:T(2,128)(2,1)S(1)}, u32[]{:S(2)}, u32[]{:S(2)}) collective-permute-start(bf16[4,2,2048]{2,1,0:T(2,128)(2,1)S(1)} %copy-done.3), channel_id=1, source_target_pairs={{8,0},{12,4},{4,8},{0,12},{9,1},{13,5},{5,9},{1,13},{10,2},{14,6},... | collective-permute-start | bytes 98312 | tf_op jit(solution)/shard_map/ppermute | solution.py:291
  6.5 0.6 %collective-permute-start = (bf16[4,2,2048]{2,1,0:T(2,128)(2,1)S(1)}, bf16[4,2,2048]{2,1,0:T(2,128)(2,1)S(1)}, u32[]{:S(2)}, u32[]{:S(2)}) collective-permute-start(bf16[4,2,2048]{2,1,0:T(2,128)(2,1)S(1)} %copy-done.3), channel_id=1, source_target_pairs={{4,0},{0,4},{12,8},{8,12},{5,1},{1,5},{13,9},{9,13},{6,2},{2,6},{1... | collective-permute-start | bytes 98312 | tf_op jit(solution)/shard_map/ppermute | solution.py:291
  7.1 0.0 copy-start.6
  7.1 0.0 copy-start.7
  7.1 0.0 copy-start.8
  7.2 3.6 %prepare.1.data_ref = bf16[32,48,16,128]{3,2,1,0:T(8,128)(2,1)S(1)} custom-call(bf16[16384,128]{1,0:T(8,128)(2,1)S(1)} %bitcast.9, bf16[512,2048]{1,0:T(8,128)(2,1)S(1)} %copy-done.1, s32[2,512]{1,0:T(2,128)S(1)} %bitcast.11, f32[1,2048]{1,0:T(1,128)S(1)} %bitcast.10, bf16[4,128,768]{2,1,0:T(8,128)(2,1)S(1)} %copy-done.2, f32[8,128]{1,0:T(8,128)S(1)} %opening.1.first_ref), custom_call_target="tpu_custom_call" | custom-call | tf_op jit(solution)/shard_map/prepare/pallas_call | solution.py:116
  10.8 0.0 collective-permute-done.2.refs_3_
  10.8 0.0 collective-permute-done.1.refs_2_
  10.9 1.7 %score.1.refs_0_ = f32[16,512]{1,0:T(8,128)S(1)} custom-call(bf16[32,48,16,128]{3,2,1,0:T(8,128)(2,1)S(1)} %prepare.1.data_ref, s32[1,2]{1,0:T(1,128)S(1)} %copy-done.6, s32[1,16]{1,0:T(1,128)S(1)} %bitcast.12, f32[1,4]{1,0:T(1,128)S(1)} %bitcast.13, bf16[4,2,2048]{2,1,0:T(2,128)(2,1)S(1)} %copy-done.3, ...), custom_call_target="tpu_custom_call" | custom-call | tf_op jit(solution)/shard_map/score/pallas_call | solution.py:181
  12.6 0.4 %collective-permute-start.5 = (f32[16,512]{1,0:T(8,128)S(1)}, f32[16,512]{1,0:T(8,128)S(1)}, u32[]{:S(2)}, u32[]{:S(2)}) collective-permute-start(f32[16,512]{1,0:T(8,128)S(1)} %score.1.refs_0_), channel_id=1, source_target_pairs={{3,0},{2,1},{1,2},{0,3},{7,4},{6,5},{5,6},{4,7},{11,8},{10,9},{9,1... | collective-permute-start | bytes 98312 | tf_op jit(solution)/shard_map/ppermute | solution.py:280
  13.0 1.2 %collective-permute-start.4 = (f32[16,512]{1,0:T(8,128)S(1)}, f32[16,512]{1,0:T(8,128)S(1)}, u32[]{:S(2)}, u32[]{:S(2)}) collective-permute-start(f32[16,512]{1,0:T(8,128)S(1)} %score.1.refs_0_), channel_id=1, source_target_pairs={{2,0},{3,1},{0,2},{1,3},{6,4},{7,5},{4,6},{5,7},{10,8},{11,9},{8,1... | collective-permute-start | bytes 98312 | tf_op jit(solution)/shard_map/ppermute | solution.py:280
  14.2 0.3 %collective-permute-start.3 = (f32[16,512]{1,0:T(8,128)S(1)}, f32[16,512]{1,0:T(8,128)S(1)}, u32[]{:S(2)}, u32[]{:S(2)}) collective-permute-start(f32[16,512]{1,0:T(8,128)S(1)} %score.1.refs_0_), channel_id=1, source_target_pairs={{1,0},{0,1},{3,2},{2,3},{5,4},{4,5},{7,6},{6,7},{9,8},{8,9},{11,10... | collective-permute-start | bytes 98312 | tf_op jit(solution)/shard_map/ppermute | solution.py:280
  14.5 1.8 %collective-permute-done.5.refs_3_ = f32[16,512]{1,0:T(8,128)S(1)} collective-permute-done((f32[16,512]{1,0:T(8,128)S(1)}, f32[16,512]{1,0:T(8,128)S(1)}, u32[]{:S(2)}, u32[]{:S(2)}) %collective-permute-start.5) | collective-permute-done | bytes 32800 | tf_op jit(solution)/shard_map/ppermute | solution.py:280
  16.3 0.7 %collective-permute-done.4.refs_2_ = f32[16,512]{1,0:T(8,128)S(1)} collective-permute-done((f32[16,512]{1,0:T(8,128)S(1)}, f32[16,512]{1,0:T(8,128)S(1)}, u32[]{:S(2)}, u32[]{:S(2)}) %collective-permute-start.4) | collective-permute-done | bytes 32800 | tf_op jit(solution)/shard_map/ppermute | solution.py:280
  17.0 0.9 %back.1 = (f32[1,128]{1,0:T(1,128)S(1)}, f32[4,6144]{1,0:T(4,128)S(1)}, bf16[4,6144]{1,0:T(4,128)(2,1)S(1)}, bf16[4,6144]{1,0:T(4,128)(2,1)S(1)}, bf16[4,6144]{1,0:T(4,128)(2,1)S(1)}) custom-call(bf16[32,48,16,128]{3,2,1,0:T(8,128)(2,1)S(1)} %prepare.1.data_ref, f32[16,512]{1,0:T(8,128)S(1)} %score.1.refs_0_, f32[16,512]{1,0:T(8,128)S(1)} %collective-permute-done.3.refs_1_, ...), custom_call_target="tpu_custom_call" | custom-call | tf_op jit(solution)/shard_map/back/pallas_call | solution.py:217
  18.0 1.4 %collective-permute-start.6 = (bf16[4,6144]{1,0:T(4,128)(2,1)S(1)}, bf16[4,6144]{1,0:T(4,128)(2,1)S(1)}, u32[]{:S(2)}, u32[]{:S(2)}) collective-permute-start(bf16[4,6144]{1,0:T(4,128)(2,1)S(1)} %get-tuple-element.14), channel_id=1, source_target_pairs={{0,4},{4,8},{8,12},{12,0},{1,5},{5,9},{9,13},{13,1},{2,6},{6,10},{... | collective-permute-start | bytes 147464 | tf_op jit(solution)/shard_map/ppermute | solution.py:304
  19.4 1.7 %collective-permute-start.7 = (bf16[4,6144]{1,0:T(4,128)(2,1)S(1)}, bf16[4,6144]{1,0:T(4,128)(2,1)S(1)}, u32[]{:S(2)}, u32[]{:S(2)}) collective-permute-start(bf16[4,6144]{1,0:T(4,128)(2,1)S(1)} %get-tuple-element.15), channel_id=1, source_target_pairs={{0,8},{4,12},{8,0},{12,4},{1,9},{5,13},{9,1},{13,5},{2,10},{6,14},... | collective-permute-start | bytes 147464 | tf_op jit(solution)/shard_map/ppermute | solution.py:304
  21.0 2.5 %collective-permute-start.8 = (bf16[4,6144]{1,0:T(4,128)(2,1)S(1)}, bf16[4,6144]{1,0:T(4,128)(2,1)S(1)}, u32[]{:S(2)}, u32[]{:S(2)}) collective-permute-start(bf16[4,6144]{1,0:T(4,128)(2,1)S(1)} %get-tuple-element.16), channel_id=1, source_target_pairs={{0,12},{4,0},{8,4},{12,8},{1,13},{5,1},{9,5},{13,9},{2,14},{6,2},{... | collective-permute-start | bytes 147464 | tf_op jit(solution)/shard_map/ppermute | solution.py:304
  23.5 0.4 %collective-permute-done.6.refs_0_ = bf16[4,6144]{1,0:T(4,128)(2,1)S(1)} collective-permute-done((bf16[4,6144]{1,0:T(4,128)(2,1)S(1)}, bf16[4,6144]{1,0:T(4,128)(2,1)S(1)}, u32[]{:S(2)}, u32[]{:S(2)}) %collective-permute-start.6) | collective-permute-done | bytes 49184 | tf_op jit(solution)/shard_map/ppermute | solution.py:304
  23.9 2.1 %collective-permute-done.7.refs_1_ = bf16[4,6144]{1,0:T(4,128)(2,1)S(1)} collective-permute-done((bf16[4,6144]{1,0:T(4,128)(2,1)S(1)}, bf16[4,6144]{1,0:T(4,128)(2,1)S(1)}, u32[]{:S(2)}, u32[]{:S(2)}) %collective-permute-start.7) | collective-permute-done | bytes 49184 | tf_op jit(solution)/shard_map/ppermute | solution.py:304
  26.0 0.7 %finish.1 = (f32[4,2,2048]{2,1,0:T(2,128)}, f32[4,2048]{1,0:T(4,128)}, f32[128]{0:T(128)}) custom-call(f32[1,128]{1,0:T(1,128)S(1)} %get-tuple-element.12.found_ref, f32[4,6144]{1,0:T(4,128)S(1)} %get-tuple-element.13.own_ref, bf16[4,6144]{1,0:T(4,128)(2,1)S(1)} %collective-permute-done.6.refs_0_, bf16[4,6144]{1,0:T(4,128)(2,1)S(1)} %collective-permute-done.7.refs_1_, ...), custom_call_target="tpu_custom_call" | custom-call | tf_op jit(solution)/shard_map/finish/pallas_call | solution.py:245
  (17 shorter events, 0.0 us)
Async XLA Ops:
  0.6 6.5 %copy-start.2 = (bf16[4,128,768]{2,1,0:T(8,128)(2,1)S(1)}, bf16[4,128,768]{2,1,0:T(8,128)(2,1)}, u32[]{:S(2)}) copy-start(bf16[4,128,768]{2,1,0:T(8,128)(2,1)} %constant.2.clone.table_ref) | copy-start | bytes 2359300
  0.6 0.8 %copy-start.3 = (bf16[4,2,2048]{2,1,0:T(2,128)(2,1)S(1)}, bf16[4,2,2048]{2,1,0:T(2,128)(2,1)}, u32[]{:S(2)}) copy-start(bf16[4,2,2048]{2,1,0:T(2,128)(2,1)} %refs_0_) | copy-start | bytes 98308
  0.7 6.4 %copy-start.4 = (f32[2048]{0:T(1024)S(1)}, f32[2048]{0:T(1024)}, u32[]{:S(2)}) copy-start(f32[2048]{0:T(1024)} %param.13) | copy-start | bytes 24580
  0.7 6.4 %copy-start.5 = (s32[512,2]{0,1:T(2,128)S(1)}, s32[512,2]{0,1:T(2,128)}, u32[]{:S(2)}) copy-start(s32[512,2]{0,1:T(2,128)} %param.12) | copy-start | bytes 12292
  0.7 6.4 %copy-start.1 = (bf16[512,2048]{1,0:T(8,128)(2,1)S(1)}, bf16[512,2048]{1,0:T(8,128)(2,1)}, u32[]{:S(2)}) copy-start(bf16[512,2048]{1,0:T(8,128)(2,1)} %ctf_ref.1) | copy-start | bytes 6291460
  0.7 6.4 %copy-start = (bf16[512,2,2048]{2,1,0:T(2,128)(2,1)S(1)}, bf16[512,2,2048]{2,1,0:T(2,128)(2,1)}, u32[]{:S(2)}) copy-start(bf16[512,2,2048]{2,1,0:T(2,128)(2,1)} %param.9) | copy-start | bytes 12582916
  1.5 9.3 %collective-permute-start.2 = (bf16[4,2,2048]{2,1,0:T(2,128)(2,1)S(1)}, bf16[4,2,2048]{2,1,0:T(2,128)(2,1)S(1)}, u32[]{:S(2)}, u32[]{:S(2)}) collective-permute-start(bf16[4,2,2048]{2,1,0:T(2,128)(2,1)S(1)} %copy-done.3), channel_id=1, source_target_pairs={{12,0},{8,4},{0,8},{4,12},{13,1},{9,5},{1,9},{5,13},{14,2},{10,6},... | collective-permute-start | bytes 98312 | tf_op jit(solution)/shard_map/ppermute | solution.py:291
  5.5 5.3 %collective-permute-start.1 = (bf16[4,2,2048]{2,1,0:T(2,128)(2,1)S(1)}, bf16[4,2,2048]{2,1,0:T(2,128)(2,1)S(1)}, u32[]{:S(2)}, u32[]{:S(2)}) collective-permute-start(bf16[4,2,2048]{2,1,0:T(2,128)(2,1)S(1)} %copy-done.3), channel_id=1, source_target_pairs={{8,0},{12,4},{4,8},{0,12},{9,1},{13,5},{5,9},{1,13},{10,2},{14,6},... | collective-permute-start | bytes 98312 | tf_op jit(solution)/shard_map/ppermute | solution.py:291
  6.5 4.3 %collective-permute-start = (bf16[4,2,2048]{2,1,0:T(2,128)(2,1)S(1)}, bf16[4,2,2048]{2,1,0:T(2,128)(2,1)S(1)}, u32[]{:S(2)}, u32[]{:S(2)}) collective-permute-start(bf16[4,2,2048]{2,1,0:T(2,128)(2,1)S(1)} %copy-done.3), channel_id=1, source_target_pairs={{4,0},{0,4},{12,8},{8,12},{5,1},{1,5},{13,9},{9,13},{6,2},{2,6},{1... | collective-permute-start | bytes 98312 | tf_op jit(solution)/shard_map/ppermute | solution.py:291
  7.1 3.7 %copy-start.6 = (s32[1,2]{1,0:T(1,128)S(1)}, s32[1,2]{1,0:T(1,128)}, u32[]{:S(2)}) copy-start(s32[1,2]{1,0:T(1,128)} %allowed_ref.1) | copy-start | bytes 28
  7.1 3.7 %copy-start.7 = (s32[16]{0:T(128)S(1)}, s32[16]{0:T(128)}, u32[]{:S(2)}) copy-start(s32[16]{0:T(128)} %param.14) | copy-start | bytes 196
  7.1 3.7 %copy-start.8 = (f32[4]{0:T(128)S(1)}, f32[4]{0:T(128)}, u32[]{:S(2)}) copy-start(f32[4]{0:T(128)} %param.15) | copy-start | bytes 52
  12.6 3.7 %collective-permute-start.5 = (f32[16,512]{1,0:T(8,128)S(1)}, f32[16,512]{1,0:T(8,128)S(1)}, u32[]{:S(2)}, u32[]{:S(2)}) collective-permute-start(f32[16,512]{1,0:T(8,128)S(1)} %score.1.refs_0_), channel_id=1, source_target_pairs={{3,0},{2,1},{1,2},{0,3},{7,4},{6,5},{5,6},{4,7},{11,8},{10,9},{9,1... | collective-permute-start | bytes 98312 | tf_op jit(solution)/shard_map/ppermute | solution.py:280
  13.0 4.0 %collective-permute-start.4 = (f32[16,512]{1,0:T(8,128)S(1)}, f32[16,512]{1,0:T(8,128)S(1)}, u32[]{:S(2)}, u32[]{:S(2)}) collective-permute-start(f32[16,512]{1,0:T(8,128)S(1)} %score.1.refs_0_), channel_id=1, source_target_pairs={{2,0},{3,1},{0,2},{1,3},{6,4},{7,5},{4,6},{5,7},{10,8},{11,9},{8,1... | collective-permute-start | bytes 98312 | tf_op jit(solution)/shard_map/ppermute | solution.py:280
  14.2 2.8 %collective-permute-start.3 = (f32[16,512]{1,0:T(8,128)S(1)}, f32[16,512]{1,0:T(8,128)S(1)}, u32[]{:S(2)}, u32[]{:S(2)}) collective-permute-start(f32[16,512]{1,0:T(8,128)S(1)} %score.1.refs_0_), channel_id=1, source_target_pairs={{1,0},{0,1},{3,2},{2,3},{5,4},{4,5},{7,6},{6,7},{9,8},{8,9},{11,10... | collective-permute-start | bytes 98312 | tf_op jit(solution)/shard_map/ppermute | solution.py:280
  18.0 5.9 %collective-permute-start.6 = (bf16[4,6144]{1,0:T(4,128)(2,1)S(1)}, bf16[4,6144]{1,0:T(4,128)(2,1)S(1)}, u32[]{:S(2)}, u32[]{:S(2)}) collective-permute-start(bf16[4,6144]{1,0:T(4,128)(2,1)S(1)} %get-tuple-element.14), channel_id=1, source_target_pairs={{0,4},{4,8},{8,12},{12,0},{1,5},{5,9},{9,13},{13,1},{2,6},{6,10},{... | collective-permute-start | bytes 147464 | tf_op jit(solution)/shard_map/ppermute | solution.py:304
  19.4 6.6 %collective-permute-start.7 = (bf16[4,6144]{1,0:T(4,128)(2,1)S(1)}, bf16[4,6144]{1,0:T(4,128)(2,1)S(1)}, u32[]{:S(2)}, u32[]{:S(2)}) collective-permute-start(bf16[4,6144]{1,0:T(4,128)(2,1)S(1)} %get-tuple-element.15), channel_id=1, source_target_pairs={{0,8},{4,12},{8,0},{12,4},{1,9},{5,13},{9,1},{13,5},{2,10},{6,14},... | collective-permute-start | bytes 147464 | tf_op jit(solution)/shard_map/ppermute | solution.py:304
  21.0 4.9 %collective-permute-start.8 = (bf16[4,6144]{1,0:T(4,128)(2,1)S(1)}, bf16[4,6144]{1,0:T(4,128)(2,1)S(1)}, u32[]{:S(2)}, u32[]{:S(2)}) collective-permute-start(bf16[4,6144]{1,0:T(4,128)(2,1)S(1)} %get-tuple-element.16), channel_id=1, source_target_pairs={{0,12},{4,0},{8,4},{12,8},{1,13},{5,1},{9,5},{13,9},{2,14},{6,2},{... | collective-permute-start | bytes 147464 | tf_op jit(solution)/shard_map/ppermute | solution.py:304
